TPU v7x, 32 devices: a whole 2x2x4 slice. The times are simulated.
32 devices in a mesh: groups: 2 (over x), lon: 16 (over z, y, core).
Axes of the slice: x: 2, y: 2, z: 4, core: 2. Of those that a mesh axis runs over, the one named last changes fastest.
Arguments:
- tokens: bfloat16 [64, 192, 1024], P(('groups', 'lon')), parts along dimension 0, may hold values from -32 to 32
- projection: bfloat16 [1024, 3072], replicated, may hold values from -1 to 1
- out_weight: bfloat16 [1024, 1024], replicated, may hold values from -1.5 to 1.5
- half_width: int32 [6], replicated, may hold values from 1 to 4, as said below
- neighbours: int32 [6, 2], replicated, may hold values from 0 to 5, as said below
Outputs:
- output: bfloat16 [64, 192, 1024], P(('groups', 'lon')), parts along dimension 0
There are 2 independent parts, one for each index of `groups`. A program takes and returns all parts, laid end to end along the dimension named above; an argument that names none is the same for every part. Nothing has to cross between parts.
Inputs may be any that keep to these rules, and one draw needn't show every extreme that they name: `half_width`: exactly one latitude block has a half-width above 2, and its half-width is 4. `neighbours`: row b names 2 different latitude blocks, b among them.
All inputs are finite; a program needn't handle non-finite values.
Results may differ from a plain program's by a relative error of at most 0.0087.
Values may be sent and summed in bfloat16 or wider, within the bound.
No kernel may reach another device: no remote copies, remote signals or barrier semaphores. Data moves between devices by JAX's collectives and lax.ppermute only.
A program may use at most 128 MiB of HBM per device.

v0:
```python
import math

import jax
import jax.numpy as jnp
from jax import lax
from jax.sharding import PartitionSpec as P

HEADS = 16
WMIN = 2
WMAX = 4


def from_behind(block, axis, distance):
    devices = range(lax.axis_size(axis))
    route = [((i - distance) % len(devices), i) for i in devices]
    return lax.ppermute(block, axis, route)


def attend(carried, queries, key_rows, visible, shared):
    running_max, running_sum, accumulated = carried
    head_count, head_size = (queries.shape[2], queries.shape[3])
    model_width = head_count * head_size
    key_part = key_rows[..., :model_width].reshape(key_rows.shape[:-1] + (head_count, head_size))
    value_part = key_rows[..., model_width:].reshape(key_rows.shape[:-1] + (head_count, head_size))
    if shared:
        form_scores = "bqhd,khd->bhqk"
        form_values = "bhqk,khd->bqhd"
    else:
        form_scores = "bqhd,bkhd->bhqk"
        form_values = "bhqk,bkhd->bqhd"
    scores = jnp.einsum(form_scores, queries, key_part, preferred_element_type=jnp.float32) * (
        1.0 / math.sqrt(head_size)
    )
    allowed = visible[:, None, None, :]
    block_max = jnp.max(jnp.where(allowed, scores, -jnp.inf), axis=-1)
    new_max = jnp.maximum(running_max, block_max)
    exponent = jnp.where(allowed, jnp.exp(scores - new_max[..., None]), 0.0)
    factor = jnp.exp(running_max - new_max)
    running_sum = running_sum * factor + jnp.sum(exponent, axis=-1)
    weights = exponent.astype(jnp.bfloat16)
    update = jnp.einsum(form_values, weights, value_part, preferred_element_type=jnp.float32)
    accumulated = accumulated * factor.transpose(0, 2, 1)[..., None] + update
    return (new_max, running_sum, accumulated)


def band_rows(key_band, neighbours, half_width, offset):
    block_rows = key_band.shape[1]
    key_rows = key_band[neighbours].reshape(neighbours.shape[0], -1, key_band.shape[2])
    visible = jnp.repeat(half_width[neighbours] >= offset, block_rows, axis=1)
    return (key_rows, visible)


def absorb(carried, queries, arrivals, neighbours, half_width, offset):
    for incoming in arrivals:
        key_rows, visible = band_rows(incoming, neighbours, half_width, offset)
        carried = attend(carried, queries, key_rows, visible, False)
    return carried


def absorb_polar(carried, queries, arrivals, neighbours, half_width, widest, offset):
    lat_blocks, block_rows = (queries.shape[0], queries.shape[1])
    member = jnp.any(neighbours == widest, axis=1)
    visible = jnp.broadcast_to(
        (member & (half_width[widest] >= offset))[:, None], (lat_blocks, block_rows)
    )
    for incoming in arrivals:
        carried = attend(carried, queries, incoming, visible, True)
    return carried


def per_device(tokens, projection, out_weight, half_width, neighbours):
    lon_cells, lat_cells, model_width = tokens.shape
    lat_blocks = neighbours.shape[0]
    lat_size = lat_cells // lat_blocks
    block_rows = lon_cells * lat_size
    head_size = model_width // HEADS
    gridded = (
        tokens.reshape(lon_cells, lat_blocks, lat_size, model_width)
        .transpose(1, 0, 2, 3)
        .reshape(-1, model_width)
    )
    projected = jnp.dot(gridded, projection, preferred_element_type=jnp.float32).astype(
        jnp.bfloat16
    )
    queries = projected[:, :model_width].reshape(lat_blocks, block_rows, HEADS, head_size)
    own_band = projected[:, model_width:].reshape(lat_blocks, block_rows, 2 * model_width)
    carried = (
        jnp.full((lat_blocks, HEADS, block_rows), -jnp.inf, jnp.float32),
        jnp.zeros((lat_blocks, HEADS, block_rows), jnp.float32),
        jnp.zeros((lat_blocks, block_rows, HEADS, head_size), jnp.float32),
    )
    key_rows, visible = band_rows(own_band, neighbours, half_width, 0)
    carried = attend(carried, queries, key_rows, visible, False)
    widest = jnp.argmax(half_width)
    eastward, westward = (own_band, own_band)
    for offset in range(1, WMIN + 1):
        eastward = from_behind(eastward, "lon", 1)
        westward = from_behind(westward, "lon", -1)
        carried = absorb(carried, queries, (eastward, westward), neighbours, half_width, offset)
    eastward = eastward[widest]
    westward = westward[widest]
    for offset in range(WMIN + 1, WMAX + 1):
        eastward = from_behind(eastward, "lon", 1)
        westward = from_behind(westward, "lon", -1)
        carried = absorb_polar(
            carried, queries, (eastward, westward), neighbours, half_width, widest, offset
        )
    running_max, running_sum, accumulated = carried
    attended = (
        (accumulated / running_sum.transpose(0, 2, 1)[..., None])
        .astype(jnp.bfloat16)
        .reshape(-1, model_width)
    )
    output = jnp.dot(attended, out_weight, preferred_element_type=jnp.float32).astype(jnp.bfloat16)
    output = output.reshape(lat_blocks, lon_cells, lat_size, model_width).transpose(1, 0, 2, 3)
    return output.reshape(lon_cells, lat_cells, model_width)


def solution(mesh):
    return jax.shard_map(
        per_device,
        mesh=mesh,
        in_specs=(P(("groups", "lon"), None, None), P(), P(), P(), P()),
        out_specs=P(("groups", "lon"), None, None),
        check_vma=False,
    )
```

profile of v0, /device:TPU:0, one launch (start us, length us, event | category | flops | bytes accessed | tf_op | source)
XLA Modules:
  0.0 199.4 jit_solution(5371935436333915647)
XLA Ops:
  1.4 5.6 %convolution_convert_fusion = bf16[384,3072]{1,0:T(8,128)(2,1)S(1)} fusion(bf16[384,1024]{1,0:T(8,128)(2,1)S(1)} %bitcast.319, bf16[1024,3072]{1,0:T(8,128)(2,1)} %param.6), kind=kOutput, calls=%fused_computation.6 | convolution fusion | flops 2417098752 | bytes 9437184 | tf_op jit(solution)/shard_map/dot_general | solution.py:82
  9.7 5.4 %collective-permute-start.1 = (bf16[6,64,2048]{2,1,0:T(8,128)(2,1)}, bf16[6,64,2048]{2,1,0:T(8,128)(2,1)}, u32[]{:S(2)}, u32[]{:S(2)}) collective-permute-start(bf16[6,64,2048]{2,1,0:T(8,128)(2,1)} %bitcast.3), channel_id=1, source_target_pairs={{1,0},{2,1},{3,2},{4,3},{5,4},{6,5},{7,6},{8,7},{9,8},{10,9},{11,1... | collective-permute-start | bytes 4718600 | tf_op jit(solution)/shard_map/ppermute | solution.py:16
  15.4 3.9 %gather_fusion.1 = bf16[12,64,2048]{2,1,0:T(8,128)(2,1)} fusion(bf16[6,64,2048]{2,1,0:T(8,128)(2,1)} %bitcast.3, s32[1024]{0:T(1024)S(1)} %pad_clamp_fusion), kind=kCustom, calls=%fused_computation.1 | custom fusion | bytes 6291504 | tf_op jit(solution)/shard_map/gather | solution.py:48
  20.0 4.0 %fusion.124 = (bf16[6,128,1024]{2,1,0:T(8,128)(2,1)}, bf16[6,128,1024]{2,1,0:T(8,128)(2,1)}) fusion(bf16[6,128,2048]{2,1,0:T(8,128)(2,1)} %bitcast.296), kind=kLoop, calls=%fused_computation.192 | loop fusion | bytes 6291456 | tf_op jit(solution)/shard_map/slice | solution.py:24
  42.9 3.9 %gather_fusion.2 = bf16[12,64,2048]{2,1,0:T(8,128)(2,1)} fusion(bf16[6,64,2048]{2,1,0:T(8,128)(2,1)} %collective-permute-done, s32[1024]{0:T(1024)S(1)} %pad_clamp_fusion), kind=kCustom, calls=%fused_computation.2 | custom fusion | bytes 6291504 | tf_op jit(solution)/shard_map/gather | solution.py:48
  46.8 3.8 %fusion.125 = (bf16[6,128,1024]{2,1,0:T(8,128)(2,1)}, bf16[6,128,1024]{2,1,0:T(8,128)(2,1)}) fusion(bf16[6,128,2048]{2,1,0:T(8,128)(2,1)} %bitcast.298), kind=kLoop, calls=%fused_computation.193 | loop fusion | bytes 6291456 | tf_op jit(solution)/shard_map/slice | solution.py:24
  53.3 4.5 %collective-permute-start.2 = (bf16[6,64,2048]{2,1,0:T(8,128)(2,1)}, bf16[6,64,2048]{2,1,0:T(8,128)(2,1)}, u32[]{:S(2)}, u32[]{:S(2)}) collective-permute-start(bf16[6,64,2048]{2,1,0:T(8,128)(2,1)} %collective-permute-done), channel_id=1, source_target_pairs={{15,0},{0,1},{1,2},{2,3},{3,4},{4,5},{5,6},{6,7},{7,8},{8,9},{9,10... | collective-permute-start | bytes 4718600 | tf_op jit(solution)/shard_map/ppermute | solution.py:16
  57.8 4.0 %gather_fusion.3 = bf16[12,64,2048]{2,1,0:T(8,128)(2,1)} fusion(bf16[6,64,2048]{2,1,0:T(8,128)(2,1)} %collective-permute-done.1, s32[1024]{0:T(1024)S(1)} %pad_clamp_fusion), kind=kCustom, calls=%fused_computation.3 | custom fusion | bytes 6291504 | tf_op jit(solution)/shard_map/gather | solution.py:48
  61.8 4.6 %select_reduce_fusion.3 = (f32[6,16,64]{2,1,0:T(8,128)S(1)}, f32[6,16,64,128]{3,2,1,0:T(8,128)}) fusion(pred[6,128]{1,0:T(8,128)(4,1)S(1)} %broadcast_in_dim.164, bf16[6,128,16,64]{1,3,2,0:T(8,128)(2,1)} %bitcast.303, bf16[6,64,16,64]{3,2,1,0:T(8,128)(2,1)} %reshape.206), kind=kOutput, calls=%fused_computation.53 | convolution fusion | flops 103016448 | bytes 5530368 | tf_op jit(solution)/shard_map/bqhd,bkhd->bhqk/dot_general | solution.py:31
  76.2 5.2 %fusion.46 = f32[6,16,64,64]{3,2,1,0:T(8,128)} fusion(bf16[6,128,16,64]{1,3,2,0:T(8,128)(2,1)} %bitcast.305, f32[6,16,64,128]{3,2,1,0:T(8,128)} %get-tuple-element.72, f32[6,16,64]{2,1,0:T(8,128)S(1)} %max.201, pred[6,128]{1,0:T(8,128)(4,1)S(1)} %broadcast_in_dim.164), kind=kOutput, calls=%fused_computation.77 | convolution fusion | flops 103809024 | bytes 6316800 | tf_op jit(solution)/shard_map/bhqk,bkhd->bqhd/dot_general | solution.py:41
  81.4 4.3 %fusion.24 = (f32[6,16,64]{2,1,0:T(8,128)}, f32[6,16,64]{2,1,0:T(8,128)S(1)}, f32[6,16,64,128]{3,2,1,0:T(8,128)}) fusion(f32[6,16,64,128]{3,2,1,0:T(8,128)S(1)} %copy-done.11, f32[6,16,64]{2,1,0:T(8,128)S(1)} %max.201, pred[6,128]{1,0:T(8,128)(4,1)S(1)} %broadcast_in_dim.164, bf16[6,128,16,64]{1,3,2,0:T(8,128)(2,1)S(1)} %bitcast.308, ...), kind=kOutput, calls=%fused_computation.58 | convolution fusion | flops 106156032 | bytes 8725248 | tf_op jit(solution)/shard_map/bqhd,bkhd->bhqk/dot_general | solution.py:31
  86.8 5.6 %collective-permute-start.5 = (bf16[64,2048]{1,0:T(8,128)(2,1)S(1)}, bf16[64,2048]{1,0:T(8,128)(2,1)}, u32[]{:S(2)}, u32[]{:S(2)}) collective-permute-start(bf16[64,2048]{1,0:T(8,128)(2,1)S(1)} %dynamic-slice_bitcast_fusion), channel_id=1, source_target_pairs={{1,0},{2,1},{3,2},{4,3},{5,4},{6,5},{7,6},{8,7},{9,8},{10,9},{11,1... | collective-permute-start | bytes 786440 | tf_op jit(solution)/shard_map/ppermute | solution.py:16
  92.4 3.9 %gather_fusion.5 = bf16[12,64,2048]{2,1,0:T(8,128)(2,1)} fusion(bf16[6,64,2048]{2,1,0:T(8,128)(2,1)} %collective-permute-done.3, s32[1024]{0:T(1024)S(1)} %pad_clamp_fusion), kind=kCustom, calls=%fused_computation.5 | custom fusion | bytes 6291504 | tf_op jit(solution)/shard_map/gather | solution.py:48
  96.3 4.0 %fusion.128 = (bf16[6,128,1024]{2,1,0:T(8,128)(2,1)}, bf16[6,128,1024]{2,1,0:T(8,128)(2,1)}) fusion(bf16[6,128,2048]{2,1,0:T(8,128)(2,1)} %bitcast.297), kind=kLoop, calls=%fused_computation.196 | loop fusion | bytes 6291456 | tf_op jit(solution)/shard_map/slice | solution.py:24
  105.6 3.9 %gather_fusion.4 = bf16[12,64,2048]{2,1,0:T(8,128)(2,1)} fusion(bf16[6,64,2048]{2,1,0:T(8,128)(2,1)} %collective-permute-done.2, s32[1024]{0:T(1024)S(1)} %pad_clamp_fusion), kind=kCustom, calls=%fused_computation.4 | custom fusion | bytes 6291504 | tf_op jit(solution)/shard_map/gather | solution.py:48
  109.5 3.9 %fusion.127 = (bf16[6,128,1024]{2,1,0:T(8,128)(2,1)}, bf16[6,128,1024]{2,1,0:T(8,128)(2,1)}) fusion(bf16[6,128,2048]{2,1,0:T(8,128)(2,1)} %bitcast.295), kind=kLoop, calls=%fused_computation.195 | loop fusion | bytes 6291456 | tf_op jit(solution)/shard_map/slice | solution.py:24
  122.4 4.3 %fusion.22 = (f32[6,16,64]{2,1,0:T(8,128)}, f32[6,16,64]{2,1,0:T(8,128)}) fusion(f32[6,16,64,128]{3,2,1,0:T(8,128)S(1)} %copy-done.7, f32[6,16,64]{2,1,0:T(8,128)S(1)} %get-tuple-element.69, pred[6,128]{1,0:T(8,128)(4,1)S(1)} %broadcast_in_dim.158, f32[6,16,64]{2,1,0:T(8,128)S(1)} %get-tuple-element.32, f32[6,16,64,128]{3,2,1,0:T(8,128)S(1)} %copy-done.10, ...), kind=kLoop, calls=%fused_computation.56 | loop fusion | flops 6279168 | bytes 6391296 | tf_op jit(solution)/shard_map/reduce_sum | solution.py:39
  129.3 4.3 %fusion.28 = (f32[6,16,64]{2,1,0:T(8,128)}, f32[6,16,64]{2,1,0:T(8,128)S(1)}, f32[6,16,64,128]{3,2,1,0:T(8,128)}) fusion(f32[6,16,64,128]{3,2,1,0:T(8,128)S(1)} %get-tuple-element.68, f32[6,16,64]{2,1,0:T(8,128)S(1)} %get-tuple-element.31, pred[6,128]{1,0:T(8,128)(4,1)S(1)} %broadcast_in_dim.167, bf16[6,128,16,64]{1,3,2,0:T(8,128)(2,1)S(1)} %bitcast.307, ...), kind=kOutput, calls=%fused_computation.62 | convolution fusion | flops 106156032 | bytes 8725248 | tf_op jit(solution)/shard_map/bqhd,bkhd->bhqk/dot_general | solution.py:31
  141.3 3.2 %fusion.14 = (f32[6,16,64]{2,0,1:T(8,128)S(1)}, f32[16,64,6,64]{3,1,2,0:T(8,128)S(1)}) fusion(pred[6]{0:T(512)(128)(4,1)S(1)} %get-tuple-element.61, bf16[6,64,16,64]{3,2,1,0:T(8,128)(2,1)} %reshape.206, bf16[64,16,64,1]{2,1,0,3:T(8,128)(2,1)S(1)} %bitcast.316), kind=kOutput, calls=%fused_computation.33 | convolution fusion | flops 51505152 | bytes 2514950 | tf_op jit(solution)/shard_map/bqhd,khd->bhqk/dot_general | solution.py:31
  144.5 4.8 %fusion.32 = (f32[6,16,64]{2,0,1:T(8,128)}, f32[6,16,64]{2,0,1:T(8,128)S(1)}, bf16[6,16,64,64]{2,3,0,1:T(8,128)(2,1)S(1)}, f32[16,64,6,64]{3,1,2,0:T(8,128)}) fusion(f32[16,64,6,64]{3,1,2,0:T(8,128)S(1)} %get-tuple-element.66, f32[6,16,64]{2,0,1:T(8,128)S(1)} %copy.192, pred[6]{0:T(512)(128)(4,1)S(1)} %get-tuple-element.61, ...), kind=kOutput, calls=%fused_computation.66 | convolution fusion | flops 53465088 | bytes 4923398 | tf_op jit(solution)/shard_map/bqhd,khd->bhqk/dot_general | solution.py:31
  164.5 4.9 %collective-permute-done.6 = bf16[64,2048]{1,0:T(8,128)(2,1)S(1)} collective-permute-done((bf16[64,2048]{1,0:T(8,128)(2,1)}, bf16[64,2048]{1,0:T(8,128)(2,1)S(1)}, u32[]{:S(2)}, u32[]{:S(2)}) %collective-permute-start.6) | collective-permute-done | bytes 262176 | tf_op jit(solution)/shard_map/ppermute | solution.py:16
  170.4 3.2 %fusion.6 = (f32[6,16,64]{2,0,1:T(8,128)S(1)}, f32[16,64,6,64]{3,1,2,0:T(8,128)S(1)}) fusion(pred[6]{0:T(512)(128)(4,1)S(1)} %get-tuple-element.62, bf16[6,64,16,64]{3,2,1,0:T(8,128)(2,1)} %reshape.206, bf16[64,16,64,1]{2,1,0,3:T(8,128)(2,1)S(1)} %bitcast.315), kind=kOutput, calls=%fused_computation.19 | convolution fusion | flops 51505152 | bytes 2514950 | tf_op jit(solution)/shard_map/bqhd,khd->bhqk/dot_general | solution.py:31
  185.4 6.2 %fusion.1 = bf16[6,64,16,64]{1,3,2,0:T(8,128)(2,1)} fusion(f32[16,64,6,64]{3,1,0,2:T(8,128)} %fusion.51, f32[16,64,6,64]{3,1,0,2:T(8,128)} %fusion.53, f32[16,64,6,64]{3,1,0,2:T(8,128)S(1)} %copy-done.17, f32[6,16,64,64]{3,2,1,0:T(8,128)} %fusion.40, f32[6,16,64,64]{3,2,1,0:T(8,128)S(1)} %copy-done.16, f32[6,16,64,64]{3,2,1,0:T(8,128)S(1)} %copy-done.15, ...), kind=kOutput, calls=%fused_computation.9 | convolution fusion | flops 57802752 | bytes 14532608 | tf_op jit(solution)/shard_map/bhqk,khd->bqhd/dot_general | solution.py:41
  191.6 3.2 %copy.219 = bf16[6,64,16,64]{3,2,1,0:T(8,128)(2,1)} copy(bf16[6,64,16,64]{1,3,2,0:T(8,128)(2,1)} %fusion.1) | data formatting | bytes 1572864 | tf_op jit(solution)/shard_map/convert_element_type | solution.py:111
  (185 shorter events, 90.7 us)
Async XLA Ops:
  0.0 197.5 %copy-start = (bf16[1024,1024]{1,0:T(8,128)(2,1)S(1)}, bf16[1024,1024]{1,0:T(8,128)(2,1)}, u32[]{:S(2)}) copy-start(bf16[1024,1024]{1,0:T(8,128)(2,1)} %param.7) | copy-start | bytes 6291460
  8.4 6.7 %copy-start.48 = (s32[6,2]{0,1:T(2,128)S(1)}, s32[6,2]{0,1:T(2,128)}, u32[]{:S(2)}) copy-start(s32[6,2]{0,1:T(2,128)} %param.9) | copy-start | bytes 148
  9.7 48.0 %collective-permute-start.1 = (bf16[6,64,2048]{2,1,0:T(8,128)(2,1)}, bf16[6,64,2048]{2,1,0:T(8,128)(2,1)}, u32[]{:S(2)}, u32[]{:S(2)}) collective-permute-start(bf16[6,64,2048]{2,1,0:T(8,128)(2,1)} %bitcast.3), channel_id=1, source_target_pairs={{1,0},{2,1},{3,2},{4,3},{5,4},{6,5},{7,6},{8,7},{9,8},{10,9},{11,1... | collective-permute-start | bytes 4718600 | tf_op jit(solution)/shard_map/ppermute | solution.py:16
  15.2 27.7 %collective-permute-start = (bf16[6,64,2048]{2,1,0:T(8,128)(2,1)}, bf16[6,64,2048]{2,1,0:T(8,128)(2,1)}, u32[]{:S(2)}, u32[]{:S(2)}) collective-permute-start(bf16[6,64,2048]{2,1,0:T(8,128)(2,1)} %bitcast.3), channel_id=1, source_target_pairs={{15,0},{0,1},{1,2},{2,3},{3,4},{4,5},{5,6},{6,7},{7,8},{8,9},{9,10... | collective-permute-start | bytes 4718600 | tf_op jit(solution)/shard_map/ppermute | solution.py:16
  20.0 9.4 %slice-start = ((bf16[384,3072]{1,0:T(8,128)(2,1)}), bf16[384,1024]{1,0:T(8,128)(2,1)S(1)}, s32[]{:S(2)}) async-start(bf16[384,3072]{1,0:T(8,128)(2,1)} %copy-done.22), calls=%async_computation | async-start | bytes 1572864 | tf_op jit(solution)/shard_map/slice | solution.py:85
  40.2 120.4 %copy-start.23 = (f32[6,16,64]{2,1,0:T(8,128)}, f32[6,16,64]{2,1,0:T(8,128)S(1)}, u32[]{:S(2)}) copy-start(f32[6,16,64]{2,1,0:T(8,128)S(1)} %get-tuple-element.69) | copy-start | bytes 73732
  53.3 49.6 %collective-permute-start.2 = (bf16[6,64,2048]{2,1,0:T(8,128)(2,1)}, bf16[6,64,2048]{2,1,0:T(8,128)(2,1)}, u32[]{:S(2)}, u32[]{:S(2)}) collective-permute-start(bf16[6,64,2048]{2,1,0:T(8,128)(2,1)} %collective-permute-done), channel_id=1, source_target_pairs={{15,0},{0,1},{1,2},{2,3},{3,4},{4,5},{5,6},{6,7},{7,8},{8,9},{9,10... | collective-permute-start | bytes 4718600 | tf_op jit(solution)/shard_map/ppermute | solution.py:16
  57.8 28.0 %collective-permute-start.3 = (bf16[6,64,2048]{2,1,0:T(8,128)(2,1)}, bf16[6,64,2048]{2,1,0:T(8,128)(2,1)}, u32[]{:S(2)}, u32[]{:S(2)}) collective-permute-start(bf16[6,64,2048]{2,1,0:T(8,128)(2,1)} %collective-permute-done.1), channel_id=1, source_target_pairs={{1,0},{2,1},{3,2},{4,3},{5,4},{6,5},{7,6},{8,7},{9,8},{10,9},{11,1... | collective-permute-start | bytes 4718600 | tf_op jit(solution)/shard_map/ppermute | solution.py:16
  66.3 94.3 %copy-start.31 = (f32[6,16,64]{2,1,0:T(8,128)}, f32[6,16,64]{2,1,0:T(8,128)S(1)}, u32[]{:S(2)}) copy-start(f32[6,16,64]{2,1,0:T(8,128)S(1)} %get-tuple-element.71) | copy-start | bytes 73732
  76.2 5.3 %copy-start.2 = (bf16[6,64,16,64]{3,2,1,0:T(8,128)(2,1)S(1)}, bf16[6,64,16,64]{3,2,1,0:T(8,128)(2,1)}, u32[]{:S(2)}) copy-start(bf16[6,64,16,64]{3,2,1,0:T(8,128)(2,1)} %reshape.206) | copy-start | bytes 2359300
  76.2 5.3 %copy-start.11 = (f32[6,16,64,128]{3,2,1,0:T(8,128)S(1)}, f32[6,16,64,128]{3,2,1,0:T(8,128)}, u32[]{:S(2)}) copy-start(f32[6,16,64,128]{3,2,1,0:T(8,128)} %get-tuple-element.72) | copy-start | bytes 9437188
  85.8 35.9 %copy-start.44 = (f32[6,16,64]{2,1,0:T(8,128)}, f32[6,16,64]{2,1,0:T(8,128)S(1)}, u32[]{:S(2)}) copy-start(f32[6,16,64]{2,1,0:T(8,128)S(1)} %get-tuple-element.8) | copy-start | bytes 73732
  86.8 51.9 %collective-permute-start.5 = (bf16[64,2048]{1,0:T(8,128)(2,1)S(1)}, bf16[64,2048]{1,0:T(8,128)(2,1)}, u32[]{:S(2)}, u32[]{:S(2)}) collective-permute-start(bf16[64,2048]{1,0:T(8,128)(2,1)S(1)} %dynamic-slice_bitcast_fusion), channel_id=1, source_target_pairs={{1,0},{2,1},{3,2},{4,3},{5,4},{6,5},{7,6},{8,7},{9,8},{10,9},{11,1... | collective-permute-start | bytes 786440 | tf_op jit(solution)/shard_map/ppermute | solution.py:16
  103.8 36.1 %collective-permute-start.4 = (bf16[64,2048]{1,0:T(8,128)(2,1)S(1)}, bf16[64,2048]{1,0:T(8,128)(2,1)}, u32[]{:S(2)}, u32[]{:S(2)}) collective-permute-start(bf16[64,2048]{1,0:T(8,128)(2,1)S(1)} %dynamic-slice_bitcast_fusion.1), channel_id=1, source_target_pairs={{15,0},{0,1},{1,2},{2,3},{3,4},{4,5},{5,6},{6,7},{7,8},{8,9},{9,10... | collective-permute-start | bytes 786440 | tf_op jit(solution)/shard_map/ppermute | solution.py:16
  121.7 39.0 %copy-start.33 = (f32[6,16,64]{2,1,0:T(8,128)}, f32[6,16,64]{2,1,0:T(8,128)S(1)}, u32[]{:S(2)}) copy-start(f32[6,16,64]{2,1,0:T(8,128)S(1)} %get-tuple-element.67) | copy-start | bytes 73732
  133.6 10.8 %copy-start.42 = (f32[6,16,64]{2,1,0:T(8,128)}, f32[6,16,64]{2,1,0:T(8,128)S(1)}, u32[]{:S(2)}) copy-start(f32[6,16,64]{2,1,0:T(8,128)S(1)} %get-tuple-element.10) | copy-start | bytes 73732
  144.4 16.2 %copy-start.29 = (f32[6,16,64]{2,0,1:T(8,128)}, f32[6,16,64]{2,0,1:T(8,128)S(1)}, u32[]{:S(2)}) copy-start(f32[6,16,64]{2,0,1:T(8,128)S(1)} %get-tuple-element.65) | copy-start | bytes 73732
  155.3 5.4 %copy-start.43 = (f32[6,16,64]{2,1,0:T(8,128)S(1)}, f32[6,16,64]{2,1,0:T(8,128)}, u32[]{:S(2)}) copy-start(f32[6,16,64]{2,1,0:T(8,128)} %copy-done.42) | copy-start | bytes 73732
  155.3 5.4 %copy-start.45 = (f32[6,16,64]{2,1,0:T(8,128)S(1)}, f32[6,16,64]{2,1,0:T(8,128)}, u32[]{:S(2)}) copy-start(f32[6,16,64]{2,1,0:T(8,128)} %copy-done.44) | copy-start | bytes 73732
  155.3 7.2 %collective-permute-start.7 = (bf16[64,2048]{1,0:T(8,128)(2,1)}, bf16[64,2048]{1,0:T(8,128)(2,1)}, u32[]{:S(2)}, u32[]{:S(2)}) collective-permute-start(bf16[64,2048]{1,0:T(8,128)(2,1)} %collective-permute-done.5), channel_id=1, source_target_pairs={{1,0},{2,1},{3,2},{4,3},{5,4},{6,5},{7,6},{8,7},{9,8},{10,9},{11,1... | collective-permute-start | bytes 786440 | tf_op jit(solution)/shard_map/ppermute | solution.py:16
  160.6 8.7 %collective-permute-start.6 = (bf16[64,2048]{1,0:T(8,128)(2,1)}, bf16[64,2048]{1,0:T(8,128)(2,1)S(1)}, u32[]{:S(2)}, u32[]{:S(2)}) collective-permute-start(bf16[64,2048]{1,0:T(8,128)(2,1)} %collective-permute-done.4), channel_id=1, source_target_pairs={{15,0},{0,1},{1,2},{2,3},{3,4},{4,5},{5,6},{6,7},{7,8},{8,9},{9,10... | collective-permute-start | bytes 786440 | tf_op jit(solution)/shard_map/ppermute | solution.py:16
  176.3 7.9 %copy-start.16 = (f32[6,16,64,64]{3,2,1,0:T(8,128)S(1)}, f32[6,16,64,64]{3,2,1,0:T(8,128)}, u32[]{:S(2)}) copy-start(f32[6,16,64,64]{3,2,1,0:T(8,128)} %fusion.42) | copy-start | bytes 4718596
  176.3 7.9 %copy-start.17 = (f32[16,64,6,64]{3,1,0,2:T(8,128)S(1)}, f32[16,64,6,64]{3,1,0,2:T(8,128)}, u32[]{:S(2)}) copy-start(f32[16,64,6,64]{3,1,0,2:T(8,128)} %fusion.55) | copy-start | bytes 4718596
  178.8 5.4 %copy-start.15 = (f32[6,16,64,64]{3,2,1,0:T(8,128)S(1)}, f32[6,16,64,64]{3,2,1,0:T(8,128)}, u32[]{:S(2)}) copy-start(f32[6,16,64,64]{3,2,1,0:T(8,128)} %fusion.44) | copy-start | bytes 4718596
  (34 other events, 122.2 us)
where the time goes:
time: 200 us; the launch traced here: 199 us
  local copies, waits for them, and re-layouts  90.3 us (45%)
  matrix products  67.6 us (34%)
  starting transfers between devices  20.2 us (10%)
  other arithmetic  12.1 us (6%)
  waiting for transfers between devices  5.1 us (3%)
  between operations  4.07 us (2%)
    dot_general x9, matrix products, attend(): jnp.einsum(form_scores, queries, key_part, preferred_element_type=jnp.flo...  33 us
    unnamed x108, local copies, waits for them, and re-layouts  31 us
    dot_general x9, matrix products, attend(): jnp.einsum(form_values, weights, value_part, preferred_element_type=jnp.f...  28 us
    slice x11, local copies, waits for them, and re-layouts, attend(): key_rows[..., model_width:]  22.4 us
    ppermute x8, starting transfers between devices, from_behind(): return lax.ppermute(block, axis, route)  20.2 us
    gather x5, local copies, waits for them, and re-layouts, band_rows(): key_band[neighbours].reshape(neighbours.shape[0], -1, key_band.shape[2])  19.6 us
    reduce_sum x3, other arithmetic, attend(): running_sum = running_sum * factor + jnp.sum(exponent, axis=-1)  9.09 us
    dot_general x1, matrix products, per_device(): jnp.dot(gridded, projection, preferred_element_type=jnp.float32)  5.62 us
  transfers between devices with their start and end apart: 8, of which 2 were waited for; matrix products, arithmetic and copies ran while one was open for 57% of the time, Pallas kernels for 0%

commit v1 on v0

v1 whole, which is shorter than its diff:
```python
import math

import jax
import jax.numpy as jnp
from jax import lax
from jax.experimental import pallas as pl
from jax.experimental.pallas import tpu as pltpu
from jax.sharding import PartitionSpec as P

HEADS = 16
HEAD = 64
PACK = 4
WIDE = PACK * HEAD
CHUNKS = 3
NEVER = -1e37
BF16 = jnp.bfloat16
F32 = jnp.float32
SCALE = math.log2(math.e) / math.sqrt(HEAD)
VMEM_LIMIT = 40 * 1024 * 1024


def lane_head(shape):
    return lax.broadcasted_iota(jnp.int32, shape, len(shape) - 1) // HEAD


def spread(packed):
    lane = lane_head((1, WIDE))
    return jnp.concatenate(
        [packed * (lane == h).astype(F32).astype(BF16) for h in range(PACK)], axis=0
    )


def gather_diagonal(full):
    lane = lane_head((HEAD, WIDE))
    total = full[:HEAD]
    for h in range(1, PACK):
        total = jnp.where(lane == h, full[h * HEAD : (h + 1) * HEAD], total)
    return total


def dot(a, b):
    return jnp.dot(a, b, preferred_element_type=F32)


def dot_nt(a, b):
    return lax.dot_general(a, b, (((1,), (1,)), ((), ())), preferred_element_type=F32)


def update(scores, values_t, carried):
    row_max, total, summed = carried
    new_max = jnp.maximum(row_max, jnp.max(scores, axis=0, keepdims=True))
    exponent = jnp.exp2((scores - new_max) * SCALE)
    factor = jnp.exp2((row_max - new_max) * SCALE)
    total = total * factor + jnp.sum(exponent, axis=0, keepdims=True)
    summed = summed * factor + gather_diagonal(dot(values_t, exponent.astype(BF16)))
    return new_max, total, summed


def halves(pair):
    lane = lax.broadcasted_iota(jnp.int32, pair.shape, 1)
    turned = pltpu.roll(pair, HEAD, 1)
    low = lane < HEAD
    zero = jnp.zeros_like(pair)
    first = (jnp.where(low, pair, zero), jnp.where(low, zero, turned))
    second = (jnp.where(low, turned, zero), jnp.where(low, zero, pair))
    return first, second


def first_kernel(nbr, x, s, w, qc, m_out, l_out, acc, wvt, own, both, keys, vals):
    nlb = nbr.shape[0]
    span = x.shape[1] // nlb
    lon = x.shape[0]
    rows = lon * span
    width = x.shape[2]
    groups = width // WIDE
    for c in range(nlb):
        for o in range(lon):
            part = x[o, c * span : (c + 1) * span, :]
            own[c * rows + o * span : c * rows + (o + 1) * span, :] = part
            at = 2 * c * rows + o * span
            both[at : at + span, :] = part
            both[at + rows : at + rows + span, :] = s[o, c * span : (c + 1) * span, :]

    def turn(i, _):
        at = pl.multiple_of(i * 256, 256)
        wvt[pl.ds(at, 256), :] = w[:, pl.ds(2 * width + at, 256)].T
        return 0

    lax.fori_loop(0, width // 256, turn, 0)

    def project(g, _):
        at = pl.multiple_of(g * WIDE, WIDE)
        q = dot(own[...], w[:, pl.ds(at, WIDE)]).astype(BF16).astype(F32)
        for b in range(nlb):
            qt = q[b * rows : (b + 1) * rows, :].T
            qc[b * groups + g] = jnp.concatenate(
                [qt[h * HEAD : (h + 1) * HEAD, :] for h in range(PACK)], axis=1
            ).astype(BF16)
        k = dot(both[...], w[:, pl.ds(width + at, WIDE)]).astype(BF16)
        v = dot_nt(wvt[pl.ds(at, WIDE), :], both[...]).astype(BF16)
        for c in range(nlb):
            keys[c, g] = k[2 * c * rows : 2 * (c + 1) * rows, :]
            vals[c, g] = v[:, 2 * c * rows : 2 * (c + 1) * rows]
        return 0

    lax.fori_loop(0, groups, project, 0)

    def attend(b, _):
        c0, c1 = nbr[b, 0], nbr[b, 1]
        for g in range(groups):
            t = b * groups + g
            k = jnp.concatenate([keys[c0, g], keys[c1, g]], axis=0)
            v = jnp.concatenate([vals[c0, g], vals[c1, g]], axis=1)
            scores = dot(k, spread(qc[t]))
            row_max = jnp.max(scores, axis=0, keepdims=True)
            exponent = jnp.exp2((scores - row_max) * SCALE)
            m_out[t] = row_max
            l_out[t] = jnp.sum(exponent, axis=0, keepdims=True)
            acc[t] = gather_diagonal(dot(v, exponent.astype(BF16)))
        return 0

    lax.fori_loop(0, nlb, attend, 0)


def fill_tokens(chunks, tokens, rows, span, lon):
    at = 0
    for chunk in chunks:
        for c in range(chunk.shape[1] // span):
            for o in range(lon):
                tokens[at : at + span, :] = chunk[o, c * span : (c + 1) * span, :]
                at += span


def wide_update(nbr, wide, qc, wkeys, wvals, carried_refs, groups):
    m, l, acc = carried_refs

    def attend(b, _):
        @pl.when((nbr[b, 0] == wide[0]) | (nbr[b, 1] == wide[0]))
        def _():
            for g in range(groups):
                t = b * groups + g
                scores = dot(wkeys[g], spread(qc[t]))
                m[t], l[t], acc[t] = update(scores, wvals[g], (m[t], l[t], acc[t]))

        return 0

    lax.fori_loop(0, nbr.shape[0], attend, 0)


def second_kernel(nbr, wide, f0, f1, f2, wf, wb, w, wvt, qc, m_in, l_in, acc_in,
                  fkeys, fvals, m, l, acc, tokens, wkeys, wvals):
    nlb = nbr.shape[0]
    lon, rows_c, width = f0.shape
    span = rows_c * CHUNKS // nlb
    rows = lon * span
    groups = width // WIDE
    fill_tokens((f0, f1, f2), tokens, rows, span, lon)
    tokens[nlb * rows : (nlb + 1) * rows, :] = wf[...]
    tokens[(nlb + 1) * rows :, :] = wb[...]
    m[...] = m_in[...]
    l[...] = l_in[...]
    acc[...] = acc_in[...]

    def project(g, _):
        at = pl.multiple_of(g * WIDE, WIDE)
        k = dot(tokens[...], w[:, pl.ds(at, WIDE)]).astype(BF16)
        v = dot_nt(wvt[pl.ds(at, WIDE), :], tokens[...])
        for c in range(0, nlb, 2):
            first, second = halves(v[:, c * rows : (c + 2) * rows])
            fkeys[c, g] = k[c * rows : (c + 1) * rows, :]
            fkeys[c + 1, g] = k[(c + 1) * rows : (c + 2) * rows, :]
            fvals[c, g] = first[0].astype(BF16)
            fvals[c + 1, g] = second[0].astype(BF16)
        wkeys[g] = k[nlb * rows :, :]
        wvals[g] = v[:, nlb * rows :].astype(BF16)
        return 0

    lax.fori_loop(0, groups, project, 0)
    wide_update(nbr, wide, qc, wkeys, wvals, (m, l, acc), groups)


def third_kernel(nbr, hw, g0, g1, g2, w, wvt, qc, fkeys, fvals, m_in, l_in, acc_in,
                 m, l, acc, tokens, keys, vals):
    nlb = nbr.shape[0]
    lon, rows_c, width = g0.shape
    span = rows_c * CHUNKS // nlb
    rows = lon * span
    groups = width // WIDE
    fill_tokens((g0, g1, g2), tokens, rows, span, lon)

    def project(g, _):
        at = pl.multiple_of(g * WIDE, WIDE)
        k = dot(tokens[...], w[:, pl.ds(at, WIDE)]).astype(BF16)
        v = dot_nt(wvt[pl.ds(at, WIDE), :], tokens[...])
        for c in range(0, nlb, 2):
            first, second = halves(v[:, c * rows : (c + 2) * rows])
            for i, part in ((c, first), (c + 1, second)):
                keys[i, g, :rows] = fkeys[i, g]
                keys[i, g, rows:] = k[i * rows : (i + 1) * rows, :]
                vals[i, g] = fvals[i, g] + part[1].astype(BF16)
        return 0

    lax.fori_loop(0, groups, project, 0)

    def attend(b, _):
        c0, c1 = nbr[b, 0], nbr[b, 1]
        seen0, seen1 = hw[c0] >= 2, hw[c1] >= 2
        for g in range(groups):
            t = b * groups + g
            q = spread(qc[t])
            k = jnp.concatenate([keys[c0, g], keys[c1, g]], axis=0)
            v = jnp.concatenate([vals[c0, g], vals[c1, g]], axis=1)
            scores = dot(k, q)
            scores = jnp.concatenate(
                [
                    jnp.where(seen0, scores[: 2 * rows], NEVER),
                    jnp.where(seen1, scores[2 * rows :], NEVER),
                ],
                axis=0,
            )
            m[t], l[t], acc[t] = update(scores, v, (m_in[t], l_in[t], acc_in[t]))
        return 0

    lax.fori_loop(0, nlb, attend, 0)


def payload_kernel(flags, f0, f1, f2, g0, g1, g2, wf, wb, out):
    lon, rows_c, width = f0.shape
    span = wf.shape[0] // lon
    per = rows_c // span
    fs, gs = (f0, f1, f2), (g0, g1, g2)
    base = CHUNKS * lon * rows_c
    rows = lon * span

    def fill(sent, other, wide_sent):
        for j in range(CHUNKS):
            for c in range(per):
                for o in range(lon):
                    at = ((j * per + c) * lon + o) * span
                    out[at : at + span, :] = sent[j][o, c * span : (c + 1) * span, :]
        out[base : base + rows, :] = wide_sent[...]
        for j in range(CHUNKS):
            for c in range(per):

                @pl.when(flags[1] == j * per + c)
                def _(j=j, c=c):
                    for o in range(lon):
                        at = base + rows + o * span
                        out[at : at + span, :] = other[j][o, c * span : (c + 1) * span, :]

    @pl.when(flags[0] == 0)
    def _():
        fill(fs, gs, wb)

    @pl.when(flags[0] != 0)
    def _():
        fill(gs, fs, wf)


def fourth_kernel(nbr, wide, e, w, wvt, wout, qc, m_in, l_in, acc_in, out,
                  m, l, acc, keys, vals, wkeys, wvals, attended):
    nlb = nbr.shape[0]
    width = e.shape[1]
    rows = e.shape[0] // (nlb + 2)
    lon = out.shape[0]
    span = rows // lon
    groups = width // WIDE

    def project(g, _):
        at = pl.multiple_of(g * WIDE, WIDE)
        k = dot(e[...], w[:, pl.ds(at, WIDE)]).astype(BF16)
        v = dot_nt(wvt[pl.ds(at, WIDE), :], e[...])
        for c in range(0, nlb, 2):
            first, second = halves(v[:, c * rows : (c + 2) * rows])
            for i, part in ((c, first), (c + 1, second)):
                keys[i, g] = k[i * rows : (i + 1) * rows, :]
                vals[0, i, g] = part[0].astype(BF16)
                vals[1, i, g] = part[1].astype(BF16)
        wkeys[g] = k[nlb * rows :, :]
        wvals[g] = v[:, nlb * rows :].astype(BF16)
        return 0

    lax.fori_loop(0, groups, project, 0)

    def attend(b, _):
        c0, c1 = nbr[b, 0], nbr[b, 1]
        for g in range(groups):
            t = b * groups + g
            k = jnp.concatenate([keys[c0, g], keys[c1, g]], axis=0)
            v = vals[0, c0, g] + vals[1, c1, g]
            scores = dot(k, spread(qc[t]))
            m[t], l[t], acc[t] = update(scores, v, (m_in[t], l_in[t], acc_in[t]))
        return 0

    lax.fori_loop(0, nlb, attend, 0)
    wide_update(nbr, wide, qc, wkeys, wvals, (m, l, acc), groups)

    def finish(b, _):
        for g in range(groups):
            t = b * groups + g
            done = (acc[t] / l[t]).T
            attended[pl.ds(pl.multiple_of(b * rows, rows), rows), g * WIDE : (g + 1) * WIDE] = (
                jnp.concatenate(
                    [done[h * HEAD : (h + 1) * HEAD, :] for h in range(PACK)], axis=1
                ).astype(BF16)
            )
        return 0

    lax.fori_loop(0, nlb, finish, 0)

    def product(g, _):
        at = pl.multiple_of(g * WIDE, WIDE)
        r = dot(attended[...], wout[:, pl.ds(at, WIDE)]).astype(BF16)
        for b in range(nlb):
            for o in range(lon):
                out[o, b * span : (b + 1) * span, pl.ds(at, WIDE)] = r[
                    b * rows + o * span : b * rows + (o + 1) * span, :
                ]
        return 0

    lax.fori_loop(0, groups, product, 0)


def call(kernel, scalars, arrays, outs, scratch, flops):
    smem = pl.BlockSpec(memory_space=pltpu.SMEM)
    vmem = pl.BlockSpec(memory_space=pltpu.VMEM)
    single = not isinstance(outs, (list, tuple))
    moved = sum(a.size * a.dtype.itemsize for a in arrays)
    return pl.pallas_call(
        kernel,
        out_shape=outs,
        in_specs=[smem] * len(scalars) + [vmem] * len(arrays),
        out_specs=vmem if single else [vmem] * len(outs),
        scratch_shapes=scratch,
        compiler_params=pltpu.CompilerParams(vmem_limit_bytes=VMEM_LIMIT),
        cost_estimate=pl.CostEstimate(flops=flops, bytes_accessed=moved, transcendentals=0),
    )(*scalars, *arrays)


def per_device(tokens, projection, out_weight, half_width, neighbours):
    lon, lat, width = tokens.shape
    nlb = neighbours.shape[0]
    span = lat // nlb
    rows = lon * span
    groups = width // WIDE
    tiles = nlb * groups
    count = lax.axis_size("lon")
    here = lax.axis_index("lon")
    devices = range(count)

    def permute(block, step):
        return lax.ppermute(block, "lon", [(i, step(i) % count) for i in devices])

    def sibling(i):
        return i ^ 1

    def across(i):
        return i ^ 2

    def onward(i):
        return i - 4 if i & 2 else i + 4

    def backward(i):
        return i + 4 if i & 2 else i - 4

    widest = jnp.argmax(half_width).astype(jnp.int32)
    wide = widest.reshape(1)
    beside = permute(tokens, sibling)
    part = lat // CHUNKS
    f = [permute(tokens[:, j * part : (j + 1) * part, :], across) for j in range(CHUNKS)]
    band = lax.dynamic_slice(tokens, (0, widest * span, 0), (lon, span, width)).reshape(rows, width)
    wf = permute(band, onward)
    wb = permute(band, backward)
    g = [permute(block, onward) for block in f]

    tile = (tiles, HEAD, WIDE)
    row = (tiles, 1, WIDE)
    carried_shapes = [
        jax.ShapeDtypeStruct(row, F32),
        jax.ShapeDtypeStruct(row, F32),
        jax.ShapeDtypeStruct(tile, F32),
    ]
    qc, m, l, acc, wvt = call(
        first_kernel,
        (neighbours,),
        (tokens, beside, projection),
        [jax.ShapeDtypeStruct(tile, BF16)] + carried_shapes + [jax.ShapeDtypeStruct((width, width), BF16)],
        [
            pltpu.VMEM((nlb * rows, width), BF16),
            pltpu.VMEM((2 * nlb * rows, width), BF16),
            pltpu.VMEM((nlb, groups, 2 * rows, WIDE), BF16),
            pltpu.VMEM((nlb, groups, WIDE, 2 * rows), BF16),
        ],
        6_000_000_000,
    )
    wk = projection[:, width : 2 * width]
    fkeys, fvals, m, l, acc = call(
        second_kernel,
        (neighbours, wide),
        (*f, wf, wb, wk, wvt, qc, m, l, acc),
        [
            jax.ShapeDtypeStruct((nlb, groups, rows, WIDE), BF16),
            jax.ShapeDtypeStruct((nlb, groups, WIDE, 2 * rows), BF16),
        ]
        + carried_shapes,
        [
            pltpu.VMEM(((nlb + 2) * rows, width), BF16),
            pltpu.VMEM((groups, 2 * rows, WIDE), BF16),
            pltpu.VMEM((groups, WIDE, 2 * rows), BF16),
        ],
        3_000_000_000,
    )
    kind = (here ^ (here >> 1)) & 1
    flags = jnp.stack([kind.astype(jnp.int32), widest])
    e = call(
        payload_kernel,
        (flags,),
        (*f, *g, wf, wb),
        jax.ShapeDtypeStruct(((nlb + 2) * rows, width), BF16),
        [],
        1_000_000,
    )
    e = permute(e, sibling)
    m, l, acc = call(
        third_kernel,
        (neighbours, half_width),
        (*g, wk, wvt, qc, fkeys, fvals, m, l, acc),
        carried_shapes,
        [
            pltpu.VMEM((nlb * rows, width), BF16),
            pltpu.VMEM((nlb, groups, 2 * rows, WIDE), BF16),
            pltpu.VMEM((nlb, groups, WIDE, 2 * rows), BF16),
        ],
        4_000_000_000,
    )
    return call(
        fourth_kernel,
        (neighbours, wide),
        (e, wk, wvt, out_weight, qc, m, l, acc),
        jax.ShapeDtypeStruct(tokens.shape, BF16),
        [
            pltpu.VMEM(row, F32),
            pltpu.VMEM(row, F32),
            pltpu.VMEM(tile, F32),
            pltpu.VMEM((nlb, groups, rows, WIDE), BF16),
            pltpu.VMEM((2, nlb, groups, WIDE, 2 * rows), BF16),
            pltpu.VMEM((groups, 2 * rows, WIDE), BF16),
            pltpu.VMEM((groups, WIDE, 2 * rows), BF16),
            pltpu.VMEM((nlb * rows, width), BF16),
        ],
        4_000_000_000,
    )


def solution(mesh):
    return jax.shard_map(
        per_device,
        mesh=mesh,
        in_specs=(P(("groups", "lon"), None, None), P(), P(), P(), P()),
        out_specs=P(("groups", "lon"), None, None),
        check_vma=False,
    )
```

time: 200 us -> 81.6 us (0.41)
  local copies, waits for them, and re-layouts: 90.3 us -> 8.06 us
  matrix products: 67.6 us -> 0 us
  Pallas kernels: 0 us -> 42.3 us
  other arithmetic: 12.1 us -> 2.07 us
  waiting for transfers between devices: 5.1 us -> 14.2 us
  starting transfers between devices: 20.2 us -> 14.5 us
  between operations: 4.07 us -> 0.75 us
    dot_general x20 -> x0, matrix products: 67.6 us -> none  [the longest x9 33 us: attend(): jnp.einsum(form_scores, queries, key_part, preferred_element_type=jnp.flo...]
    pallas_call x0 -> x5, Pallas kernels: none -> 42.3 us  [call(): pl.pallas_call(kernel, out_shape=outs, in_specs=[smem] * len(scalars) + [...]
    unnamed x108 -> x9, local copies, waits for them, and re-layouts: 31 us -> 3.56 us
    slice x16 -> x2, local copies, waits for them, and re-layouts: 24.7 us -> 2.92 us  [the longest x1 1.76 us: per_device(): wk = projection[:, width:2 * width]]
    gather x6 -> x0, local copies, waits for them, and re-layouts: 20.3 us -> none  [the longest x5 19.6 us: band_rows(): key_band[neighbours].reshape(neighbours.shape[0], -1, key_band.shape[2])]
    ppermute x8 -> x10, waiting for transfers between devices: 5.1 us -> 14.2 us  [permute(): return lax.ppermute(block, 'lon', [(i, step(i) % count) for i in devices])]
    reduce_sum x3 -> x0, other arithmetic: 9.09 us -> none  [attend(): running_sum = running_sum * factor + jnp.sum(exponent, axis=-1)]
    ppermute x8 -> x10, starting transfers between devices: 20.2 us -> 14.5 us  [permute(): return lax.ppermute(block, 'lon', [(i, step(i) % count) for i in devices])]
  transfers between devices with their start and end apart: 8 -> 10, of which waited for: 2 -> 3; matrix products, arithmetic and copies ran while one was open for 57% -> 9% of each run, Pallas kernels for 0% -> 34%
where the time goes in v1:
time: 81.6 us; the launch traced here: 81.9 us
  Pallas kernels  42.3 us (52%)
  starting transfers between devices  14.5 us (18%)
  waiting for transfers between devices  14.2 us (17%)
  local copies, waits for them, and re-layouts  8.06 us (10%)
  other arithmetic  2.07 us (3%)
    pallas_call x5, Pallas kernels, call(): pl.pallas_call(kernel, out_shape=outs, in_specs=[smem] * len(scalars) + [...  42.3 us
    ppermute x10, starting transfers between devices, permute(): return lax.ppermute(block, 'lon', [(i, step(i) % count) for i in devices])  14.5 us
    ppermute x10, waiting for transfers between devices, permute(): return lax.ppermute(block, 'lon', [(i, step(i) % count) for i in devices])  14.2 us
    unnamed x9, local copies, waits for them, and re-layouts  3.56 us
    slice x1, local copies, waits for them, and re-layouts, per_device(): wk = projection[:, width:2 * width]  1.76 us
  transfers between devices with their start and end apart: 10, of which 3 were waited for; matrix products, arithmetic and copies ran while one was open for 9% of the time, Pallas kernels for 34%

profile of v1, /device:TPU:0, one launch (start us, length us, event | category | flops | bytes accessed | tf_op | source)
XLA Modules:
  0.0 81.9 jit_solution(17553802374515083156)
XLA Ops:
  0.0 0.5 collective-permute-start.9
  0.5 1.2 %fusion = (bf16[2,64,1024]{2,1,0:T(8,128)(2,1)S(1)}, bf16[2,64,1024]{2,1,0:T(8,128)(2,1)S(1)}, bf16[2,64,1024]{2,1,0:T(8,128)(2,1)S(1)}) fusion(bf16[2,192,1024]{2,1,0:T(8,128)(2,1)} %x.1), kind=kLoop, calls=%fused_computation.3 | loop fusion | bytes 1572864 | tf_op jit(solution)/shard_map/slice | solution.py:370
  1.6 2.6 %collective-permute-start = (bf16[2,64,1024]{2,1,0:T(8,128)(2,1)S(1)}, bf16[2,64,1024]{2,1,0:T(8,128)(2,1)S(1)}, u32[]{:S(2)}, u32[]{:S(2)}) collective-permute-start(bf16[2,64,1024]{2,1,0:T(8,128)(2,1)S(1)} %get-tuple-element.35), channel_id=1, source_target_pairs={{0,2},{1,3},{2,0},{3,1},{4,6},{5,7},{6,4},{7,5},{8,10},{9,11},{10,... | collective-permute-start | bytes 786440 | tf_op jit(solution)/shard_map/ppermute | solution.py:352
  4.3 1.9 %collective-permute-start.2 = (bf16[2,64,1024]{2,1,0:T(8,128)(2,1)S(1)}, bf16[2,64,1024]{2,1,0:T(8,128)(2,1)}, u32[]{:S(2)}, u32[]{:S(2)}) collective-permute-start(bf16[2,64,1024]{2,1,0:T(8,128)(2,1)S(1)} %get-tuple-element.33), channel_id=1, source_target_pairs={{0,2},{1,3},{2,0},{3,1},{4,6},{5,7},{6,4},{7,5},{8,10},{9,11},{10,... | collective-permute-start | bytes 786440 | tf_op jit(solution)/shard_map/ppermute | solution.py:352
  6.2 1.3 %iota_reduce_fusion = (s32[]{:T(128)}, s32[]{:T(128)}) fusion(s32[6]{0:T(128)} %hw.1), kind=kLoop, calls=%fused_computation.1 | loop fusion | flops 35 | bytes 32 | tf_op jit(solution)/shard_map/per_device/reduce | solution.py:366
  8.2 1.6 %constant_dynamic-slice_fusion = bf16[2,32,1024]{2,1,0:T(8,128)(2,1)} fusion(bf16[2,192,1024]{2,1,0:T(8,128)(2,1)} %x.1, s32[]{:T(128)S(6)} %select_n.7), kind=kLoop, calls=%fused_computation.2 | loop fusion | bytes 262148 | tf_op jit(solution)/shard_map/dynamic_slice | solution.py:371
  9.7 1.6 %collective-permute-start.6 = (bf16[64,1024]{1,0:T(8,128)(2,1)}, bf16[64,1024]{1,0:T(8,128)(2,1)S(1)}, u32[]{:S(2)}, u32[]{:S(2)}) collective-permute-start(bf16[64,1024]{1,0:T(8,128)(2,1)} %bitcast.2), channel_id=1, source_target_pairs={{0,4},{1,5},{2,14},{3,15},{4,8},{5,9},{6,2},{7,3},{8,12},{9,13},{1... | collective-permute-start | bytes 393224 | tf_op jit(solution)/shard_map/ppermute | solution.py:352
  11.4 2.0 %collective-permute-start.3 = (bf16[2,64,1024]{2,1,0:T(8,128)(2,1)S(1)}, bf16[2,64,1024]{2,1,0:T(8,128)(2,1)}, u32[]{:S(2)}, u32[]{:S(2)}) collective-permute-start(bf16[2,64,1024]{2,1,0:T(8,128)(2,1)S(1)} %collective-permute-done.f0), channel_id=1, source_target_pairs={{0,4},{1,5},{2,14},{3,15},{4,8},{5,9},{6,2},{7,3},{8,12},{9,13},{1... | collective-permute-start | bytes 786440 | tf_op jit(solution)/shard_map/ppermute | solution.py:352
  13.4 3.6 %collective-permute-done.1.f1 = bf16[2,64,1024]{2,1,0:T(8,128)(2,1)S(1)} collective-permute-done((bf16[2,64,1024]{2,1,0:T(8,128)(2,1)S(1)}, bf16[2,64,1024]{2,1,0:T(8,128)(2,1)S(1)}, u32[]{:S(2)}, u32[]{:S(2)}) %collective-permute-start.1) | collective-permute-done | bytes 262176 | tf_op jit(solution)/shard_map/ppermute | solution.py:352
  17.0 2.0 %collective-permute-start.4 = (bf16[2,64,1024]{2,1,0:T(8,128)(2,1)S(1)}, bf16[2,64,1024]{2,1,0:T(8,128)(2,1)}, u32[]{:S(2)}, u32[]{:S(2)}) collective-permute-start(bf16[2,64,1024]{2,1,0:T(8,128)(2,1)S(1)} %collective-permute-done.1.f1), channel_id=1, source_target_pairs={{0,4},{1,5},{2,14},{3,15},{4,8},{5,9},{6,2},{7,3},{8,12},{9,13},{1... | collective-permute-start | bytes 786440 | tf_op jit(solution)/shard_map/ppermute | solution.py:352
  19.0 3.5 %collective-permute-done.2.f2 = bf16[2,64,1024]{2,1,0:T(8,128)(2,1)} collective-permute-done((bf16[2,64,1024]{2,1,0:T(8,128)(2,1)S(1)}, bf16[2,64,1024]{2,1,0:T(8,128)(2,1)}, u32[]{:S(2)}, u32[]{:S(2)}) %collective-permute-start.2) | collective-permute-done | bytes 262176 | tf_op jit(solution)/shard_map/ppermute | solution.py:352
  22.5 1.8 %collective-permute-start.5 = (bf16[2,64,1024]{2,1,0:T(8,128)(2,1)}, bf16[2,64,1024]{2,1,0:T(8,128)(2,1)}, u32[]{:S(2)}, u32[]{:S(2)}) collective-permute-start(bf16[2,64,1024]{2,1,0:T(8,128)(2,1)} %collective-permute-done.2.f2), channel_id=1, source_target_pairs={{0,4},{1,5},{2,14},{3,15},{4,8},{5,9},{6,2},{7,3},{8,12},{9,13},{1... | collective-permute-start | bytes 786440 | tf_op jit(solution)/shard_map/ppermute | solution.py:352
  24.3 2.0 %collective-permute-start.7 = (bf16[64,1024]{1,0:T(8,128)(2,1)}, bf16[64,1024]{1,0:T(8,128)(2,1)}, u32[]{:S(2)}, u32[]{:S(2)}) collective-permute-start(bf16[64,1024]{1,0:T(8,128)(2,1)} %bitcast.2), channel_id=1, source_target_pairs={{0,12},{1,13},{2,6},{3,7},{4,0},{5,1},{6,10},{7,11},{8,4},{9,5},{1... | collective-permute-start | bytes 393224 | tf_op jit(solution)/shard_map/ppermute | solution.py:352
  26.3 0.8 copy.9.nbr
  27.1 1.8 %slice.15.w = bf16[1024,1024]{1,0:T(8,128)(2,1)S(1)} slice(bf16[1024,3072]{1,0:T(8,128)(2,1)} %w.1), slice={[0:1024], [1024:2048]} | slice | bytes 4194304 | tf_op jit(solution)/shard_map/slice | solution.py:396
  28.9 0.8 pad_add_fusion.flags
  29.7 7.0 %collective-permute-done.7.wb = bf16[64,1024]{1,0:T(8,128)(2,1)} collective-permute-done((bf16[64,1024]{1,0:T(8,128)(2,1)}, bf16[64,1024]{1,0:T(8,128)(2,1)}, u32[]{:S(2)}, u32[]{:S(2)}) %collective-permute-start.7) | collective-permute-done | bytes 131104 | tf_op jit(solution)/shard_map/ppermute | solution.py:352
  36.7 1.3 %shard_map.55 = bf16[512,1024]{1,0:T(8,128)(2,1)S(1)} custom-call(s32[2]{0:T(128)S(1)} %pad_add_fusion.flags, bf16[2,64,1024]{2,1,0:T(8,128)(2,1)S(1)} %collective-permute-done.f0, bf16[2,64,1024]{2,1,0:T(8,128)(2,1)S(1)} %collective-permute-done.1.f1, bf16[2,64,1024]{2,1,0:T(8,128)(2,1)} %collective-permute-done.2.f2, ...), custom_call_target="tpu_custom_call" | custom-call | flops 1000000 | bytes 1835008 | tf_op jit(solution)/shard_map/pallas_call | solution.py:329
  38.0 0.1 collective-permute-start.8
  38.1 2.8 %copy-done.1 = bf16[1024,3072]{1,0:T(8,128)(2,1)S(1)} copy-done((bf16[1024,3072]{1,0:T(8,128)(2,1)S(1)}, bf16[1024,3072]{1,0:T(8,128)(2,1)}, u32[]{:S(2)}) %copy-start.1) | copy-done | bytes 6291480
  40.9 11.1 %shard_map.56 = (bf16[24,64,256]{2,1,0:T(8,128)(2,1)S(1)}, f32[24,1,256]{2,1,0:T(1,128)S(1)}, f32[24,1,256]{2,1,0:T(1,128)S(1)}, f32[24,64,256]{2,1,0:T(8,128)S(1)}, bf16[1024,1024]{1,0:T(8,128)(2,1)S(1)}) custom-call(s32[6,2]{1,0:T(8,128)S(1)} %copy.9.nbr, bf16[2,192,1024]{2,1,0:T(8,128)(2,1)S(1)} %copy-done, ...), custom_call_target="tpu_custom_call" | custom-call | flops 6000000000 | bytes 7864320 | tf_op jit(solution)/shard_map/pallas_call | solution.py:329
  52.1 6.5 %shard_map.57 = (bf16[6,4,64,256]{3,2,1,0:T(8,128)(2,1)S(1)}, bf16[6,4,256,128]{3,2,1,0:T(8,128)(2,1)S(1)}, f32[24,1,256]{2,1,0:T(1,128)S(1)}, f32[24,1,256]{2,1,0:T(1,128)S(1)}, f32[24,64,256]{2,1,0:T(8,128)S(1)}) custom-call(s32[6,2]{1,0:T(8,128)S(1)} %copy.9.nbr, s32[1]{0:T(128)} %bitcast.wide, bf16[2,64,1024]{2,1,0:T(8,128)(2,1)S(1)} %collective-permute-done.f0, ...), custom_call_target="tpu_custom_call" | custom-call | flops 3000000000 | bytes 7651328 | tf_op jit(solution)/shard_map/pallas_call | solution.py:329
  58.6 8.6 %shard_map.58 = (f32[24,1,256]{2,1,0:T(1,128)S(1)}, f32[24,1,256]{2,1,0:T(1,128)S(1)}, f32[24,64,256]{2,1,0:T(8,128)S(1)}) custom-call(s32[6,2]{1,0:T(8,128)S(1)} %copy.9.nbr, s32[6]{0:T(128)S(1)} %copy-done.3, bf16[2,64,1024]{2,1,0:T(8,128)(2,1)} %collective-permute-done.3.g0, bf16[2,64,1024]{2,1,0:T(8,128)(2,1)} %collective-permute-done.4.g1, ...), custom_call_target="tpu_custom_call" | custom-call | flops 4000000000 | bytes 9748480 | tf_op jit(solution)/shard_map/pallas_call | solution.py:329
  67.2 14.7 %shard_map.59 = bf16[2,192,1024]{2,1,0:T(8,128)(2,1)} custom-call(s32[6,2]{1,0:T(8,128)S(1)} %copy.9.nbr, s32[1]{0:T(128)} %bitcast.wide, bf16[512,1024]{1,0:T(8,128)(2,1)S(1)} %collective-permute-done.8.e, bf16[1024,1024]{1,0:T(8,128)(2,1)S(1)} %slice.15.w, bf16[1024,1024]{1,0:T(8,128)(2,1)S(1)} %get-tuple-element.20.wvt, bf16[1024,1024]{1,0:T(8,128)(2,1)S(1)} %copy-done.2, ...), custom_call_target="tpu_custom_call" | custom-call | flops 4000000000 | bytes 9748480 | tf_op jit(solution)/shard_map/pallas_call | solution.py:329
  (15 shorter events, 0.2 us)
Async XLA Ops:
  0.0 38.1 %collective-permute-start.9 = (bf16[2,192,1024]{2,1,0:T(8,128)(2,1)}, bf16[2,192,1024]{2,1,0:T(8,128)(2,1)}, u32[]{:S(2)}, u32[]{:S(2)}) collective-permute-start(bf16[2,192,1024]{2,1,0:T(8,128)(2,1)} %x.1), channel_id=1, source_target_pairs={{0,1},{1,0},{2,3},{3,2},{4,5},{5,4},{6,7},{7,6},{8,9},{9,8},{10,11... | collective-permute-start | bytes 2359304 | tf_op jit(solution)/shard_map/ppermute | solution.py:352
  1.6 9.7 %collective-permute-start = (bf16[2,64,1024]{2,1,0:T(8,128)(2,1)S(1)}, bf16[2,64,1024]{2,1,0:T(8,128)(2,1)S(1)}, u32[]{:S(2)}, u32[]{:S(2)}) collective-permute-start(bf16[2,64,1024]{2,1,0:T(8,128)(2,1)S(1)} %get-tuple-element.35), channel_id=1, source_target_pairs={{0,2},{1,3},{2,0},{3,1},{4,6},{5,7},{6,4},{7,5},{8,10},{9,11},{10,... | collective-permute-start | bytes 786440 | tf_op jit(solution)/shard_map/ppermute | solution.py:352
  4.2 12.8 %collective-permute-start.1 = (bf16[2,64,1024]{2,1,0:T(8,128)(2,1)S(1)}, bf16[2,64,1024]{2,1,0:T(8,128)(2,1)S(1)}, u32[]{:S(2)}, u32[]{:S(2)}) collective-permute-start(bf16[2,64,1024]{2,1,0:T(8,128)(2,1)S(1)} %get-tuple-element.34), channel_id=1, source_target_pairs={{0,2},{1,3},{2,0},{3,1},{4,6},{5,7},{6,4},{7,5},{8,10},{9,11},{10,... | collective-permute-start | bytes 786440 | tf_op jit(solution)/shard_map/ppermute | solution.py:352
  4.3 18.2 %collective-permute-start.2 = (bf16[2,64,1024]{2,1,0:T(8,128)(2,1)S(1)}, bf16[2,64,1024]{2,1,0:T(8,128)(2,1)}, u32[]{:S(2)}, u32[]{:S(2)}) collective-permute-start(bf16[2,64,1024]{2,1,0:T(8,128)(2,1)S(1)} %get-tuple-element.33), channel_id=1, source_target_pairs={{0,2},{1,3},{2,0},{3,1},{4,6},{5,7},{6,4},{7,5},{8,10},{9,11},{10,... | collective-permute-start | bytes 786440 | tf_op jit(solution)/shard_map/ppermute | solution.py:352
  9.7 14.6 %collective-permute-start.6 = (bf16[64,1024]{1,0:T(8,128)(2,1)}, bf16[64,1024]{1,0:T(8,128)(2,1)S(1)}, u32[]{:S(2)}, u32[]{:S(2)}) collective-permute-start(bf16[64,1024]{1,0:T(8,128)(2,1)} %bitcast.2), channel_id=1, source_target_pairs={{0,4},{1,5},{2,14},{3,15},{4,8},{5,9},{6,2},{7,3},{8,12},{9,13},{1... | collective-permute-start | bytes 393224 | tf_op jit(solution)/shard_map/ppermute | solution.py:352
  11.4 25.3 %collective-permute-start.3 = (bf16[2,64,1024]{2,1,0:T(8,128)(2,1)S(1)}, bf16[2,64,1024]{2,1,0:T(8,128)(2,1)}, u32[]{:S(2)}, u32[]{:S(2)}) collective-permute-start(bf16[2,64,1024]{2,1,0:T(8,128)(2,1)S(1)} %collective-permute-done.f0), channel_id=1, source_target_pairs={{0,4},{1,5},{2,14},{3,15},{4,8},{5,9},{6,2},{7,3},{8,12},{9,13},{1... | collective-permute-start | bytes 786440 | tf_op jit(solution)/shard_map/ppermute | solution.py:352
  17.0 19.7 %collective-permute-start.4 = (bf16[2,64,1024]{2,1,0:T(8,128)(2,1)S(1)}, bf16[2,64,1024]{2,1,0:T(8,128)(2,1)}, u32[]{:S(2)}, u32[]{:S(2)}) collective-permute-start(bf16[2,64,1024]{2,1,0:T(8,128)(2,1)S(1)} %collective-permute-done.1.f1), channel_id=1, source_target_pairs={{0,4},{1,5},{2,14},{3,15},{4,8},{5,9},{6,2},{7,3},{8,12},{9,13},{1... | collective-permute-start | bytes 786440 | tf_op jit(solution)/shard_map/ppermute | solution.py:352
  22.5 14.1 %collective-permute-start.5 = (bf16[2,64,1024]{2,1,0:T(8,128)(2,1)}, bf16[2,64,1024]{2,1,0:T(8,128)(2,1)}, u32[]{:S(2)}, u32[]{:S(2)}) collective-permute-start(bf16[2,64,1024]{2,1,0:T(8,128)(2,1)} %collective-permute-done.2.f2), channel_id=1, source_target_pairs={{0,4},{1,5},{2,14},{3,15},{4,8},{5,9},{6,2},{7,3},{8,12},{9,13},{1... | collective-permute-start | bytes 786440 | tf_op jit(solution)/shard_map/ppermute | solution.py:352
  24.3 12.3 %collective-permute-start.7 = (bf16[64,1024]{1,0:T(8,128)(2,1)}, bf16[64,1024]{1,0:T(8,128)(2,1)}, u32[]{:S(2)}, u32[]{:S(2)}) collective-permute-start(bf16[64,1024]{1,0:T(8,128)(2,1)} %bitcast.2), channel_id=1, source_target_pairs={{0,12},{1,13},{2,6},{3,7},{4,0},{5,1},{6,10},{7,11},{8,4},{9,5},{1... | collective-permute-start | bytes 393224 | tf_op jit(solution)/shard_map/ppermute | solution.py:352
  28.9 9.2 %copy-start = (bf16[2,192,1024]{2,1,0:T(8,128)(2,1)S(1)}, bf16[2,192,1024]{2,1,0:T(8,128)(2,1)}, u32[]{:S(2)}) copy-start(bf16[2,192,1024]{2,1,0:T(8,128)(2,1)} %x.1) | copy-start | bytes 2359300
  38.0 29.2 %collective-permute-start.8 = (bf16[512,1024]{1,0:T(8,128)(2,1)S(1)}, bf16[512,1024]{1,0:T(8,128)(2,1)S(1)}, u32[]{:S(2)}, u32[]{:S(2)}) collective-permute-start(bf16[512,1024]{1,0:T(8,128)(2,1)S(1)} %shard_map.55), channel_id=1, source_target_pairs={{0,1},{1,0},{2,3},{3,2},{4,5},{5,4},{6,7},{7,6},{8,9},{9,8},{10,11... | collective-permute-start | bytes 3145736 | tf_op jit(solution)/shard_map/ppermute | solution.py:352
  38.1 2.8 %copy-start.1 = (bf16[1024,3072]{1,0:T(8,128)(2,1)S(1)}, bf16[1024,3072]{1,0:T(8,128)(2,1)}, u32[]{:S(2)}) copy-start(bf16[1024,3072]{1,0:T(8,128)(2,1)} %w.1) | copy-start | bytes 18874372
  52.1 6.6 %copy-start.3 = (s32[6]{0:T(128)S(1)}, s32[6]{0:T(128)}, u32[]{:S(2)}) copy-start(s32[6]{0:T(128)} %hw.1) | copy-start | bytes 76
  58.6 8.6 %copy-start.2 = (bf16[1024,1024]{1,0:T(8,128)(2,1)S(1)}, bf16[1024,1024]{1,0:T(8,128)(2,1)}, u32[]{:S(2)}) copy-start(bf16[1024,1024]{1,0:T(8,128)(2,1)} %wout.1) | copy-start | bytes 6291460

commit v2 on v0

v2 whole, which is shorter than its diff:
```python
import math

import jax
import jax.numpy as jnp
from jax import lax
from jax.experimental import pallas as pl
from jax.experimental.pallas import tpu as pltpu
from jax.sharding import PartitionSpec as P

HEADS = 16
HEAD = 64
PACK = 4
WIDE = PACK * HEAD
CHUNKS = 3
NEVER = -1e37
BF16 = jnp.bfloat16
F32 = jnp.float32
SCALE = math.log2(math.e) / math.sqrt(HEAD)
VMEM_LIMIT = 40 * 1024 * 1024


def lane_head(shape):
    return lax.broadcasted_iota(jnp.int32, shape, len(shape) - 1) // HEAD


def spread(packed):
    lane = lane_head((1, WIDE))
    return jnp.concatenate(
        [packed * (lane == h).astype(F32).astype(BF16) for h in range(PACK)], axis=0
    )


def gather_diagonal(full):
    lane = lane_head((HEAD, WIDE))
    total = full[:HEAD]
    for h in range(1, PACK):
        total = jnp.where(lane == h, full[h * HEAD : (h + 1) * HEAD], total)
    return total


def dot(a, b):
    return jnp.dot(a, b, preferred_element_type=F32)


def dot_nt(a, b):
    return lax.dot_general(a, b, (((1,), (1,)), ((), ())), preferred_element_type=F32)


def update(scores, values_t, carried):
    row_max, total, summed = carried
    new_max = jnp.maximum(row_max, jnp.max(scores, axis=0, keepdims=True))
    exponent = jnp.exp2((scores - new_max) * SCALE)
    factor = jnp.exp2((row_max - new_max) * SCALE)
    total = total * factor + jnp.sum(exponent, axis=0, keepdims=True)
    summed = summed * factor + gather_diagonal(dot(values_t, exponent.astype(BF16)))
    return new_max, total, summed


def halves(pair):
    lane = lax.broadcasted_iota(jnp.int32, pair.shape, 1)
    turned = pltpu.roll(pair, HEAD, 1)
    low = lane < HEAD
    zero = jnp.zeros_like(pair)
    first = (jnp.where(low, pair, zero), jnp.where(low, zero, turned))
    second = (jnp.where(low, turned, zero), jnp.where(low, zero, pair))
    return first, second


def widest_of(hw):
    best, where = hw[0], 0
    for c in range(1, hw.shape[0]):
        larger = hw[c] > best
        best = jnp.where(larger, hw[c], best)
        where = jnp.where(larger, c, where)
    return where


def project_values(wvt, tokens, g, blocks, rows):
    v = dot_nt(wvt[g * WIDE : (g + 1) * WIDE, :], tokens)
    parts = []
    for c in range(0, blocks, 2):
        for left, right in halves(v[:, c * rows : (c + 2) * rows]):
            parts.append((left.astype(BF16), right.astype(BF16)))
    return parts, v[:, blocks * rows :].astype(BF16)


def columns(which, g, width):
    return slice(which * width + g * WIDE, which * width + (g + 1) * WIDE)


def prepare_kernel(hw, x, f0, f1, f2, band):
    lon, lat, width = x.shape
    span = lat // hw.shape[0]
    out = (f0, f1, f2)
    per = hw.shape[0] // CHUNKS
    for c in range(hw.shape[0]):
        for o in range(lon):
            at = ((c % per) * lon + o) * span
            out[c // per][at : at + span, :] = x[o, c * span : (c + 1) * span, :]
    begin = pl.multiple_of(widest_of(hw) * span, span)
    for o in range(lon):
        band[o * span : (o + 1) * span, :] = x[o, pl.ds(begin, span), :]


def own_kernel(x, w, qc, keys, vals, wvt, own):
    lon, _, width = x.shape
    nlb, groups, rows, _ = keys.shape
    span = rows // lon
    for c in range(nlb):
        for o in range(lon):
            own[c * rows + o * span : c * rows + (o + 1) * span, :] = x[o, c * span : (c + 1) * span, :]
    for i in range(0, width, WIDE):
        wvt[i : i + WIDE, :] = w[:, 2 * width + i : 2 * width + i + WIDE].T
    for g in range(groups):
        q = dot(own[...], w[:, columns(0, g, width)]).astype(BF16).astype(F32)
        for b in range(nlb):
            qt = q[b * rows : (b + 1) * rows, :].T
            qc[b * groups + g] = jnp.concatenate(
                [qt[h * HEAD : (h + 1) * HEAD, :] for h in range(PACK)], axis=1
            ).astype(BF16)
        k = dot(own[...], w[:, columns(1, g, width)]).astype(BF16)
        parts, _ = project_values(wvt, own[...], g, nlb, rows)
        for c in range(nlb):
            keys[c, g] = k[c * rows : (c + 1) * rows, :]
            vals[c, g] = parts[c][0]


def near_kernel(nbr, s, w, wvt, qc, okeys, ovals, m, l, acc, near, keys, vals):
    lon, _, width = s.shape
    nlb, groups, rows, _ = okeys.shape
    span = rows // lon
    for c in range(nlb):
        for o in range(lon):
            near[c * rows + o * span : c * rows + (o + 1) * span, :] = s[o, c * span : (c + 1) * span, :]
    for g in range(groups):
        k = dot(near[...], w[:, columns(1, g, width)]).astype(BF16)
        parts, _ = project_values(wvt, near[...], g, nlb, rows)
        for c in range(nlb):
            keys[c, g, :rows] = okeys[c, g]
            keys[c, g, rows:] = k[c * rows : (c + 1) * rows, :]
            vals[c, g] = ovals[c, g] + parts[c][1]
    for b in range(nlb):
        c0, c1 = nbr[b, 0], nbr[b, 1]
        for g in range(groups):
            t = b * groups + g
            k = jnp.concatenate([keys[c0, g], keys[c1, g]], axis=0)
            v = jnp.concatenate([vals[c0, g], vals[c1, g]], axis=1)
            scores = dot(k, spread(qc[t]))
            row_max = jnp.max(scores, axis=0, keepdims=True)
            exponent = jnp.exp2((scores - row_max) * SCALE)
            m[t] = row_max
            l[t] = jnp.sum(exponent, axis=0, keepdims=True)
            acc[t] = gather_diagonal(dot(v, exponent.astype(BF16)))


def project_far(tokens, w, wvt, keys, vals, wkeys, wvals):
    nlb, groups, rows, _ = keys.shape
    width = tokens.shape[1]
    for g in range(groups):
        k = dot(tokens[...], w[:, columns(1, g, width)]).astype(BF16)
        parts, rest = project_values(wvt, tokens[...], g, nlb, rows)
        for c in range(nlb):
            keys[c, g] = k[c * rows : (c + 1) * rows, :]
            vals[0, c, g] = parts[c][0]
            vals[1, c, g] = parts[c][1]
        if wkeys is not None:
            wkeys[g] = k[nlb * rows :, :]
            wvals[g] = rest


def attend_far(nbr, seen, wide, qc, keys, vals, wkeys, wvals, before, after):
    nlb, groups, rows, _ = keys.shape
    for b in range(nlb):
        c0, c1 = nbr[b, 0], nbr[b, 1]
        for g in range(groups):
            t = b * groups + g
            q = spread(qc[t])
            ks = [keys[c0, g], keys[c1, g]]
            v = vals[0, c0, g] + vals[1, c1, g]
            if wkeys is not None:
                ks.append(wkeys[g])
                v = jnp.concatenate([v, wvals[g]], axis=1)
            scores = dot(jnp.concatenate(ks, axis=0), q)
            pieces = [scores[:rows], scores[rows : 2 * rows], scores[2 * rows :]]
            if seen is not None:
                pieces[0] = jnp.where(seen[c0] >= 2, pieces[0], NEVER)
                pieces[1] = jnp.where(seen[c1] >= 2, pieces[1], NEVER)
            if wkeys is None:
                pieces = pieces[:2]
            else:
                pieces[2] = jnp.where((c0 == wide) | (c1 == wide), pieces[2], NEVER)
            scores = jnp.concatenate(pieces, axis=0)
            m, l, acc = update(scores, v, tuple(r[t] for r in before))
            after[0][t], after[1][t], after[2][t] = m, l, acc


def across_kernel(nbr, hw, f0, f1, f2, wf, wb, w, wvt, qc, m_in, l_in, acc_in,
                  m, l, acc, tokens, keys, vals, wkeys, wvals):
    at = 0
    for part in (f0, f1, f2, wf, wb):
        tokens[at : at + part.shape[0], :] = part[...]
        at += part.shape[0]
    project_far(tokens, w, wvt, keys, vals, wkeys, wvals)
    attend_far(nbr, hw, widest_of(hw), qc, keys, vals, wkeys, wvals, (m_in, l_in, acc_in), (m, l, acc))


def onward_kernel(nbr, hw, g0, g1, g2, w, wvt, qc, m_in, l_in, acc_in, m, l, acc, tokens, keys, vals):
    at = 0
    for part in (g0, g1, g2):
        tokens[at : at + part.shape[0], :] = part[...]
        at += part.shape[0]
    project_far(tokens, w, wvt, keys, vals, None, None)
    attend_far(nbr, hw, None, qc, keys, vals, None, None, (m_in, l_in, acc_in), (m, l, acc))


def payload_kernel(hw, f0, f1, f2, g0, g1, g2, wf, wb, _, out):
    here = lax.axis_index("lon")
    wide = widest_of(hw)
    size = f0.shape[0]
    rows = wf.shape[0]
    per = size // rows
    base = CHUNKS * size

    def fill(sent, other, wide_sent):
        for j in range(CHUNKS):
            out[j * size : (j + 1) * size, :] = sent[j][...]
        out[base : base + rows, :] = wide_sent[...]
        for c in range(CHUNKS * per):

            @pl.when(wide == c)
            def _(c=c):
                at = (c % per) * rows
                out[base + rows :, :] = other[c // per][at : at + rows, :]

    kind = (here ^ (here >> 1)) & 1

    @pl.when(kind == 0)
    def _():
        fill((f0, f1, f2), (g0, g1, g2), wb)

    @pl.when(kind != 0)
    def _():
        fill((g0, g1, g2), (f0, f1, f2), wf)


def last_kernel(nbr, hw, e, w, wvt, wout, qc, m_in, l_in, acc_in, out,
                m, l, acc, keys, vals, wkeys, wvals, attended):
    nlb, groups, rows, _ = keys.shape
    lon = out.shape[0]
    span = rows // lon
    project_far(e, w, wvt, keys, vals, wkeys, wvals)
    attend_far(nbr, None, widest_of(hw), qc, keys, vals, wkeys, wvals, (m_in, l_in, acc_in), (m, l, acc))
    for b in range(nlb):
        for g in range(groups):
            t = b * groups + g
            done = (acc[t] / l[t]).T
            attended[b * rows : (b + 1) * rows, g * WIDE : (g + 1) * WIDE] = jnp.concatenate(
                [done[h * HEAD : (h + 1) * HEAD, :] for h in range(PACK)], axis=1
            ).astype(BF16)
    for g in range(groups):
        r = dot(attended[...], wout[:, columns(0, g, 0)]).astype(BF16)
        for b in range(nlb):
            for o in range(lon):
                at = b * rows + o * span
                out[o, b * span : (b + 1) * span, g * WIDE : (g + 1) * WIDE] = r[at : at + span, :]


def call(kernel, scalars, arrays, outs, scratch, flops, unread=0):
    smem = pl.BlockSpec(memory_space=pltpu.SMEM)
    vmem = pl.BlockSpec(memory_space=pltpu.VMEM)
    single = not isinstance(outs, (list, tuple))
    moved = sum(a.size * a.dtype.itemsize for a in arrays)
    specs = [vmem] * (len(arrays) - unread) + [pl.BlockSpec(memory_space=pl.ANY)] * unread
    return pl.pallas_call(
        kernel,
        out_shape=outs,
        in_specs=[smem] * len(scalars) + specs,
        out_specs=vmem if single else [vmem] * len(outs),
        scratch_shapes=scratch,
        compiler_params=pltpu.CompilerParams(vmem_limit_bytes=VMEM_LIMIT),
        cost_estimate=pl.CostEstimate(flops=flops, bytes_accessed=moved, transcendentals=0),
    )(*scalars, *arrays)


def after(value, *others):
    return lax.optimization_barrier((value, *others))[0]


def per_device(tokens, projection, out_weight, half_width, neighbours):
    lon, lat, width = tokens.shape
    nlb = neighbours.shape[0]
    span = lat // nlb
    rows = lon * span
    groups = width // WIDE
    tiles = nlb * groups
    count = lax.axis_size("lon")
    devices = range(count)

    def permute(block, step):
        return lax.ppermute(block, "lon", [(i, step(i) % count) for i in devices])

    def sibling(i):
        return i ^ 1

    def across(i):
        return i ^ 2

    def onward(i):
        return i - 4 if i & 2 else i + 4

    def backward(i):
        return i + 4 if i & 2 else i - 4

    tile = (tiles, HEAD, WIDE)
    row = (tiles, 1, WIDE)
    carried_shapes = [
        jax.ShapeDtypeStruct(row, F32),
        jax.ShapeDtypeStruct(row, F32),
        jax.ShapeDtypeStruct(tile, F32),
    ]
    key_scratch = pltpu.VMEM((nlb, groups, rows, WIDE), BF16)
    val_scratch = pltpu.VMEM((2, nlb, groups, WIDE, 2 * rows), BF16)
    wide_scratch = [
        pltpu.VMEM((groups, 2 * rows, WIDE), BF16),
        pltpu.VMEM((groups, WIDE, 2 * rows), BF16),
    ]

    beside = permute(tokens, sibling)
    chunk = jax.ShapeDtypeStruct((nlb * rows // CHUNKS, width), BF16)
    *parts, band = call(
        prepare_kernel,
        (half_width,),
        (tokens,),
        [chunk] * CHUNKS + [jax.ShapeDtypeStruct((rows, width), BF16)],
        [],
        1_000_000,
    )
    f = [permute(part, across) for part in parts]
    wf = permute(band, onward)
    wb = permute(band, backward)
    g0 = permute(f[0], onward)
    qc, okeys, ovals, wvt = call(
        own_kernel,
        (),
        (after(tokens, f[0]), projection),
        [
            jax.ShapeDtypeStruct(tile, BF16),
            jax.ShapeDtypeStruct((nlb, groups, rows, WIDE), BF16),
            jax.ShapeDtypeStruct((nlb, groups, WIDE, 2 * rows), BF16),
            jax.ShapeDtypeStruct((width, width), BF16),
        ],
        [pltpu.VMEM((nlb * rows, width), BF16)],
        4_000_000_000,
    )
    g1 = permute(after(f[1], qc), onward)
    m, l, acc = call(
        near_kernel,
        (neighbours,),
        (after(beside, f[1]), projection, wvt, qc, okeys, ovals),
        carried_shapes,
        [
            pltpu.VMEM((nlb * rows, width), BF16),
            pltpu.VMEM((nlb, groups, 2 * rows, WIDE), BF16),
            pltpu.VMEM((nlb, groups, WIDE, 2 * rows), BF16),
        ],
        4_000_000_000,
    )
    g2 = permute(after(f[2], m), onward)
    m, l, acc = call(
        across_kernel,
        (neighbours, half_width),
        (*f, wf, wb, projection, wvt, qc, m, l, acc),
        carried_shapes,
        [pltpu.VMEM(((nlb + 2) * rows, width), BF16), key_scratch, val_scratch, *wide_scratch],
        6_000_000_000,
    )
    e = call(
        payload_kernel,
        (half_width,),
        (*f, g0, g1, g2, wf, wb, m),
        jax.ShapeDtypeStruct(((nlb + 2) * rows, width), BF16),
        [],
        1_000_000,
        unread=1,
    )
    e = permute(e, sibling)
    m, l, acc = call(
        onward_kernel,
        (neighbours, half_width),
        (g0, g1, g2, projection, wvt, qc, m, l, acc),
        carried_shapes,
        [pltpu.VMEM((nlb * rows, width), BF16), key_scratch, val_scratch],
        4_000_000_000,
    )
    return call(
        last_kernel,
        (neighbours, half_width),
        (e, projection, wvt, out_weight, qc, m, l, acc),
        jax.ShapeDtypeStruct(tokens.shape, BF16),
        [
            pltpu.VMEM(row, F32),
            pltpu.VMEM(row, F32),
            pltpu.VMEM(tile, F32),
            key_scratch,
            val_scratch,
            *wide_scratch,
            pltpu.VMEM((nlb * rows, width), BF16),
        ],
        6_000_000_000,
    )


def solution(mesh):
    return jax.shard_map(
        per_device,
        mesh=mesh,
        in_specs=(P(("groups", "lon"), None, None), P(), P(), P(), P()),
        out_specs=P(("groups", "lon"), None, None),
        check_vma=False,
    )
```

time: 200 us -> 58.2 us (0.29)
  local copies, waits for them, and re-layouts: 90.3 us -> 8.07 us
  matrix products: 67.6 us -> 0 us
  Pallas kernels: 0 us -> 31 us
  other arithmetic: 12.1 us -> 0 us
  starting transfers between devices: 20.2 us -> 14.2 us
  between operations: 4.07 us -> 0.15 us
    dot_general x20 -> x0, matrix products: 67.6 us -> none  [the longest x9 33 us: attend(): jnp.einsum(form_scores, queries, key_part, preferred_element_type=jnp.flo...]
    pallas_call x0 -> x7, Pallas kernels: none -> 31 us  [call(): pl.pallas_call(kernel, out_shape=outs, in_specs=[smem] * len(scalars) + s...]
    slice x16 -> x0, local copies, waits for them, and re-layouts: 24.7 us -> none  [the longest x11 22.4 us: attend(): key_rows[..., model_width:]]
    unnamed x108 -> x19, local copies, waits for them, and re-layouts: 31 us -> 8.07 us
    gather x6 -> x0, local copies, waits for them, and re-layouts: 20.3 us -> none  [the longest x5 19.6 us: band_rows(): key_band[neighbours].reshape(neighbours.shape[0], -1, key_band.shape[2])]
    reduce_sum x3 -> x0, other arithmetic: 9.09 us -> none  [attend(): running_sum = running_sum * factor + jnp.sum(exponent, axis=-1)]
    ppermute x8 -> x10, starting transfers between devices: 20.2 us -> 14.2 us  [permute(): return lax.ppermute(block, 'lon', [(i, step(i) % count) for i in devices])]
    reshape x6 -> x0, local copies, waits for them, and re-layouts: 5.31 us -> none  [the longest x1 2.7 us: per_device(): attended = (accumulated / running_sum.transpose(0, 2, 1)[..., None]).asty...]
  transfers between devices with their start and end apart: 8 -> 10, of which waited for: 2 -> 2; matrix products, arithmetic and copies ran while one was open for 57% -> 1% of each run, Pallas kernels for 0% -> 37%
where the time goes in v2:
time: 58.2 us; the launch traced here: 57.9 us
  Pallas kernels  31 us (53%)
  starting transfers between devices  14.2 us (24%)
  local copies, waits for them, and re-layouts  8.07 us (14%)
  waiting for transfers between devices  4.54 us (8%)
    pallas_call x7, Pallas kernels, call(): pl.pallas_call(kernel, out_shape=outs, in_specs=[smem] * len(scalars) + s...  31 us
    ppermute x10, starting transfers between devices, permute(): return lax.ppermute(block, 'lon', [(i, step(i) % count) for i in devices])  14.2 us
    unnamed x19, local copies, waits for them, and re-layouts  8.07 us
    ppermute x10, waiting for transfers between devices, permute(): return lax.ppermute(block, 'lon', [(i, step(i) % count) for i in devices])  4.54 us
  transfers between devices with their start and end apart: 10, of which 2 were waited for; matrix products, arithmetic and copies ran while one was open for 1% of the time, Pallas kernels for 37%

profile of v2, /device:TPU:0, one launch (start us, length us, event | category | flops | bytes accessed | tf_op | source)
XLA Modules:
  0.0 57.9 jit_solution(8514455484408295138)
XLA Ops:
  0.0 0.5 collective-permute-start.5
  0.5 1.1 %copy-done = bf16[2,192,1024]{2,1,0:T(8,128)(2,1)S(1)} copy-done((bf16[2,192,1024]{2,1,0:T(8,128)(2,1)S(1)}, bf16[2,192,1024]{2,1,0:T(8,128)(2,1)}, u32[]{:S(2)}) %copy-start) | copy-done | bytes 786456
  1.6 0.7 %copy-done.2 = s32[6]{0:T(128)S(1)} copy-done((s32[6]{0:T(128)S(1)}, s32[6]{0:T(128)}, u32[]{:S(2)}) %copy-start.2) | copy-done | bytes 48
  2.2 0.6 %shard_map.55 = (bf16[128,1024]{1,0:T(8,128)(2,1)S(1)}, bf16[128,1024]{1,0:T(8,128)(2,1)S(1)}, bf16[128,1024]{1,0:T(8,128)(2,1)S(1)}, bf16[64,1024]{1,0:T(8,128)(2,1)S(1)}) custom-call(s32[6]{0:T(128)S(1)} %copy-done.2, bf16[2,192,1024]{2,1,0:T(8,128)(2,1)S(1)} %copy-done), custom_call_target="tpu_custom_call" | custom-call | flops 1000000 | bytes 786432 | tf_op jit(solution)/shard_map/pallas_call | solution.py:274
  2.9 2.6 %collective-permute-start = (bf16[128,1024]{1,0:T(8,128)(2,1)S(1)}, bf16[128,1024]{1,0:T(8,128)(2,1)S(1)}, u32[]{:S(2)}, u32[]{:S(2)}) collective-permute-start(bf16[128,1024]{1,0:T(8,128)(2,1)S(1)} %get-tuple-element.26), channel_id=1, source_target_pairs={{0,2},{1,3},{2,0},{3,1},{4,6},{5,7},{6,4},{7,5},{8,10},{9,11},{10,... | collective-permute-start | bytes 786440 | tf_op jit(solution)/shard_map/ppermute | solution.py:300
  5.4 1.6 %collective-permute-start.7 = (bf16[64,1024]{1,0:T(8,128)(2,1)S(1)}, bf16[64,1024]{1,0:T(8,128)(2,1)S(1)}, u32[]{:S(2)}, u32[]{:S(2)}) collective-permute-start(bf16[64,1024]{1,0:T(8,128)(2,1)S(1)} %get-tuple-element.38), channel_id=1, source_target_pairs={{0,4},{1,5},{2,14},{3,15},{4,8},{5,9},{6,2},{7,3},{8,12},{9,13},{1... | collective-permute-start | bytes 393224 | tf_op jit(solution)/shard_map/ppermute | solution.py:300
  7.0 2.2 %collective-permute-start.8 = (bf16[64,1024]{1,0:T(8,128)(2,1)S(1)}, bf16[64,1024]{1,0:T(8,128)(2,1)S(1)}, u32[]{:S(2)}, u32[]{:S(2)}) collective-permute-start(bf16[64,1024]{1,0:T(8,128)(2,1)S(1)} %get-tuple-element.38), channel_id=1, source_target_pairs={{0,12},{1,13},{2,6},{3,7},{4,0},{5,1},{6,10},{7,11},{8,4},{9,5},{1... | collective-permute-start | bytes 393224 | tf_op jit(solution)/shard_map/ppermute | solution.py:300
  9.3 0.3 collective-permute-start.1
  9.5 0.8 %copy.9.nbr = s32[6,2]{1,0:T(8,128)S(1)} copy(s32[6,2]{0,1:T(2,128)} %param.9) | data formatting | bytes 96 | tf_op args[4]
  10.3 2.3 %collective-permute-done.f0 = bf16[128,1024]{1,0:T(8,128)(2,1)S(1)} collective-permute-done((bf16[128,1024]{1,0:T(8,128)(2,1)S(1)}, bf16[128,1024]{1,0:T(8,128)(2,1)S(1)}, u32[]{:S(2)}, u32[]{:S(2)}) %collective-permute-start) | collective-permute-done | bytes 262176 | tf_op jit(solution)/shard_map/ppermute | solution.py:300
  12.6 1.9 %collective-permute-start.2 = (bf16[128,1024]{1,0:T(8,128)(2,1)S(1)}, bf16[128,1024]{1,0:T(8,128)(2,1)S(1)}, u32[]{:S(2)}, u32[]{:S(2)}) collective-permute-start(bf16[128,1024]{1,0:T(8,128)(2,1)S(1)} %get-tuple-element.28), channel_id=1, source_target_pairs={{0,2},{1,3},{2,0},{3,1},{4,6},{5,7},{6,4},{7,5},{8,10},{9,11},{10,... | collective-permute-start | bytes 786440 | tf_op jit(solution)/shard_map/ppermute | solution.py:300
  14.5 1.1 %copy-done.1 = bf16[2,192,1024]{2,1,0:T(8,128)(2,1)S(1)} copy-done((bf16[2,192,1024]{2,1,0:T(8,128)(2,1)S(1)}, bf16[2,192,1024]{2,1,0:T(8,128)(2,1)}, u32[]{:S(2)}) %copy-start.1) | copy-done | bytes 786456
  15.7 2.8 %copy-done.4 = bf16[1024,3072]{1,0:T(8,128)(2,1)S(1)} copy-done((bf16[1024,3072]{1,0:T(8,128)(2,1)S(1)}, bf16[1024,3072]{1,0:T(8,128)(2,1)}, u32[]{:S(2)}) %copy-start.4) | copy-done | bytes 6291480
  18.5 3.1 %shard_map.56 = (bf16[24,64,256]{2,1,0:T(8,128)(2,1)S(1)}, bf16[6,4,64,256]{3,2,1,0:T(8,128)(2,1)S(1)}, bf16[6,4,256,128]{3,2,1,0:T(8,128)(2,1)S(1)}, bf16[1024,1024]{1,0:T(8,128)(2,1)S(1)}) custom-call(bf16[2,192,1024]{2,1,0:T(8,128)(2,1)S(1)} %copy-done.1, bf16[1024,3072]{1,0:T(8,128)(2,1)S(1)} %copy-done.4), custom_call_target="tpu_custom_call" | custom-call | flops 4000000000 | bytes 7077888 | tf_op jit(solution)/shard_map/pallas_call | solution.py:274
  21.5 1.6 %collective-permute-start.4 = (bf16[128,1024]{1,0:T(8,128)(2,1)S(1)}, bf16[128,1024]{1,0:T(8,128)(2,1)S(1)}, u32[]{:S(2)}, u32[]{:S(2)}) collective-permute-start(bf16[128,1024]{1,0:T(8,128)(2,1)S(1)} %collective-permute-done.1.f1), channel_id=1, source_target_pairs={{0,4},{1,5},{2,14},{3,15},{4,8},{5,9},{6,2},{7,3},{8,12},{9,13},{1... | collective-permute-start | bytes 786440 | tf_op jit(solution)/shard_map/ppermute | solution.py:300
  23.2 1.6 %collective-permute-start.3 = (bf16[128,1024]{1,0:T(8,128)(2,1)S(1)}, bf16[128,1024]{1,0:T(8,128)(2,1)S(1)}, u32[]{:S(2)}, u32[]{:S(2)}) collective-permute-start(bf16[128,1024]{1,0:T(8,128)(2,1)S(1)} %collective-permute-done.f0), channel_id=1, source_target_pairs={{0,4},{1,5},{2,14},{3,15},{4,8},{5,9},{6,2},{7,3},{8,12},{9,13},{1... | collective-permute-start | bytes 786440 | tf_op jit(solution)/shard_map/ppermute | solution.py:300
  24.8 5.4 %shard_map.57 = (f32[24,1,256]{2,1,0:T(1,128)S(1)}, f32[24,1,256]{2,1,0:T(1,128)S(1)}, f32[24,64,256]{2,1,0:T(8,128)S(1)}) custom-call(s32[6,2]{1,0:T(8,128)S(1)} %copy.9.nbr, bf16[2,192,1024]{2,1,0:T(8,128)(2,1)S(1)} %collective-permute-done.5.s, bf16[1024,3072]{1,0:T(8,128)(2,1)S(1)} %copy-done.5, bf16[1024,1024]{1,0:T(8,128)(2,1)S(1)} %get-tuple-element.33.wvt, ...), custom_call_target="tpu_custom_call" | custom-call | flops 4000000000 | bytes 12320768 | tf_op jit(solution)/shard_map/pallas_call | solution.py:274
  30.2 1.8 %collective-permute-start.6 = (bf16[128,1024]{1,0:T(8,128)(2,1)S(1)}, bf16[128,1024]{1,0:T(8,128)(2,1)S(1)}, u32[]{:S(2)}, u32[]{:S(2)}) collective-permute-start(bf16[128,1024]{1,0:T(8,128)(2,1)S(1)} %collective-permute-done.2.f2), channel_id=1, source_target_pairs={{0,4},{1,5},{2,14},{3,15},{4,8},{5,9},{6,2},{7,3},{8,12},{9,13},{1... | collective-permute-start | bytes 786440 | tf_op jit(solution)/shard_map/ppermute | solution.py:300
  32.0 1.6 %copy-done.8 = bf16[1024,1024]{1,0:T(8,128)(2,1)S(1)} copy-done((bf16[1024,1024]{1,0:T(8,128)(2,1)S(1)}, bf16[1024,1024]{1,0:T(8,128)(2,1)}, u32[]{:S(2)}) %copy-start.8) | copy-done | bytes 2097176
  33.6 6.1 %shard_map.58 = (f32[24,1,256]{2,1,0:T(1,128)S(1)}, f32[24,1,256]{2,1,0:T(1,128)S(1)}, f32[24,64,256]{2,1,0:T(8,128)S(1)}) custom-call(s32[6,2]{1,0:T(8,128)S(1)} %copy.9.nbr, s32[6]{0:T(128)S(1)} %copy-done.3, bf16[128,1024]{1,0:T(8,128)(2,1)S(1)} %collective-permute-done.f0, bf16[128,1024]{1,0:T(8,128)(2,1)S(1)} %collective-permute-done.1.f1, ...), custom_call_target="tpu_custom_call" | custom-call | flops 6000000000 | bytes 11845632 | tf_op jit(solution)/shard_map/pallas_call | solution.py:274
  39.7 2.2 %collective-permute-done.6.g2 = bf16[128,1024]{1,0:T(8,128)(2,1)S(1)} collective-permute-done((bf16[128,1024]{1,0:T(8,128)(2,1)S(1)}, bf16[128,1024]{1,0:T(8,128)(2,1)S(1)}, u32[]{:S(2)}, u32[]{:S(2)}) %collective-permute-start.6) | collective-permute-done | bytes 262176 | tf_op jit(solution)/shard_map/ppermute | solution.py:300
  42.0 0.9 %shard_map.59 = bf16[512,1024]{1,0:T(8,128)(2,1)S(1)} custom-call(s32[6]{0:T(128)S(1)} %copy-done.3, bf16[128,1024]{1,0:T(8,128)(2,1)S(1)} %collective-permute-done.f0, bf16[128,1024]{1,0:T(8,128)(2,1)S(1)} %collective-permute-done.1.f1, bf16[128,1024]{1,0:T(8,128)(2,1)S(1)} %collective-permute-done.2.f2, bf16[128,1024]{1,0:T(8,128)(2,1)S(1)} %collective-permute-done.3.g0, ...), custom_call_target="tpu_custom_call" | custom-call | flops 1000000 | bytes 1859584 | tf_op jit(solution)/shard_map/pallas_call | solution.py:274
  42.9 6.4 %shard_map.60 = (f32[24,1,256]{2,1,0:T(1,128)S(1)}, f32[24,1,256]{2,1,0:T(1,128)S(1)}, f32[24,64,256]{2,1,0:T(8,128)S(1)}) custom-call(s32[6,2]{1,0:T(8,128)S(1)} %copy.9.nbr, s32[6]{0:T(128)S(1)} %copy-done.3, bf16[128,1024]{1,0:T(8,128)(2,1)S(1)} %collective-permute-done.3.g0, bf16[128,1024]{1,0:T(8,128)(2,1)S(1)} %collective-permute-done.4.g1, ...), custom_call_target="tpu_custom_call" | custom-call | flops 4000000000 | bytes 11583488 | tf_op jit(solution)/shard_map/pallas_call | solution.py:274
  49.4 8.6 %shard_map.61 = bf16[2,192,1024]{2,1,0:T(8,128)(2,1)} custom-call(s32[6,2]{1,0:T(8,128)S(1)} %copy.9.nbr, s32[6]{0:T(128)S(1)} %copy-done.3, bf16[512,1024]{1,0:T(8,128)(2,1)S(1)} %collective-permute-done.9.e, bf16[1024,3072]{1,0:T(8,128)(2,1)S(1)} %copy-done.5, bf16[1024,1024]{1,0:T(8,128)(2,1)S(1)} %copy-done.8, bf16[1024,1024]{1,0:T(8,128)(2,1)S(1)} %copy-done.6, ...), custom_call_target="tpu_custom_call" | custom-call | flops 6000000000 | bytes 13942784 | tf_op jit(solution)/shard_map/pallas_call | solution.py:274
  (22 shorter events, 0.1 us)
Async XLA Ops:
  0.0 23.2 %collective-permute-start.5 = (bf16[2,192,1024]{2,1,0:T(8,128)(2,1)}, bf16[2,192,1024]{2,1,0:T(8,128)(2,1)S(1)}, u32[]{:S(2)}, u32[]{:S(2)}) collective-permute-start(bf16[2,192,1024]{2,1,0:T(8,128)(2,1)} %x.2), channel_id=1, source_target_pairs={{0,1},{1,0},{2,3},{3,2},{4,5},{5,4},{6,7},{7,6},{8,9},{9,8},{10,11... | collective-permute-start | bytes 2359304 | tf_op jit(solution)/shard_map/ppermute | solution.py:300
  0.5 1.1 %copy-start = (bf16[2,192,1024]{2,1,0:T(8,128)(2,1)S(1)}, bf16[2,192,1024]{2,1,0:T(8,128)(2,1)}, u32[]{:S(2)}) copy-start(bf16[2,192,1024]{2,1,0:T(8,128)(2,1)} %x.2) | copy-start | bytes 2359300
  1.6 0.7 %copy-start.2 = (s32[6]{0:T(128)S(1)}, s32[6]{0:T(128)}, u32[]{:S(2)}) copy-start(s32[6]{0:T(128)} %hw.9) | copy-start | bytes 76
  2.9 9.7 %collective-permute-start = (bf16[128,1024]{1,0:T(8,128)(2,1)S(1)}, bf16[128,1024]{1,0:T(8,128)(2,1)S(1)}, u32[]{:S(2)}, u32[]{:S(2)}) collective-permute-start(bf16[128,1024]{1,0:T(8,128)(2,1)S(1)} %get-tuple-element.26), channel_id=1, source_target_pairs={{0,2},{1,3},{2,0},{3,1},{4,6},{5,7},{6,4},{7,5},{8,10},{9,11},{10,... | collective-permute-start | bytes 786440 | tf_op jit(solution)/shard_map/ppermute | solution.py:300
  5.4 26.5 %collective-permute-start.7 = (bf16[64,1024]{1,0:T(8,128)(2,1)S(1)}, bf16[64,1024]{1,0:T(8,128)(2,1)S(1)}, u32[]{:S(2)}, u32[]{:S(2)}) collective-permute-start(bf16[64,1024]{1,0:T(8,128)(2,1)S(1)} %get-tuple-element.38), channel_id=1, source_target_pairs={{0,4},{1,5},{2,14},{3,15},{4,8},{5,9},{6,2},{7,3},{8,12},{9,13},{1... | collective-permute-start | bytes 393224 | tf_op jit(solution)/shard_map/ppermute | solution.py:300
  7.0 25.0 %collective-permute-start.8 = (bf16[64,1024]{1,0:T(8,128)(2,1)S(1)}, bf16[64,1024]{1,0:T(8,128)(2,1)S(1)}, u32[]{:S(2)}, u32[]{:S(2)}) collective-permute-start(bf16[64,1024]{1,0:T(8,128)(2,1)S(1)} %get-tuple-element.38), channel_id=1, source_target_pairs={{0,12},{1,13},{2,6},{3,7},{4,0},{5,1},{6,10},{7,11},{8,4},{9,5},{1... | collective-permute-start | bytes 393224 | tf_op jit(solution)/shard_map/ppermute | solution.py:300
  9.3 12.3 %collective-permute-start.1 = (bf16[128,1024]{1,0:T(8,128)(2,1)S(1)}, bf16[128,1024]{1,0:T(8,128)(2,1)S(1)}, u32[]{:S(2)}, u32[]{:S(2)}) collective-permute-start(bf16[128,1024]{1,0:T(8,128)(2,1)S(1)} %get-tuple-element.27), channel_id=1, source_target_pairs={{0,2},{1,3},{2,0},{3,1},{4,6},{5,7},{6,4},{7,5},{8,10},{9,11},{10,... | collective-permute-start | bytes 786440 | tf_op jit(solution)/shard_map/ppermute | solution.py:300
  12.6 17.6 %collective-permute-start.2 = (bf16[128,1024]{1,0:T(8,128)(2,1)S(1)}, bf16[128,1024]{1,0:T(8,128)(2,1)S(1)}, u32[]{:S(2)}, u32[]{:S(2)}) collective-permute-start(bf16[128,1024]{1,0:T(8,128)(2,1)S(1)} %get-tuple-element.28), channel_id=1, source_target_pairs={{0,2},{1,3},{2,0},{3,1},{4,6},{5,7},{6,4},{7,5},{8,10},{9,11},{10,... | collective-permute-start | bytes 786440 | tf_op jit(solution)/shard_map/ppermute | solution.py:300
  14.5 1.1 %copy-start.1 = (bf16[2,192,1024]{2,1,0:T(8,128)(2,1)S(1)}, bf16[2,192,1024]{2,1,0:T(8,128)(2,1)}, u32[]{:S(2)}) copy-start(bf16[2,192,1024]{2,1,0:T(8,128)(2,1)} %x.2) | copy-start | bytes 2359300
  15.7 2.8 %copy-start.4 = (bf16[1024,3072]{1,0:T(8,128)(2,1)S(1)}, bf16[1024,3072]{1,0:T(8,128)(2,1)}, u32[]{:S(2)}) copy-start(bf16[1024,3072]{1,0:T(8,128)(2,1)} %w.9) | copy-start | bytes 18874372
  18.5 6.3 %copy-start.5 = (bf16[1024,3072]{1,0:T(8,128)(2,1)S(1)}, bf16[1024,3072]{1,0:T(8,128)(2,1)}, u32[]{:S(2)}) copy-start(bf16[1024,3072]{1,0:T(8,128)(2,1)} %w.9) | copy-start | bytes 18874372
  21.5 8.6 %copy-start.7 = (bf16[1024,1024]{1,0:T(8,128)(2,1)}, bf16[1024,1024]{1,0:T(8,128)(2,1)S(1)}, u32[]{:S(2)}) copy-start(bf16[1024,1024]{1,0:T(8,128)(2,1)S(1)} %get-tuple-element.33.wvt) | copy-start | bytes 6291460
  21.5 18.2 %collective-permute-start.4 = (bf16[128,1024]{1,0:T(8,128)(2,1)S(1)}, bf16[128,1024]{1,0:T(8,128)(2,1)S(1)}, u32[]{:S(2)}, u32[]{:S(2)}) collective-permute-start(bf16[128,1024]{1,0:T(8,128)(2,1)S(1)} %collective-permute-done.1.f1), channel_id=1, source_target_pairs={{0,4},{1,5},{2,14},{3,15},{4,8},{5,9},{6,2},{7,3},{8,12},{9,13},{1... | collective-permute-start | bytes 786440 | tf_op jit(solution)/shard_map/ppermute | solution.py:300
  23.2 16.5 %collective-permute-start.3 = (bf16[128,1024]{1,0:T(8,128)(2,1)S(1)}, bf16[128,1024]{1,0:T(8,128)(2,1)S(1)}, u32[]{:S(2)}, u32[]{:S(2)}) collective-permute-start(bf16[128,1024]{1,0:T(8,128)(2,1)S(1)} %collective-permute-done.f0), channel_id=1, source_target_pairs={{0,4},{1,5},{2,14},{3,15},{4,8},{5,9},{6,2},{7,3},{8,12},{9,13},{1... | collective-permute-start | bytes 786440 | tf_op jit(solution)/shard_map/ppermute | solution.py:300
  24.8 7.2 %copy-start.3 = (s32[6]{0:T(128)S(1)}, s32[6]{0:T(128)}, u32[]{:S(2)}) copy-start(s32[6]{0:T(128)} %hw.9) | copy-start | bytes 76
  30.2 11.8 %collective-permute-start.6 = (bf16[128,1024]{1,0:T(8,128)(2,1)S(1)}, bf16[128,1024]{1,0:T(8,128)(2,1)S(1)}, u32[]{:S(2)}, u32[]{:S(2)}) collective-permute-start(bf16[128,1024]{1,0:T(8,128)(2,1)S(1)} %collective-permute-done.2.f2), channel_id=1, source_target_pairs={{0,4},{1,5},{2,14},{3,15},{4,8},{5,9},{6,2},{7,3},{8,12},{9,13},{1... | collective-permute-start | bytes 786440 | tf_op jit(solution)/shard_map/ppermute | solution.py:300
  32.0 1.6 %copy-start.8 = (bf16[1024,1024]{1,0:T(8,128)(2,1)S(1)}, bf16[1024,1024]{1,0:T(8,128)(2,1)}, u32[]{:S(2)}) copy-start(bf16[1024,1024]{1,0:T(8,128)(2,1)} %copy-done.7) | copy-start | bytes 6291460
  42.8 6.5 %collective-permute-start.9 = (bf16[512,1024]{1,0:T(8,128)(2,1)S(1)}, bf16[512,1024]{1,0:T(8,128)(2,1)S(1)}, u32[]{:S(2)}, u32[]{:S(2)}) collective-permute-start(bf16[512,1024]{1,0:T(8,128)(2,1)S(1)} %shard_map.59), channel_id=1, source_target_pairs={{0,1},{1,0},{2,3},{3,2},{4,5},{5,4},{6,7},{7,6},{8,9},{9,8},{10,11... | collective-permute-start | bytes 3145736 | tf_op jit(solution)/shard_map/ppermute | solution.py:300
  42.9 6.4 %copy-start.6 = (bf16[1024,1024]{1,0:T(8,128)(2,1)S(1)}, bf16[1024,1024]{1,0:T(8,128)(2,1)}, u32[]{:S(2)}) copy-start(bf16[1024,1024]{1,0:T(8,128)(2,1)} %wout.1) | copy-start | bytes 6291460

commit v3 on v2

v3 whole, which is shorter than its diff:
```python
import math

import jax
import jax.numpy as jnp
from jax import lax
from jax.experimental import pallas as pl
from jax.experimental.pallas import tpu as pltpu
from jax.sharding import PartitionSpec as P

HEADS = 16
HEAD = 64
PACK = 4
WIDE = PACK * HEAD
CHUNKS = 3
NEVER = -1e37
BF16 = jnp.bfloat16
F32 = jnp.float32
SCALE = math.log2(math.e) / math.sqrt(HEAD)
VMEM_LIMIT = 28 * 1024 * 1024
COST = 4000000000
EARLY_COST = 4000000000
NEAR_COST = 4000000000
ACROSS_COST = 4000000000


def lane_head(shape):
    return lax.broadcasted_iota(jnp.int32, shape, len(shape) - 1) // HEAD


def spread(packed):
    lane = lane_head((1, WIDE))
    return jnp.concatenate(
        [packed * (lane == h).astype(F32).astype(BF16) for h in range(PACK)], axis=0
    )


def gather_diagonal(full):
    lane = lane_head((HEAD, WIDE))
    total = full[:HEAD]
    for h in range(1, PACK):
        total = jnp.where(lane == h, full[h * HEAD : (h + 1) * HEAD], total)
    return total


def dot(a, b):
    return jnp.dot(a, b, preferred_element_type=F32)


def dot_nt(a, b):
    return lax.dot_general(a, b, (((1,), (1,)), ((), ())), preferred_element_type=F32)


def update(scores, values_t, carried):
    row_max, total, summed = carried
    new_max = jnp.maximum(row_max, jnp.max(scores, axis=0, keepdims=True))
    exponent = jnp.exp2((scores - new_max) * SCALE)
    factor = jnp.exp2((row_max - new_max) * SCALE)
    total = total * factor + jnp.sum(exponent, axis=0, keepdims=True)
    summed = summed * factor + gather_diagonal(dot(values_t, exponent.astype(BF16)))
    return new_max, total, summed


def halves(pair):
    lane = lax.broadcasted_iota(jnp.int32, pair.shape, 1)
    turned = pltpu.roll(pair, HEAD, 1)
    low = lane < HEAD
    zero = jnp.zeros_like(pair)
    first = (jnp.where(low, pair, zero), jnp.where(low, zero, turned))
    second = (jnp.where(low, turned, zero), jnp.where(low, zero, pair))
    return first, second


def widest_of(hw):
    best, where = hw[0], 0
    for c in range(1, hw.shape[0]):
        larger = hw[c] > best
        best = jnp.where(larger, hw[c], best)
        where = jnp.where(larger, c, where)
    return where


def project_values(wvt, tokens, g, blocks, rows):
    v = dot_nt(wvt[g * WIDE : (g + 1) * WIDE, :], tokens)
    parts = []
    for c in range(0, blocks, 2):
        for left, right in halves(v[:, c * rows : (c + 2) * rows]):
            parts.append((left.astype(BF16), right.astype(BF16)))
    return parts, v[:, blocks * rows :].astype(BF16)


def prepare_kernel(x, f0, f1, f2, sems):
    lon, lat, _ = x.shape
    span = lat * lon // sems.shape[0]
    out = (f0, f1, f2)
    count = f0.shape[0] // span // lon
    copies = []
    for j in range(CHUNKS):
        for c in range(count):
            for o in range(lon):
                at = (c * lon + o) * span
                copies.append(
                    pltpu.make_async_copy(
                        x.at[o, pl.ds((j * count + c) * span, span), :],
                        out[j].at[pl.ds(at, span), :],
                        sems.at[len(copies)],
                    )
                )
                copies[-1].start()
    for copy in copies:
        copy.wait()


def band_kernel(hw, x0, x1, x2, band):
    wide = widest_of(hw)
    rows = band.shape[0]
    per = x0.shape[0] // rows
    for c in range(CHUNKS * per):

        @pl.when(wide == c)
        def _(c=c):
            at = (c % per) * rows
            band[...] = (x0, x1, x2)[c // per][at : at + rows, :]


def own_kernel(x0, x1, x2, s, w, qc, keys, vals, wk, wvt, own, both, wq, wv, sems):
    lon, _, width = s.shape
    nlb, groups, rows, _ = keys.shape
    rows //= 2
    span = rows // lon
    fetch = []
    for which, place in ((1, wk), (0, wq), (2, wv)):
        for g in range(groups):
            fetch.append(
                pltpu.make_async_copy(
                    w.at[:, pl.ds(which * width + g * WIDE, WIDE)],
                    place.at[:, pl.ds(g * WIDE, WIDE)],
                    sems.at[len(fetch)],
                )
            )
            fetch[-1].start()
    at = 0
    for part in (x0, x1, x2):
        for c in range(part.shape[0] // rows):
            block = part[c * rows : (c + 1) * rows, :]
            own[at : at + rows, :] = block
            both[2 * at : 2 * at + rows, :] = block
            at += rows
    for c in range(nlb):
        for o in range(lon):
            at = (2 * c + 1) * rows + o * span
            both[at : at + span, :] = s[o, c * span : (c + 1) * span, :]
    for g in range(groups):
        fetch[g].wait()
        k = dot(both[...], wk[:, g * WIDE : (g + 1) * WIDE]).astype(BF16)
        for c in range(nlb):
            keys[c, g] = k[2 * c * rows : 2 * (c + 1) * rows, :]
    for g in range(groups):
        fetch[groups + g].wait()
        q = dot(own[...], wq[:, g * WIDE : (g + 1) * WIDE]).astype(BF16).astype(F32)
        for b in range(nlb):
            qt = q[b * rows : (b + 1) * rows, :].T
            qc[b * groups + g] = jnp.concatenate(
                [qt[h * HEAD : (h + 1) * HEAD, :] for h in range(PACK)], axis=1
            ).astype(BF16)
    for g in range(groups):
        fetch[2 * groups + g].wait()
        wvt[g * WIDE : (g + 1) * WIDE, :] = wv[:, g * WIDE : (g + 1) * WIDE].T
        v = dot_nt(wvt[g * WIDE : (g + 1) * WIDE, :], both[...]).astype(BF16)
        for c in range(nlb):
            vals[c, g] = v[:, 2 * c * rows : 2 * (c + 1) * rows]


def near_kernel(nbr, qc, keys, vals, m, l, acc):
    nlb, groups, _, _ = keys.shape
    for b in range(nlb):
        c0, c1 = nbr[b, 0], nbr[b, 1]
        for g in range(groups):
            t = b * groups + g
            k = jnp.concatenate([keys[c0, g], keys[c1, g]], axis=0)
            v = jnp.concatenate([vals[c0, g], vals[c1, g]], axis=1)
            scores = dot(k, spread(qc[t]))
            row_max = jnp.max(scores, axis=0, keepdims=True)
            exponent = jnp.exp2((scores - row_max) * SCALE)
            m[t] = row_max
            l[t] = jnp.sum(exponent, axis=0, keepdims=True)
            acc[t] = gather_diagonal(dot(v, exponent.astype(BF16)))


def project_far(tokens, w, wvt, keys, vals, wkeys, wvals):
    nlb, groups, rows, _ = keys.shape
    for g in range(groups):
        k = dot(tokens[...], w[:, g * WIDE : (g + 1) * WIDE]).astype(BF16)
        parts, rest = project_values(wvt, tokens[...], g, nlb, rows)
        for c in range(nlb):
            keys[c, g] = k[c * rows : (c + 1) * rows, :]
            vals[0, c, g] = parts[c][0]
            vals[1, c, g] = parts[c][1]
        if wkeys is not None:
            wkeys[g] = k[nlb * rows :, :]
            wvals[g] = rest


def attend_far(nbr, seen, wide, qc, pick_keys, pick_vals, wkeys, wvals, before, finish):
    nlb = nbr.shape[0]
    groups = qc.shape[0] // nlb
    for b in range(nlb):
        c0, c1 = nbr[b, 0], nbr[b, 1]
        for g in range(groups):
            t = b * groups + g
            q = spread(qc[t])
            ks = [pick_keys(c0, g), pick_keys(c1, g)]
            rows = ks[0].shape[0]
            v = pick_vals(0, c0, g) + pick_vals(1, c1, g)
            if wkeys is not None:
                ks.append(wkeys[g])
                v = jnp.concatenate([v, wvals[g]], axis=1)
            scores = dot(jnp.concatenate(ks, axis=0), q)
            pieces = [scores[:rows], scores[rows : 2 * rows]]
            if seen is not None:
                pieces[0] = jnp.where(seen[c0] >= 2, pieces[0], NEVER)
                pieces[1] = jnp.where(seen[c1] >= 2, pieces[1], NEVER)
            if wkeys is not None:
                member = (c0 == wide) | (c1 == wide)
                pieces.append(jnp.where(member, scores[2 * rows :], NEVER))
            scores = jnp.concatenate(pieces, axis=0)
            finish(b, g, *update(scores, v, tuple(r[t] for r in before)))


def from_one(keys, vals):
    return (lambda c, g: keys[c, g]), (lambda side, c, g: vals[side, c, g])


def from_two(keys, vals, more_keys, more_vals):
    first = keys.shape[0]

    def pick_keys(c, g):
        here, there = keys[jnp.minimum(c, first - 1), g], more_keys[jnp.maximum(c - first, 0), g]
        return jnp.where(c < first, here, there)

    def pick_vals(side, c, g):
        here = vals[side, jnp.minimum(c, first - 1), g]
        there = more_vals[side, jnp.maximum(c - first, 0), g]
        return jnp.where(c < first, here, there)

    return pick_keys, pick_vals


def keep(m, l, acc, groups):
    def store(b, g, row_max, total, summed):
        t = b * groups + g
        m[t], l[t], acc[t] = row_max, total, summed

    return store


def across_kernel(nbr, hw, f0, f1, f2, wf, wb, w, wvt, qc, m_in, l_in, acc_in,
                  m, l, acc, tokens, keys, vals, wkeys, wvals):
    at = 0
    for part in (f0, f1, f2, wf, wb):
        tokens[at : at + part.shape[0], :] = part[...]
        at += part.shape[0]
    project_far(tokens, w, wvt, keys, vals, wkeys, wvals)
    attend_far(nbr, hw, widest_of(hw), qc, *from_one(keys, vals), wkeys, wvals, (m_in, l_in, acc_in), keep(m, l, acc, keys.shape[1]))


def early_kernel(g0, g1, w, wvt, keys, vals, tokens):
    tokens[: g0.shape[0], :] = g0[...]
    tokens[g0.shape[0] :, :] = g1[...]
    project_far(tokens, w, wvt, keys, vals, None, None)


def onward_kernel(nbr, hw, g2, w, wvt, qc, early_keys, early_vals, m_in, l_in, acc_in, m, l, acc, keys, vals):
    project_far(g2, w, wvt, keys, vals, None, None)
    picks = from_two(early_keys, early_vals, keys, vals)
    store = keep(m, l, acc, keys.shape[1])
    attend_far(nbr, hw, None, qc, *picks, None, None, (m_in, l_in, acc_in), store)


def payload_kernel(hw, f0, f1, f2, g0, g1, g2, wf, wb, out):
    here = lax.axis_index("lon")
    wide = widest_of(hw)
    size = f0.shape[0]
    rows = wf.shape[0]
    per = size // rows
    base = CHUNKS * size

    def fill(sent, other, wide_sent):
        for j in range(CHUNKS):
            out[j * size : (j + 1) * size, :] = sent[j][...]
        out[base : base + rows, :] = wide_sent[...]
        for c in range(CHUNKS * per):

            @pl.when(wide == c)
            def _(c=c):
                at = (c % per) * rows
                out[base + rows :, :] = other[c // per][at : at + rows, :]

    kind = (here ^ (here >> 1)) & 1

    @pl.when(kind == 0)
    def _():
        fill((f0, f1, f2), (g0, g1, g2), wb)

    @pl.when(kind != 0)
    def _():
        fill((g0, g1, g2), (f0, f1, f2), wf)


def last_kernel(nbr, hw, e, w, wvt, wout, qc, m_in, l_in, acc_in, out, keys, vals, wkeys, wvals, attended):
    nlb, groups, rows, _ = keys.shape
    lon = out.shape[0]
    span = rows // lon

    def store(b, g, _, total, summed):
        done = (summed * (1.0 / total)).T
        attended[b * rows : (b + 1) * rows, g * WIDE : (g + 1) * WIDE] = jnp.concatenate(
            [done[h * HEAD : (h + 1) * HEAD, :] for h in range(PACK)], axis=1
        ).astype(BF16)

    project_far(e, w, wvt, keys, vals, wkeys, wvals)
    attend_far(nbr, None, widest_of(hw), qc, *from_one(keys, vals), wkeys, wvals, (m_in, l_in, acc_in), store)
    for g in range(groups):
        r = dot(attended[...], wout[:, g * WIDE : (g + 1) * WIDE]).astype(BF16)
        for b in range(nlb):
            for o in range(lon):
                at = b * rows + o * span
                out[o, b * span : (b + 1) * span, g * WIDE : (g + 1) * WIDE] = r[at : at + span, :]


def call(kernel, scalars, arrays, outs, scratch, unread=0, cost=COST):
    smem = pl.BlockSpec(memory_space=pltpu.SMEM)
    vmem = pl.BlockSpec(memory_space=pltpu.VMEM)
    single = not isinstance(outs, (list, tuple))
    specs = [vmem] * (len(arrays) - unread) + [pl.BlockSpec(memory_space=pltpu.HBM)] * unread
    read = len(arrays) - unread
    arrays = [
        a if i < read else pltpu.with_memory_space_constraint(a, pltpu.HBM)
        for i, a in enumerate(arrays)
    ]
    return pl.pallas_call(
        kernel,
        out_shape=outs,
        in_specs=[smem] * len(scalars) + specs,
        out_specs=vmem if single else [vmem] * len(outs),
        scratch_shapes=scratch,
        compiler_params=pltpu.CompilerParams(vmem_limit_bytes=VMEM_LIMIT),
        cost_estimate=pl.CostEstimate(flops=cost, bytes_accessed=1000, transcendentals=0),
    )(*scalars, *arrays)


def after(value, *others):
    return lax.optimization_barrier((value, *others))[0]


def per_device(tokens, projection, out_weight, half_width, neighbours):
    lon, lat, width = tokens.shape
    nlb = neighbours.shape[0]
    span = lat // nlb
    rows = lon * span
    groups = width // WIDE
    tiles = nlb * groups
    count = lax.axis_size("lon")
    devices = range(count)

    def permute(block, step):
        return lax.ppermute(block, "lon", [(i, step(i) % count) for i in devices])

    def sibling(i):
        return i ^ 1

    def across(i):
        return i ^ 2

    def onward(i):
        return i - 4 if i & 2 else i + 4

    def backward(i):
        return i + 4 if i & 2 else i - 4

    tile = (tiles, HEAD, WIDE)
    row = (tiles, 1, WIDE)
    carried_shapes = [
        jax.ShapeDtypeStruct(row, F32),
        jax.ShapeDtypeStruct(row, F32),
        jax.ShapeDtypeStruct(tile, F32),
    ]
    key_scratch = pltpu.VMEM((nlb, groups, rows, WIDE), BF16)
    val_scratch = pltpu.VMEM((2, nlb, groups, WIDE, 2 * rows), BF16)
    wide_scratch = [
        pltpu.VMEM((groups, 2 * rows, WIDE), BF16),
        pltpu.VMEM((groups, WIDE, 2 * rows), BF16),
    ]

    beside = permute(tokens, sibling)
    chunk = jax.ShapeDtypeStruct((nlb * rows // CHUNKS, width), BF16)
    parts = call(
        prepare_kernel, (), (tokens,), [chunk] * CHUNKS, [pltpu.SemaphoreType.DMA((nlb * lon,))], unread=1
    )
    f = [permute(part, across) for part in parts]
    band = call(
        band_kernel, (half_width,), tuple(parts), jax.ShapeDtypeStruct((rows, width), BF16), []
    )
    wf = permute(band, onward)
    wb = permute(band, backward)
    g0 = permute(f[0], onward)
    held, *_ = lax.optimization_barrier((parts[0], f[0]))
    qc, keys, vals, wk, wvt = call(
        own_kernel,
        (),
        (held, *parts[1:], beside, projection),
        [
            jax.ShapeDtypeStruct(tile, BF16),
            jax.ShapeDtypeStruct((nlb, groups, 2 * rows, WIDE), BF16),
            jax.ShapeDtypeStruct((nlb, groups, WIDE, 2 * rows), BF16),
            jax.ShapeDtypeStruct((width, width), BF16),
            jax.ShapeDtypeStruct((width, width), BF16),
        ],
        [
            pltpu.VMEM((nlb * rows, width), BF16),
            pltpu.VMEM((2 * nlb * rows, width), BF16),
            pltpu.VMEM((width, width), BF16),
            pltpu.VMEM((width, width), BF16),
            pltpu.SemaphoreType.DMA((3 * groups,)),
        ],
        unread=1,
    )
    g1 = permute(after(f[1], qc), onward)
    m, l, acc = call(
        near_kernel,
        (neighbours,),
        (after(qc, f[1]), keys, vals),
        carried_shapes,
        [],
        cost=NEAR_COST,
    )
    g2 = permute(after(f[2], m), onward)
    m, l, acc = call(
        across_kernel,
        (neighbours, half_width),
        (*f, wf, wb, wk, wvt, qc, m, l, acc),
        carried_shapes,
        [pltpu.VMEM(((nlb + 2) * rows, width), BF16), key_scratch, val_scratch, *wide_scratch],
        cost=ACROSS_COST,
    )
    early = nlb // CHUNKS * (CHUNKS - 1)
    early_keys, early_vals = call(
        early_kernel,
        (),
        (after(g0, m), g1, wk, wvt),
        [
            jax.ShapeDtypeStruct((early, groups, rows, WIDE), BF16),
            jax.ShapeDtypeStruct((2, early, groups, WIDE, 2 * rows), BF16),
        ],
        [pltpu.VMEM((early * rows, width), BF16)],
        cost=EARLY_COST,
    )
    e = call(
        payload_kernel,
        (half_width,),
        (*f, g0, g1, g2, after(wf, early_keys), wb),
        jax.ShapeDtypeStruct(((nlb + 2) * rows, width), BF16),
        [],
    )
    e = permute(e, sibling)
    m, l, acc = call(
        onward_kernel,
        (neighbours, half_width),
        (g2, wk, wvt, qc, early_keys, early_vals, m, l, acc),
        carried_shapes,
        [
            pltpu.VMEM((nlb - early, groups, rows, WIDE), BF16),
            pltpu.VMEM((2, nlb - early, groups, WIDE, 2 * rows), BF16),
        ],
    )
    return call(
        last_kernel,
        (neighbours, half_width),
        (e, wk, wvt, out_weight, qc, m, l, acc),
        jax.ShapeDtypeStruct(tokens.shape, BF16),
        [
            key_scratch,
            val_scratch,
            *wide_scratch,
            pltpu.VMEM((nlb * rows, width), BF16),
        ],
    )


def solution(mesh):
    return jax.shard_map(
        per_device,
        mesh=mesh,
        in_specs=(P(("groups", "lon"), None, None), P(), P(), P(), P()),
        out_specs=P(("groups", "lon"), None, None),
        check_vma=False,
    )
```

time: 58.2 us -> 56.9 us (0.978)
  local copies, waits for them, and re-layouts: 8.07 us -> 0.11 us
  Pallas kernels: 31 us -> 38.6 us
  starting transfers between devices: 14.2 us -> 12.6 us
  waiting for transfers between devices: 4.54 us -> 5.21 us
    unnamed x19 -> x7, local copies, waits for them, and re-layouts: 8.07 us -> 0.11 us
    pallas_call x7 -> x9, Pallas kernels: 31 us -> 38.6 us  [call(): pl.pallas_call(kernel, out_shape=outs, in_specs=[smem] * len(scalars) + s...]
    ppermute x10, starting transfers between devices: 14.2 us -> 12.6 us  [permute(): return lax.ppermute(block, 'lon', [(i, step(i) % count) for i in devices])]
    ppermute x10, waiting for transfers between devices: 4.54 us -> 5.21 us  [permute(): return lax.ppermute(block, 'lon', [(i, step(i) % count) for i in devices])]
  transfers between devices with their start and end apart: 10 -> 10, of which waited for: 2 -> 3; matrix products, arithmetic and copies ran while one was open for 1% -> 0% of each run, Pallas kernels for 37% -> 52%
where the time goes in v3:
time: 56.9 us; the launch traced here: 56.7 us
  Pallas kernels  38.6 us (68%)
  starting transfers between devices  12.6 us (22%)
  waiting for transfers between devices  5.21 us (9%)
    pallas_call x9, Pallas kernels, call(): pl.pallas_call(kernel, out_shape=outs, in_specs=[smem] * len(scalars) + s...  38.6 us
    ppermute x10, starting transfers between devices, permute(): return lax.ppermute(block, 'lon', [(i, step(i) % count) for i in devices])  12.6 us
    ppermute x10, waiting for transfers between devices, permute(): return lax.ppermute(block, 'lon', [(i, step(i) % count) for i in devices])  5.21 us
  transfers between devices with their start and end apart: 10, of which 3 were waited for; matrix products, arithmetic and copies ran while one was open for 0% of the time, Pallas kernels for 52%

profile of v3, /device:TPU:0, one launch (start us, length us, event | category | flops | bytes accessed | tf_op | source)
XLA Modules:
  0.0 56.7 jit_solution(10343299270414840112)
XLA Ops:
  0.0 0.5 collective-permute-start.4
  0.5 1.3 %shard_map.55 = (bf16[128,1024]{1,0:T(8,128)(2,1)S(1)}, bf16[128,1024]{1,0:T(8,128)(2,1)S(1)}, bf16[128,1024]{1,0:T(8,128)(2,1)S(1)}) custom-call(bf16[2,192,1024]{2,1,0:T(8,128)(2,1)} %x.1), custom_call_target="tpu_custom_call" | custom-call | flops 4000000000 | bytes 1000 | tf_op jit(solution)/shard_map/pallas_call | solution.py:340
  1.7 2.6 %collective-permute-start = (bf16[128,1024]{1,0:T(8,128)(2,1)S(1)}, bf16[128,1024]{1,0:T(8,128)(2,1)S(1)}, u32[]{:S(2)}, u32[]{:S(2)}) collective-permute-start(bf16[128,1024]{1,0:T(8,128)(2,1)S(1)} %get-tuple-element.33.x0), channel_id=1, source_target_pairs={{0,2},{1,3},{2,0},{3,1},{4,6},{5,7},{6,4},{7,5},{8,10},{9,11},{10,... | collective-permute-start | bytes 786440 | tf_op jit(solution)/shard_map/ppermute | solution.py:366
  4.3 0.1 collective-permute-start.1
  4.4 1.9 %collective-permute-start.2 = (bf16[128,1024]{1,0:T(8,128)(2,1)S(1)}, bf16[128,1024]{1,0:T(8,128)(2,1)S(1)}, u32[]{:S(2)}, u32[]{:S(2)}) collective-permute-start(bf16[128,1024]{1,0:T(8,128)(2,1)S(1)} %get-tuple-element.32.x2), channel_id=1, source_target_pairs={{0,2},{1,3},{2,0},{3,1},{4,6},{5,7},{6,4},{7,5},{8,10},{9,11},{10,... | collective-permute-start | bytes 786440 | tf_op jit(solution)/shard_map/ppermute | solution.py:366
  6.3 0.6 %shard_map.58 = bf16[64,1024]{1,0:T(8,128)(2,1)S(1)} custom-call(s32[6]{0:T(128)S(1)} %copy-done.1, bf16[128,1024]{1,0:T(8,128)(2,1)S(1)} %get-tuple-element.33.x0, bf16[128,1024]{1,0:T(8,128)(2,1)S(1)} %get-tuple-element.31.x1, bf16[128,1024]{1,0:T(8,128)(2,1)S(1)} %get-tuple-element.32.x2), custom_call_target="tpu_custom_call" | custom-call | flops 4000000000 | bytes 1000 | tf_op jit(solution)/shard_map/pallas_call | solution.py:340
  6.9 1.6 %collective-permute-start.7 = (bf16[64,1024]{1,0:T(8,128)(2,1)S(1)}, bf16[64,1024]{1,0:T(8,128)(2,1)S(1)}, u32[]{:S(2)}, u32[]{:S(2)}) collective-permute-start(bf16[64,1024]{1,0:T(8,128)(2,1)S(1)} %shard_map.58), channel_id=1, source_target_pairs={{0,4},{1,5},{2,14},{3,15},{4,8},{5,9},{6,2},{7,3},{8,12},{9,13},{1... | collective-permute-start | bytes 393224 | tf_op jit(solution)/shard_map/ppermute | solution.py:366
  8.6 0.1 copy.9.nbr
  8.7 2.8 %collective-permute-done.f0 = bf16[128,1024]{1,0:T(8,128)(2,1)S(1)} collective-permute-done((bf16[128,1024]{1,0:T(8,128)(2,1)S(1)}, bf16[128,1024]{1,0:T(8,128)(2,1)S(1)}, u32[]{:S(2)}, u32[]{:S(2)}) %collective-permute-start) | collective-permute-done | bytes 262176 | tf_op jit(solution)/shard_map/ppermute | solution.py:366
  11.5 4.0 %collective-permute-start.8 = (bf16[64,1024]{1,0:T(8,128)(2,1)S(1)}, bf16[64,1024]{1,0:T(8,128)(2,1)S(1)}, u32[]{:S(2)}, u32[]{:S(2)}) collective-permute-start(bf16[64,1024]{1,0:T(8,128)(2,1)S(1)} %shard_map.58), channel_id=1, source_target_pairs={{0,12},{1,13},{2,6},{3,7},{4,0},{5,1},{6,10},{7,11},{8,4},{9,5},{1... | collective-permute-start | bytes 393224 | tf_op jit(solution)/shard_map/ppermute | solution.py:366
  15.5 0.0 collective-permute-done.4.s
  15.5 11.5 %shard_map.56 = (bf16[24,64,256]{2,1,0:T(8,128)(2,1)S(1)}, bf16[6,4,128,256]{3,2,1,0:T(8,128)(2,1)S(1)}, bf16[6,4,256,128]{3,2,1,0:T(8,128)(2,1)S(1)}, bf16[1024...) custom-call(bf16[128,1024]{1,0:T(8,128)(2,1)S(1)} %get-tuple-element.33.x0, bf16[128,1024]{1,0:T(8,128)(2,1)S(1)} %get-tuple-element.31.x1, ...), custom_call_target="tpu_custom_call" | custom-call | flops 4000000000 | bytes 1000 | tf_op jit(solution)/shard_map/pallas_call | solution.py:340
  27.0 0.1 collective-permute-start.5
  27.1 2.9 %shard_map.57 = (f32[24,1,256]{2,1,0:T(1,128)S(1)}, f32[24,1,256]{2,1,0:T(1,128)S(1)}, f32[24,64,256]{2,1,0:T(8,128)S(1)}) custom-call(s32[6,2]{1,0:T(8,128)S(1)} %copy.9.nbr, bf16[24,64,256]{2,1,0:T(8,128)(2,1)S(1)} %get-tuple-element.36.qc, bf16[6,4,128,256]{3,2,1,0:T(8,128)(2,1)S(1)} %get-tuple-element.37.keys, ...), custom_call_target="tpu_custom_call" | custom-call | flops 4000000000 | bytes 1000 | tf_op jit(solution)/shard_map/pallas_call | solution.py:340
  30.0 1.8 %collective-permute-start.6 = (bf16[128,1024]{1,0:T(8,128)(2,1)S(1)}, bf16[128,1024]{1,0:T(8,128)(2,1)S(1)}, u32[]{:S(2)}, u32[]{:S(2)}) collective-permute-start(bf16[128,1024]{1,0:T(8,128)(2,1)S(1)} %collective-permute-done.2.f2), channel_id=1, source_target_pairs={{0,4},{1,5},{2,14},{3,15},{4,8},{5,9},{6,2},{7,3},{8,12},{9,13},{1... | collective-permute-start | bytes 786440 | tf_op jit(solution)/shard_map/ppermute | solution.py:366
  31.8 6.2 %shard_map.59 = (f32[24,1,256]{2,1,0:T(1,128)S(1)}, f32[24,1,256]{2,1,0:T(1,128)S(1)}, f32[24,64,256]{2,1,0:T(8,128)S(1)}) custom-call(s32[6,2]{1,0:T(8,128)S(1)} %copy.9.nbr, s32[6]{0:T(128)S(1)} %copy-done.1, bf16[128,1024]{1,0:T(8,128)(2,1)S(1)} %collective-permute-done.f0, bf16[128,1024]{1,0:T(8,128)(2,1)S(1)} %collective-permute-done.1.f1, ...), custom_call_target="tpu_custom_call" | custom-call | flops 4000000000 | bytes 1000 | tf_op jit(solution)/shard_map/pallas_call | solution.py:340
  38.0 0.1 collective-permute-done.5.g1
  38.1 1.4 %shard_map.60 = (bf16[4,4,64,256]{3,2,1,0:T(8,128)(2,1)S(1)}, bf16[2,4,4,256,128]{4,3,2,1,0:T(8,128)(2,1)S(1)}) custom-call(bf16[128,1024]{1,0:T(8,128)(2,1)S(1)} %collective-permute-done.3.g0, bf16[128,1024]{1,0:T(8,128)(2,1)S(1)} %collective-permute-done.5.g1, bf16[1024,1024]{1,0:T(8,128)(2,1)S(1)} %get-tuple-element.41.w, ...), custom_call_target="tpu_custom_call" | custom-call | flops 4000000000 | bytes 1000 | tf_op jit(solution)/shard_map/pallas_call | solution.py:340
  39.5 2.3 %collective-permute-done.6.g2 = bf16[128,1024]{1,0:T(8,128)(2,1)S(1)} collective-permute-done((bf16[128,1024]{1,0:T(8,128)(2,1)S(1)}, bf16[128,1024]{1,0:T(8,128)(2,1)S(1)}, u32[]{:S(2)}, u32[]{:S(2)}) %collective-permute-start.6) | collective-permute-done | bytes 262176 | tf_op jit(solution)/shard_map/ppermute | solution.py:366
  41.8 0.9 %shard_map.61 = bf16[512,1024]{1,0:T(8,128)(2,1)S(1)} custom-call(s32[6]{0:T(128)S(1)} %copy-done.1, bf16[128,1024]{1,0:T(8,128)(2,1)S(1)} %collective-permute-done.f0, bf16[128,1024]{1,0:T(8,128)(2,1)S(1)} %collective-permute-done.1.f1, bf16[128,1024]{1,0:T(8,128)(2,1)S(1)} %collective-permute-done.2.f2, bf16[128,1024]{1,0:T(8,128)(2,1)S(1)} %collective-permute-done.3.g0, ...), custom_call_target="tpu_custom_call" | custom-call | flops 4000000000 | bytes 1000 | tf_op jit(solution)/shard_map/pallas_call | solution.py:340
  42.6 0.1 collective-permute-start.9
  42.7 0.0 copy-start
  42.7 5.6 %shard_map.62 = (f32[24,1,256]{2,1,0:T(1,128)S(1)}, f32[24,1,256]{2,1,0:T(1,128)S(1)}, f32[24,64,256]{2,1,0:T(8,128)S(1)}) custom-call(s32[6,2]{1,0:T(8,128)S(1)} %copy.9.nbr, s32[6]{0:T(128)S(1)} %copy-done.1, bf16[128,1024]{1,0:T(8,128)(2,1)S(1)} %collective-permute-done.6.g2, bf16[1024,1024]{1,0:T(8,128)(2,1)S(1)} %get-tuple-element.41.w, ...), custom_call_target="tpu_custom_call" | custom-call | flops 4000000000 | bytes 1000 | tf_op jit(solution)/shard_map/pallas_call | solution.py:340
  48.3 8.4 %shard_map.63 = bf16[2,192,1024]{2,1,0:T(8,128)(2,1)} custom-call(s32[6,2]{1,0:T(8,128)S(1)} %copy.9.nbr, s32[6]{0:T(128)S(1)} %copy-done.1, bf16[512,1024]{1,0:T(8,128)(2,1)S(1)} %collective-permute-done.9.e, bf16[1024,1024]{1,0:T(8,128)(2,1)S(1)} %get-tuple-element.41.w, bf16[1024,1024]{1,0:T(8,128)(2,1)S(1)} %get-tuple-element.42.wvt, ...), custom_call_target="tpu_custom_call" | custom-call | flops 4000000000 | bytes 1000 | tf_op jit(solution)/shard_map/pallas_call | solution.py:340
  (12 shorter events, 0.0 us)
Async XLA Ops:
  0.0 6.3 %copy-start.1 = (s32[6]{0:T(128)S(1)}, s32[6]{0:T(128)}, u32[]{:S(2)}) copy-start(s32[6]{0:T(128)} %hw.9) | copy-start | bytes 76
  0.0 15.5 %collective-permute-start.4 = (bf16[2,192,1024]{2,1,0:T(8,128)(2,1)}, bf16[2,192,1024]{2,1,0:T(8,128)(2,1)S(1)}, u32[]{:S(2)}, u32[]{:S(2)}) collective-permute-start(bf16[2,192,1024]{2,1,0:T(8,128)(2,1)} %x.1), channel_id=1, source_target_pairs={{0,1},{1,0},{2,3},{3,2},{4,5},{5,4},{6,7},{7,6},{8,9},{9,8},{10,11... | collective-permute-start | bytes 2359304 | tf_op jit(solution)/shard_map/ppermute | solution.py:366
  1.7 9.8 %collective-permute-start = (bf16[128,1024]{1,0:T(8,128)(2,1)S(1)}, bf16[128,1024]{1,0:T(8,128)(2,1)S(1)}, u32[]{:S(2)}, u32[]{:S(2)}) collective-permute-start(bf16[128,1024]{1,0:T(8,128)(2,1)S(1)} %get-tuple-element.33.x0), channel_id=1, source_target_pairs={{0,2},{1,3},{2,0},{3,1},{4,6},{5,7},{6,4},{7,5},{8,10},{9,11},{10,... | collective-permute-start | bytes 786440 | tf_op jit(solution)/shard_map/ppermute | solution.py:366
  4.3 22.7 %collective-permute-start.1 = (bf16[128,1024]{1,0:T(8,128)(2,1)S(1)}, bf16[128,1024]{1,0:T(8,128)(2,1)S(1)}, u32[]{:S(2)}, u32[]{:S(2)}) collective-permute-start(bf16[128,1024]{1,0:T(8,128)(2,1)S(1)} %get-tuple-element.31.x1), channel_id=1, source_target_pairs={{0,2},{1,3},{2,0},{3,1},{4,6},{5,7},{6,4},{7,5},{8,10},{9,11},{10,... | collective-permute-start | bytes 786440 | tf_op jit(solution)/shard_map/ppermute | solution.py:366
  4.4 4.2 %copy-start.2 = (s32[6,2]{0,1:T(2,128)S(1)}, s32[6,2]{0,1:T(2,128)}, u32[]{:S(2)}) copy-start(s32[6,2]{0,1:T(2,128)} %param.9) | copy-start | bytes 148
  4.4 25.6 %collective-permute-start.2 = (bf16[128,1024]{1,0:T(8,128)(2,1)S(1)}, bf16[128,1024]{1,0:T(8,128)(2,1)S(1)}, u32[]{:S(2)}, u32[]{:S(2)}) collective-permute-start(bf16[128,1024]{1,0:T(8,128)(2,1)S(1)} %get-tuple-element.32.x2), channel_id=1, source_target_pairs={{0,2},{1,3},{2,0},{3,1},{4,6},{5,7},{6,4},{7,5},{8,10},{9,11},{10,... | collective-permute-start | bytes 786440 | tf_op jit(solution)/shard_map/ppermute | solution.py:366
  6.9 24.9 %collective-permute-start.7 = (bf16[64,1024]{1,0:T(8,128)(2,1)S(1)}, bf16[64,1024]{1,0:T(8,128)(2,1)S(1)}, u32[]{:S(2)}, u32[]{:S(2)}) collective-permute-start(bf16[64,1024]{1,0:T(8,128)(2,1)S(1)} %shard_map.58), channel_id=1, source_target_pairs={{0,4},{1,5},{2,14},{3,15},{4,8},{5,9},{6,2},{7,3},{8,12},{9,13},{1... | collective-permute-start | bytes 393224 | tf_op jit(solution)/shard_map/ppermute | solution.py:366
  11.5 20.4 %collective-permute-start.8 = (bf16[64,1024]{1,0:T(8,128)(2,1)S(1)}, bf16[64,1024]{1,0:T(8,128)(2,1)S(1)}, u32[]{:S(2)}, u32[]{:S(2)}) collective-permute-start(bf16[64,1024]{1,0:T(8,128)(2,1)S(1)} %shard_map.58), channel_id=1, source_target_pairs={{0,12},{1,13},{2,6},{3,7},{4,0},{5,1},{6,10},{7,11},{8,4},{9,5},{1... | collective-permute-start | bytes 393224 | tf_op jit(solution)/shard_map/ppermute | solution.py:366
  15.5 22.5 %collective-permute-start.3 = (bf16[128,1024]{1,0:T(8,128)(2,1)S(1)}, bf16[128,1024]{1,0:T(8,128)(2,1)S(1)}, u32[]{:S(2)}, u32[]{:S(2)}) collective-permute-start(bf16[128,1024]{1,0:T(8,128)(2,1)S(1)} %collective-permute-done.f0), channel_id=1, source_target_pairs={{0,4},{1,5},{2,14},{3,15},{4,8},{5,9},{6,2},{7,3},{8,12},{9,13},{1... | collective-permute-start | bytes 786440 | tf_op jit(solution)/shard_map/ppermute | solution.py:366
  27.0 11.1 %collective-permute-start.5 = (bf16[128,1024]{1,0:T(8,128)(2,1)S(1)}, bf16[128,1024]{1,0:T(8,128)(2,1)S(1)}, u32[]{:S(2)}, u32[]{:S(2)}) collective-permute-start(bf16[128,1024]{1,0:T(8,128)(2,1)S(1)} %collective-permute-done.1.f1), channel_id=1, source_target_pairs={{0,4},{1,5},{2,14},{3,15},{4,8},{5,9},{6,2},{7,3},{8,12},{9,13},{1... | collective-permute-start | bytes 786440 | tf_op jit(solution)/shard_map/ppermute | solution.py:366
  30.0 11.7 %collective-permute-start.6 = (bf16[128,1024]{1,0:T(8,128)(2,1)S(1)}, bf16[128,1024]{1,0:T(8,128)(2,1)S(1)}, u32[]{:S(2)}, u32[]{:S(2)}) collective-permute-start(bf16[128,1024]{1,0:T(8,128)(2,1)S(1)} %collective-permute-done.2.f2), channel_id=1, source_target_pairs={{0,4},{1,5},{2,14},{3,15},{4,8},{5,9},{6,2},{7,3},{8,12},{9,13},{1... | collective-permute-start | bytes 786440 | tf_op jit(solution)/shard_map/ppermute | solution.py:366
  42.6 5.7 %collective-permute-start.9 = (bf16[512,1024]{1,0:T(8,128)(2,1)S(1)}, bf16[512,1024]{1,0:T(8,128)(2,1)S(1)}, u32[]{:S(2)}, u32[]{:S(2)}) collective-permute-start(bf16[512,1024]{1,0:T(8,128)(2,1)S(1)} %shard_map.61), channel_id=1, source_target_pairs={{0,1},{1,0},{2,3},{3,2},{4,5},{5,4},{6,7},{7,6},{8,9},{9,8},{10,11... | collective-permute-start | bytes 3145736 | tf_op jit(solution)/shard_map/ppermute | solution.py:366
  42.7 5.6 %copy-start = (bf16[1024,1024]{1,0:T(8,128)(2,1)S(1)}, bf16[1024,1024]{1,0:T(8,128)(2,1)}, u32[]{:S(2)}) copy-start(bf16[1024,1024]{1,0:T(8,128)(2,1)} %wout.1) | copy-start | bytes 6291460

commit v4 on v3

--- a/solution.py
+++ b/solution.py
@@ -17,10 +17,10 @@
 F32 = jnp.float32
 SCALE = math.log2(math.e) / math.sqrt(HEAD)
 VMEM_LIMIT = 28 * 1024 * 1024
-COST = 4000000000
+COST = 2000000000
 EARLY_COST = 4000000000
-NEAR_COST = 4000000000
-ACROSS_COST = 4000000000
+NEAR_COST = 2000000000
+ACROSS_COST = 2000000000
 
 
 def lane_head(shape):
@@ -110,34 +110,27 @@
         copy.wait()
 
 
-def band_kernel(hw, x0, x1, x2, band):
+def band_kernel(hw, x0, x1, x2, s, bands):
     wide = widest_of(hw)
-    rows = band.shape[0]
+    lon = s.shape[0]
+    rows = bands.shape[0] // 2
+    span = rows // lon
     per = x0.shape[0] // rows
     for c in range(CHUNKS * per):
 
         @pl.when(wide == c)
         def _(c=c):
             at = (c % per) * rows
-            band[...] = (x0, x1, x2)[c // per][at : at + rows, :]
-
-
-def own_kernel(x0, x1, x2, s, w, qc, keys, vals, wk, wvt, own, both, wq, wv, sems):
+            bands[:rows, :] = (x0, x1, x2)[c // per][at : at + rows, :]
+            for o in range(lon):
+                bands[rows + o * span : rows + (o + 1) * span, :] = s[o, c * span : (c + 1) * span, :]
+
+
+def own_kernel(x0, x1, x2, s, w, qc, keys, vals, wvt, own, both):
     lon, _, width = s.shape
     nlb, groups, rows, _ = keys.shape
     rows //= 2
     span = rows // lon
-    fetch = []
-    for which, place in ((1, wk), (0, wq), (2, wv)):
-        for g in range(groups):
-            fetch.append(
-                pltpu.make_async_copy(
-                    w.at[:, pl.ds(which * width + g * WIDE, WIDE)],
-                    place.at[:, pl.ds(g * WIDE, WIDE)],
-                    sems.at[len(fetch)],
-                )
-            )
-            fetch[-1].start()
     at = 0
     for part in (x0, x1, x2):
         for c in range(part.shape[0] // rows):
@@ -150,21 +143,17 @@
             at = (2 * c + 1) * rows + o * span
             both[at : at + span, :] = s[o, c * span : (c + 1) * span, :]
     for g in range(groups):
-        fetch[g].wait()
-        k = dot(both[...], wk[:, g * WIDE : (g + 1) * WIDE]).astype(BF16)
+        k = dot(both[...], w[:, width + g * WIDE : width + (g + 1) * WIDE]).astype(BF16)
         for c in range(nlb):
             keys[c, g] = k[2 * c * rows : 2 * (c + 1) * rows, :]
-    for g in range(groups):
-        fetch[groups + g].wait()
-        q = dot(own[...], wq[:, g * WIDE : (g + 1) * WIDE]).astype(BF16).astype(F32)
+        q = dot(own[...], w[:, g * WIDE : (g + 1) * WIDE]).astype(BF16).astype(F32)
         for b in range(nlb):
             qt = q[b * rows : (b + 1) * rows, :].T
             qc[b * groups + g] = jnp.concatenate(
                 [qt[h * HEAD : (h + 1) * HEAD, :] for h in range(PACK)], axis=1
             ).astype(BF16)
-    for g in range(groups):
-        fetch[2 * groups + g].wait()
-        wvt[g * WIDE : (g + 1) * WIDE, :] = wv[:, g * WIDE : (g + 1) * WIDE].T
+        at = 2 * width + g * WIDE
+        wvt[g * WIDE : (g + 1) * WIDE, :] = w[:, at : at + WIDE].T
         v = dot_nt(wvt[g * WIDE : (g + 1) * WIDE, :], both[...]).astype(BF16)
         for c in range(nlb):
             vals[c, g] = v[:, 2 * c * rows : 2 * (c + 1) * rows]
@@ -188,8 +177,9 @@
 
 def project_far(tokens, w, wvt, keys, vals, wkeys, wvals):
     nlb, groups, rows, _ = keys.shape
+    width = tokens.shape[1]
     for g in range(groups):
-        k = dot(tokens[...], w[:, g * WIDE : (g + 1) * WIDE]).astype(BF16)
+        k = dot(tokens[...], w[:, width + g * WIDE : width + (g + 1) * WIDE]).astype(BF16)
         parts, rest = project_values(wvt, tokens[...], g, nlb, rows)
         for c in range(nlb):
             keys[c, g] = k[c * rows : (c + 1) * rows, :]
@@ -253,10 +243,10 @@
     return store
 
 
-def across_kernel(nbr, hw, f0, f1, f2, wf, wb, w, wvt, qc, m_in, l_in, acc_in,
+def across_kernel(nbr, hw, f0, f1, f2, bands, w, wvt, qc, m_in, l_in, acc_in,
                   m, l, acc, tokens, keys, vals, wkeys, wvals):
     at = 0
-    for part in (f0, f1, f2, wf, wb):
+    for part in (f0, f1, f2, bands):
         tokens[at : at + part.shape[0], :] = part[...]
         at += part.shape[0]
     project_far(tokens, w, wvt, keys, vals, wkeys, wvals)
@@ -276,18 +266,18 @@
     attend_far(nbr, hw, None, qc, *picks, None, None, (m_in, l_in, acc_in), store)
 
 
-def payload_kernel(hw, f0, f1, f2, g0, g1, g2, wf, wb, out):
+def payload_kernel(hw, f0, f1, f2, g0, g1, g2, bands, out):
     here = lax.axis_index("lon")
     wide = widest_of(hw)
     size = f0.shape[0]
-    rows = wf.shape[0]
+    rows = bands.shape[0] // 2
     per = size // rows
     base = CHUNKS * size
 
-    def fill(sent, other, wide_sent):
+    def fill(sent, other):
         for j in range(CHUNKS):
             out[j * size : (j + 1) * size, :] = sent[j][...]
-        out[base : base + rows, :] = wide_sent[...]
+        out[base : base + rows, :] = bands[rows:, :]
         for c in range(CHUNKS * per):
 
             @pl.when(wide == c)
@@ -299,11 +289,11 @@
 
     @pl.when(kind == 0)
     def _():
-        fill((f0, f1, f2), (g0, g1, g2), wb)
+        fill((f0, f1, f2), (g0, g1, g2))
 
     @pl.when(kind != 0)
     def _():
-        fill((g0, g1, g2), (f0, f1, f2), wf)
+        fill((g0, g1, g2), (f0, f1, f2))
 
 
 def last_kernel(nbr, hw, e, w, wvt, wout, qc, m_in, l_in, acc_in, out, keys, vals, wkeys, wvals, attended):
@@ -374,8 +364,8 @@
     def onward(i):
         return i - 4 if i & 2 else i + 4
 
-    def backward(i):
-        return i + 4 if i & 2 else i - 4
+    def outward(i):
+        return i - 4 if i & 1 else i + 4
 
     tile = (tiles, HEAD, WIDE)
     row = (tiles, 1, WIDE)
@@ -397,14 +387,13 @@
         prepare_kernel, (), (tokens,), [chunk] * CHUNKS, [pltpu.SemaphoreType.DMA((nlb * lon,))], unread=1
     )
     f = [permute(part, across) for part in parts]
-    band = call(
-        band_kernel, (half_width,), tuple(parts), jax.ShapeDtypeStruct((rows, width), BF16), []
-    )
-    wf = permute(band, onward)
-    wb = permute(band, backward)
+    bands = call(
+        band_kernel, (half_width,), (*parts, beside), jax.ShapeDtypeStruct((2 * rows, width), BF16), []
+    )
+    bands = permute(bands, outward)
     g0 = permute(f[0], onward)
     held, *_ = lax.optimization_barrier((parts[0], f[0]))
-    qc, keys, vals, wk, wvt = call(
+    qc, keys, vals, wvt = call(
         own_kernel,
         (),
         (held, *parts[1:], beside, projection),
@@ -413,22 +402,14 @@
             jax.ShapeDtypeStruct((nlb, groups, 2 * rows, WIDE), BF16),
             jax.ShapeDtypeStruct((nlb, groups, WIDE, 2 * rows), BF16),
             jax.ShapeDtypeStruct((width, width), BF16),
-            jax.ShapeDtypeStruct((width, width), BF16),
         ],
-        [
-            pltpu.VMEM((nlb * rows, width), BF16),
-            pltpu.VMEM((2 * nlb * rows, width), BF16),
-            pltpu.VMEM((width, width), BF16),
-            pltpu.VMEM((width, width), BF16),
-            pltpu.SemaphoreType.DMA((3 * groups,)),
-        ],
-        unread=1,
+        [pltpu.VMEM((nlb * rows, width), BF16), pltpu.VMEM((2 * nlb * rows, width), BF16)],
     )
     g1 = permute(after(f[1], qc), onward)
     m, l, acc = call(
         near_kernel,
         (neighbours,),
-        (after(qc, f[1]), keys, vals),
+        (after(qc, f[1], bands), keys, vals),
         carried_shapes,
         [],
         cost=NEAR_COST,
@@ -437,7 +418,7 @@
     m, l, acc = call(
         across_kernel,
         (neighbours, half_width),
-        (*f, wf, wb, wk, wvt, qc, m, l, acc),
+        (*f, bands, projection, wvt, qc, m, l, acc),
         carried_shapes,
         [pltpu.VMEM(((nlb + 2) * rows, width), BF16), key_scratch, val_scratch, *wide_scratch],
         cost=ACROSS_COST,
@@ -446,7 +427,7 @@
     early_keys, early_vals = call(
         early_kernel,
         (),
-        (after(g0, m), g1, wk, wvt),
+        (after(g0, m), g1, projection, wvt),
         [
             jax.ShapeDtypeStruct((early, groups, rows, WIDE), BF16),
             jax.ShapeDtypeStruct((2, early, groups, WIDE, 2 * rows), BF16),
@@ -457,7 +438,7 @@
     e = call(
         payload_kernel,
         (half_width,),
-        (*f, g0, g1, g2, after(wf, early_keys), wb),
+        (*f, g0, g1, g2, after(bands, early_keys)),
         jax.ShapeDtypeStruct(((nlb + 2) * rows, width), BF16),
         [],
     )
@@ -465,7 +446,7 @@
     m, l, acc = call(
         onward_kernel,
         (neighbours, half_width),
-        (g2, wk, wvt, qc, early_keys, early_vals, m, l, acc),
+        (g2, projection, wvt, qc, early_keys, early_vals, m, l, acc),
         carried_shapes,
         [
             pltpu.VMEM((nlb - early, groups, rows, WIDE), BF16),
@@ -475,7 +456,7 @@
     return call(
         last_kernel,
         (neighbours, half_width),
-        (e, wk, wvt, out_weight, qc, m, l, acc),
+        (e, projection, wvt, out_weight, qc, m, l, acc),
         jax.ShapeDtypeStruct(tokens.shape, BF16),
         [
             key_scratch,

time: 56.9 us -> 50.5 us (0.89)
  Pallas kernels: 38.6 us -> 31.4 us
  local copies, waits for them, and re-layouts: 0.11 us -> 2.89 us
  waiting for transfers between devices: 5.21 us -> 3.6 us
    pallas_call x9, Pallas kernels: 38.6 us -> 31.4 us  [call(): pl.pallas_call(kernel, out_shape=outs, in_specs=[smem] * len(scalars) + s...]
    unnamed x7 -> x11, local copies, waits for them, and re-layouts: 0.11 us -> 2.89 us
    ppermute x10 -> x9, waiting for transfers between devices: 5.21 us -> 3.6 us  [permute(): return lax.ppermute(block, 'lon', [(i, step(i) % count) for i in devices])]
    ppermute x10 -> x9, starting transfers between devices: 12.6 us -> 12.2 us  [permute(): return lax.ppermute(block, 'lon', [(i, step(i) % count) for i in devices])]
  transfers between devices with their start and end apart: 10 -> 9, of which waited for: 3 -> 2; matrix products, arithmetic and copies ran while one was open for 0% -> 0% of each run, Pallas kernels for 52% -> 44%
where the time goes in v4:
time: 50.5 us; the launch traced here: 50.3 us
  Pallas kernels  31.4 us (62%)
  starting transfers between devices  12.2 us (24%)
  waiting for transfers between devices  3.6 us (7%)
  local copies, waits for them, and re-layouts  2.89 us (6%)
    pallas_call x9, Pallas kernels, call(): pl.pallas_call(kernel, out_shape=outs, in_specs=[smem] * len(scalars) + s...  31.4 us
    ppermute x9, starting transfers between devices, permute(): return lax.ppermute(block, 'lon', [(i, step(i) % count) for i in devices])  12.2 us
    ppermute x9, waiting for transfers between devices, permute(): return lax.ppermute(block, 'lon', [(i, step(i) % count) for i in devices])  3.6 us
    unnamed x11, local copies, waits for them, and re-layouts  2.89 us
  transfers between devices with their start and end apart: 9, of which 2 were waited for; matrix products, arithmetic and copies ran while one was open for 0% of the time, Pallas kernels for 44%

profile of v4, /device:TPU:0, one launch (start us, length us, event | category | flops | bytes accessed | tf_op | source)
XLA Modules:
  0.0 50.3 jit_solution(14157152740715505683)
XLA Ops:
  0.0 0.5 collective-permute-start.4
  0.5 1.3 %shard_map.55 = (bf16[128,1024]{1,0:T(8,128)(2,1)S(1)}, bf16[128,1024]{1,0:T(8,128)(2,1)S(1)}, bf16[128,1024]{1,0:T(8,128)(2,1)S(1)}) custom-call(bf16[2,192,1024]{2,1,0:T(8,128)(2,1)} %x.1), custom_call_target="tpu_custom_call" | custom-call | flops 2000000000 | bytes 1000 | tf_op jit(solution)/shard_map/pallas_call | solution.py:330
  1.7 2.6 %collective-permute-start = (bf16[128,1024]{1,0:T(8,128)(2,1)S(1)}, bf16[128,1024]{1,0:T(8,128)(2,1)S(1)}, u32[]{:S(2)}, u32[]{:S(2)}) collective-permute-start(bf16[128,1024]{1,0:T(8,128)(2,1)S(1)} %get-tuple-element.32.x0), channel_id=1, source_target_pairs={{0,2},{1,3},{2,0},{3,1},{4,6},{5,7},{6,4},{7,5},{8,10},{9,11},{10,... | collective-permute-start | bytes 786440 | tf_op jit(solution)/shard_map/ppermute | solution.py:356
  4.3 0.1 collective-permute-start.1
  4.4 0.6 %shard_map.57 = bf16[128,1024]{1,0:T(8,128)(2,1)S(1)} custom-call(s32[6]{0:T(128)S(1)} %copy-done.3, bf16[128,1024]{1,0:T(8,128)(2,1)S(1)} %get-tuple-element.32.x0, bf16[128,1024]{1,0:T(8,128)(2,1)S(1)} %get-tuple-element.30.x1, bf16[128,1024]{1,0:T(8,128)(2,1)S(1)} %get-tuple-element.31.x2, bf16[2,192,1024]{2,1,0:T(8,128)(2,1)S(1)} %collective-permute-done.4.s), custom_call_target="tpu_custom_call" | custom-call | flops 2000000000 | bytes 1000 | tf_op jit(solution)/shard_map/pallas_call | solution.py:330
  5.0 2.1 %collective-permute-start.6 = (bf16[128,1024]{1,0:T(8,128)(2,1)S(1)}, bf16[128,1024]{1,0:T(8,128)(2,1)S(1)}, u32[]{:S(2)}, u32[]{:S(2)}) collective-permute-start(bf16[128,1024]{1,0:T(8,128)(2,1)S(1)} %shard_map.57), channel_id=1, source_target_pairs={{0,4},{1,13},{2,6},{3,15},{4,8},{5,1},{6,10},{7,3},{8,12},{9,5},{1... | collective-permute-start | bytes 786440 | tf_op jit(solution)/shard_map/ppermute | solution.py:356
  7.1 1.5 %collective-permute-start.2 = (bf16[128,1024]{1,0:T(8,128)(2,1)S(1)}, bf16[128,1024]{1,0:T(8,128)(2,1)S(1)}, u32[]{:S(2)}, u32[]{:S(2)}) collective-permute-start(bf16[128,1024]{1,0:T(8,128)(2,1)S(1)} %get-tuple-element.31.x2), channel_id=1, source_target_pairs={{0,2},{1,3},{2,0},{3,1},{4,6},{5,7},{6,4},{7,5},{8,10},{9,11},{10,... | collective-permute-start | bytes 786440 | tf_op jit(solution)/shard_map/ppermute | solution.py:356
  8.6 0.1 copy.9.nbr
  8.7 2.8 %collective-permute-done.f0 = bf16[128,1024]{1,0:T(8,128)(2,1)S(1)} collective-permute-done((bf16[128,1024]{1,0:T(8,128)(2,1)S(1)}, bf16[128,1024]{1,0:T(8,128)(2,1)S(1)}, u32[]{:S(2)}, u32[]{:S(2)}) %collective-permute-start) | collective-permute-done | bytes 262176 | tf_op jit(solution)/shard_map/ppermute | solution.py:356
  11.5 2.0 %collective-permute-start.3 = (bf16[128,1024]{1,0:T(8,128)(2,1)S(1)}, bf16[128,1024]{1,0:T(8,128)(2,1)S(1)}, u32[]{:S(2)}, u32[]{:S(2)}) collective-permute-start(bf16[128,1024]{1,0:T(8,128)(2,1)S(1)} %collective-permute-done.f0), channel_id=1, source_target_pairs={{0,4},{1,5},{2,14},{3,15},{4,8},{5,9},{6,2},{7,3},{8,12},{9,13},{1... | collective-permute-start | bytes 786440 | tf_op jit(solution)/shard_map/ppermute | solution.py:356
  13.5 2.8 %copy-done = bf16[1024,3072]{1,0:T(8,128)(2,1)S(1)} copy-done((bf16[1024,3072]{1,0:T(8,128)(2,1)S(1)}, bf16[1024,3072]{1,0:T(8,128)(2,1)}, u32[]{:S(2)}) %copy-start) | copy-done | bytes 6291480
  16.3 4.3 %shard_map.56 = (bf16[24,64,256]{2,1,0:T(8,128)(2,1)S(1)}, bf16[6,4,128,256]{3,2,1,0:T(8,128)(2,1)S(1)}, bf16[6,4,256,128]{3,2,1,0:T(8,128)(2,1)S(1)}, bf16[1024,1024]{1,0:T(8,128)(2,1)S(1)}) custom-call(bf16[128,1024]{1,0:T(8,128)(2,1)S(1)} %get-tuple-element.32.x0, bf16[128,1024]{1,0:T(8,128)(2,1)S(1)} %get-tuple-element.30.x1, ...), custom_call_target="tpu_custom_call" | custom-call | flops 2000000000 | bytes 1000 | tf_op jit(solution)/shard_map/pallas_call | solution.py:330
  20.6 1.6 %collective-permute-start.5 = (bf16[128,1024]{1,0:T(8,128)(2,1)S(1)}, bf16[128,1024]{1,0:T(8,128)(2,1)S(1)}, u32[]{:S(2)}, u32[]{:S(2)}) collective-permute-start(bf16[128,1024]{1,0:T(8,128)(2,1)S(1)} %collective-permute-done.1.f1), channel_id=1, source_target_pairs={{0,4},{1,5},{2,14},{3,15},{4,8},{5,9},{6,2},{7,3},{8,12},{9,13},{1... | collective-permute-start | bytes 786440 | tf_op jit(solution)/shard_map/ppermute | solution.py:356
  22.2 2.9 %shard_map.58 = (f32[24,1,256]{2,1,0:T(1,128)S(1)}, f32[24,1,256]{2,1,0:T(1,128)S(1)}, f32[24,64,256]{2,1,0:T(8,128)S(1)}) custom-call(s32[6,2]{1,0:T(8,128)S(1)} %copy.9.nbr, bf16[24,64,256]{2,1,0:T(8,128)(2,1)S(1)} %get-tuple-element.35.qc, bf16[6,4,128,256]{3,2,1,0:T(8,128)(2,1)S(1)} %get-tuple-element.36.keys, ...), custom_call_target="tpu_custom_call" | custom-call | flops 2000000000 | bytes 1000 | tf_op jit(solution)/shard_map/pallas_call | solution.py:330
  25.1 1.8 %collective-permute-start.7 = (bf16[128,1024]{1,0:T(8,128)(2,1)S(1)}, bf16[128,1024]{1,0:T(8,128)(2,1)S(1)}, u32[]{:S(2)}, u32[]{:S(2)}) collective-permute-start(bf16[128,1024]{1,0:T(8,128)(2,1)S(1)} %collective-permute-done.2.f2), channel_id=1, source_target_pairs={{0,4},{1,5},{2,14},{3,15},{4,8},{5,9},{6,2},{7,3},{8,12},{9,13},{1... | collective-permute-start | bytes 786440 | tf_op jit(solution)/shard_map/ppermute | solution.py:356
  26.9 6.2 %shard_map.59 = (f32[24,1,256]{2,1,0:T(1,128)S(1)}, f32[24,1,256]{2,1,0:T(1,128)S(1)}, f32[24,64,256]{2,1,0:T(8,128)S(1)}) custom-call(s32[6,2]{1,0:T(8,128)S(1)} %copy.9.nbr, s32[6]{0:T(128)S(1)} %copy-done.3, bf16[128,1024]{1,0:T(8,128)(2,1)S(1)} %collective-permute-done.f0, bf16[128,1024]{1,0:T(8,128)(2,1)S(1)} %collective-permute-done.1.f1, ...), custom_call_target="tpu_custom_call" | custom-call | flops 2000000000 | bytes 1000 | tf_op jit(solution)/shard_map/pallas_call | solution.py:330
  33.1 0.0 collective-permute-done.3.g0
  33.1 1.4 %shard_map.60 = (bf16[4,4,64,256]{3,2,1,0:T(8,128)(2,1)S(1)}, bf16[2,4,4,256,128]{4,3,2,1,0:T(8,128)(2,1)S(1)}) custom-call(bf16[128,1024]{1,0:T(8,128)(2,1)S(1)} %collective-permute-done.3.g0, bf16[128,1024]{1,0:T(8,128)(2,1)S(1)} %collective-permute-done.5.g1, bf16[1024,3072]{1,0:T(8,128)(2,1)S(1)} %copy-done.1, bf16[1024,1024]{1,0:T(8,128)(2,1)S(1)} %get-tuple-element.40.wvt), custom_call_target="tpu_custom_call" | custom-call | flops 4000000000 | bytes 1000 | tf_op jit(solution)/shard_map/pallas_call | solution.py:330
  34.5 0.8 %collective-permute-done.7.g2 = bf16[128,1024]{1,0:T(8,128)(2,1)S(1)} collective-permute-done((bf16[128,1024]{1,0:T(8,128)(2,1)S(1)}, bf16[128,1024]{1,0:T(8,128)(2,1)S(1)}, u32[]{:S(2)}, u32[]{:S(2)}) %collective-permute-start.7) | collective-permute-done | bytes 262176 | tf_op jit(solution)/shard_map/ppermute | solution.py:356
  35.3 0.9 %shard_map.61 = bf16[512,1024]{1,0:T(8,128)(2,1)S(1)} custom-call(s32[6]{0:T(128)S(1)} %copy-done.3, bf16[128,1024]{1,0:T(8,128)(2,1)S(1)} %collective-permute-done.f0, bf16[128,1024]{1,0:T(8,128)(2,1)S(1)} %collective-permute-done.1.f1, bf16[128,1024]{1,0:T(8,128)(2,1)S(1)} %collective-permute-done.2.f2, bf16[128,1024]{1,0:T(8,128)(2,1)S(1)} %collective-permute-done.3.g0, ...), custom_call_target="tpu_custom_call" | custom-call | flops 2000000000 | bytes 1000 | tf_op jit(solution)/shard_map/pallas_call | solution.py:330
  36.2 0.1 collective-permute-start.8
  36.2 0.0 copy-start.2
  36.2 5.6 %shard_map.62 = (f32[24,1,256]{2,1,0:T(1,128)S(1)}, f32[24,1,256]{2,1,0:T(1,128)S(1)}, f32[24,64,256]{2,1,0:T(8,128)S(1)}) custom-call(s32[6,2]{1,0:T(8,128)S(1)} %copy.9.nbr, s32[6]{0:T(128)S(1)} %copy-done.3, bf16[128,1024]{1,0:T(8,128)(2,1)S(1)} %collective-permute-done.7.g2, bf16[1024,3072]{1,0:T(8,128)(2,1)S(1)} %copy-done.1, ...), custom_call_target="tpu_custom_call" | custom-call | flops 2000000000 | bytes 1000 | tf_op jit(solution)/shard_map/pallas_call | solution.py:330
  41.8 8.4 %shard_map.63 = bf16[2,192,1024]{2,1,0:T(8,128)(2,1)} custom-call(s32[6,2]{1,0:T(8,128)S(1)} %copy.9.nbr, s32[6]{0:T(128)S(1)} %copy-done.3, bf16[512,1024]{1,0:T(8,128)(2,1)S(1)} %collective-permute-done.8.e, bf16[1024,3072]{1,0:T(8,128)(2,1)S(1)} %copy-done.1, bf16[1024,1024]{1,0:T(8,128)(2,1)S(1)} %get-tuple-element.40.wvt, ...), custom_call_target="tpu_custom_call" | custom-call | flops 2000000000 | bytes 1000 | tf_op jit(solution)/shard_map/pallas_call | solution.py:330
  (14 shorter events, 0.0 us)
Async XLA Ops:
  0.0 4.4 %copy-start.3 = (s32[6]{0:T(128)S(1)}, s32[6]{0:T(128)}, u32[]{:S(2)}) copy-start(s32[6]{0:T(128)} %hw.9) | copy-start | bytes 76
  0.0 4.4 %collective-permute-start.4 = (bf16[2,192,1024]{2,1,0:T(8,128)(2,1)}, bf16[2,192,1024]{2,1,0:T(8,128)(2,1)S(1)}, u32[]{:S(2)}, u32[]{:S(2)}) collective-permute-start(bf16[2,192,1024]{2,1,0:T(8,128)(2,1)} %x.1), channel_id=1, source_target_pairs={{0,1},{1,0},{2,3},{3,2},{4,5},{5,4},{6,7},{7,6},{8,9},{9,8},{10,11... | collective-permute-start | bytes 2359304 | tf_op jit(solution)/shard_map/ppermute | solution.py:356
  1.7 9.8 %collective-permute-start = (bf16[128,1024]{1,0:T(8,128)(2,1)S(1)}, bf16[128,1024]{1,0:T(8,128)(2,1)S(1)}, u32[]{:S(2)}, u32[]{:S(2)}) collective-permute-start(bf16[128,1024]{1,0:T(8,128)(2,1)S(1)} %get-tuple-element.32.x0), channel_id=1, source_target_pairs={{0,2},{1,3},{2,0},{3,1},{4,6},{5,7},{6,4},{7,5},{8,10},{9,11},{10,... | collective-permute-start | bytes 786440 | tf_op jit(solution)/shard_map/ppermute | solution.py:356
  4.3 16.2 %collective-permute-start.1 = (bf16[128,1024]{1,0:T(8,128)(2,1)S(1)}, bf16[128,1024]{1,0:T(8,128)(2,1)S(1)}, u32[]{:S(2)}, u32[]{:S(2)}) collective-permute-start(bf16[128,1024]{1,0:T(8,128)(2,1)S(1)} %get-tuple-element.30.x1), channel_id=1, source_target_pairs={{0,2},{1,3},{2,0},{3,1},{4,6},{5,7},{6,4},{7,5},{8,10},{9,11},{10,... | collective-permute-start | bytes 786440 | tf_op jit(solution)/shard_map/ppermute | solution.py:356
  4.4 4.2 %copy-start.4 = (s32[6,2]{0,1:T(2,128)S(1)}, s32[6,2]{0,1:T(2,128)}, u32[]{:S(2)}) copy-start(s32[6,2]{0,1:T(2,128)} %param.9) | copy-start | bytes 148
  5.0 17.2 %collective-permute-start.6 = (bf16[128,1024]{1,0:T(8,128)(2,1)S(1)}, bf16[128,1024]{1,0:T(8,128)(2,1)S(1)}, u32[]{:S(2)}, u32[]{:S(2)}) collective-permute-start(bf16[128,1024]{1,0:T(8,128)(2,1)S(1)} %shard_map.57), channel_id=1, source_target_pairs={{0,4},{1,13},{2,6},{3,15},{4,8},{5,1},{6,10},{7,3},{8,12},{9,5},{1... | collective-permute-start | bytes 786440 | tf_op jit(solution)/shard_map/ppermute | solution.py:356
  7.1 18.1 %collective-permute-start.2 = (bf16[128,1024]{1,0:T(8,128)(2,1)S(1)}, bf16[128,1024]{1,0:T(8,128)(2,1)S(1)}, u32[]{:S(2)}, u32[]{:S(2)}) collective-permute-start(bf16[128,1024]{1,0:T(8,128)(2,1)S(1)} %get-tuple-element.31.x2), channel_id=1, source_target_pairs={{0,2},{1,3},{2,0},{3,1},{4,6},{5,7},{6,4},{7,5},{8,10},{9,11},{10,... | collective-permute-start | bytes 786440 | tf_op jit(solution)/shard_map/ppermute | solution.py:356
  11.5 21.6 %collective-permute-start.3 = (bf16[128,1024]{1,0:T(8,128)(2,1)S(1)}, bf16[128,1024]{1,0:T(8,128)(2,1)S(1)}, u32[]{:S(2)}, u32[]{:S(2)}) collective-permute-start(bf16[128,1024]{1,0:T(8,128)(2,1)S(1)} %collective-permute-done.f0), channel_id=1, source_target_pairs={{0,4},{1,5},{2,14},{3,15},{4,8},{5,9},{6,2},{7,3},{8,12},{9,13},{1... | collective-permute-start | bytes 786440 | tf_op jit(solution)/shard_map/ppermute | solution.py:356
  13.5 2.8 %copy-start = (bf16[1024,3072]{1,0:T(8,128)(2,1)S(1)}, bf16[1024,3072]{1,0:T(8,128)(2,1)}, u32[]{:S(2)}) copy-start(bf16[1024,3072]{1,0:T(8,128)(2,1)} %w.9) | copy-start | bytes 18874372
  20.6 12.6 %collective-permute-start.5 = (bf16[128,1024]{1,0:T(8,128)(2,1)S(1)}, bf16[128,1024]{1,0:T(8,128)(2,1)S(1)}, u32[]{:S(2)}, u32[]{:S(2)}) collective-permute-start(bf16[128,1024]{1,0:T(8,128)(2,1)S(1)} %collective-permute-done.1.f1), channel_id=1, source_target_pairs={{0,4},{1,5},{2,14},{3,15},{4,8},{5,9},{6,2},{7,3},{8,12},{9,13},{1... | collective-permute-start | bytes 786440 | tf_op jit(solution)/shard_map/ppermute | solution.py:356
  22.2 4.7 %copy-start.1 = (bf16[1024,3072]{1,0:T(8,128)(2,1)S(1)}, bf16[1024,3072]{1,0:T(8,128)(2,1)}, u32[]{:S(2)}) copy-start(bf16[1024,3072]{1,0:T(8,128)(2,1)} %w.9) | copy-start | bytes 18874372
  25.1 10.2 %collective-permute-start.7 = (bf16[128,1024]{1,0:T(8,128)(2,1)S(1)}, bf16[128,1024]{1,0:T(8,128)(2,1)S(1)}, u32[]{:S(2)}, u32[]{:S(2)}) collective-permute-start(bf16[128,1024]{1,0:T(8,128)(2,1)S(1)} %collective-permute-done.2.f2), channel_id=1, source_target_pairs={{0,4},{1,5},{2,14},{3,15},{4,8},{5,9},{6,2},{7,3},{8,12},{9,13},{1... | collective-permute-start | bytes 786440 | tf_op jit(solution)/shard_map/ppermute | solution.py:356
  36.2 5.7 %collective-permute-start.8 = (bf16[512,1024]{1,0:T(8,128)(2,1)S(1)}, bf16[512,1024]{1,0:T(8,128)(2,1)S(1)}, u32[]{:S(2)}, u32[]{:S(2)}) collective-permute-start(bf16[512,1024]{1,0:T(8,128)(2,1)S(1)} %shard_map.61), channel_id=1, source_target_pairs={{0,1},{1,0},{2,3},{3,2},{4,5},{5,4},{6,7},{7,6},{8,9},{9,8},{10,11... | collective-permute-start | bytes 3145736 | tf_op jit(solution)/shard_map/ppermute | solution.py:356
  36.2 5.6 %copy-start.2 = (bf16[1024,1024]{1,0:T(8,128)(2,1)S(1)}, bf16[1024,1024]{1,0:T(8,128)(2,1)}, u32[]{:S(2)}) copy-start(bf16[1024,1024]{1,0:T(8,128)(2,1)} %wout.1) | copy-start | bytes 6291460

commit v5 on v4

--- a/solution.py
+++ b/solution.py
@@ -16,7 +16,7 @@
 BF16 = jnp.bfloat16
 F32 = jnp.float32
 SCALE = math.log2(math.e) / math.sqrt(HEAD)
-VMEM_LIMIT = 28 * 1024 * 1024
+MIB = 1024 * 1024
 COST = 2000000000
 EARLY_COST = 4000000000
 NEAR_COST = 2000000000
@@ -178,8 +178,12 @@
 def project_far(tokens, w, wvt, keys, vals, wkeys, wvals):
     nlb, groups, rows, _ = keys.shape
     width = tokens.shape[1]
+    ks = [
+        dot(tokens[...], w[:, width + g * WIDE : width + (g + 1) * WIDE]).astype(BF16)
+        for g in range(groups)
+    ]
     for g in range(groups):
-        k = dot(tokens[...], w[:, width + g * WIDE : width + (g + 1) * WIDE]).astype(BF16)
+        k = ks[g]
         parts, rest = project_values(wvt, tokens[...], g, nlb, rows)
         for c in range(nlb):
             keys[c, g] = k[c * rows : (c + 1) * rows, :]
@@ -190,7 +194,7 @@
             wvals[g] = rest
 
 
-def attend_far(nbr, seen, wide, qc, pick_keys, pick_vals, wkeys, wvals, before, finish):
+def attend_far(nbr, seen, wide, qc, keys, vals, wkeys, wvals, before, finish):
     nlb = nbr.shape[0]
     groups = qc.shape[0] // nlb
     for b in range(nlb):
@@ -198,41 +202,24 @@
         for g in range(groups):
             t = b * groups + g
             q = spread(qc[t])
-            ks = [pick_keys(c0, g), pick_keys(c1, g)]
+            ks = [keys[c0, g], keys[c1, g]]
             rows = ks[0].shape[0]
-            v = pick_vals(0, c0, g) + pick_vals(1, c1, g)
+            v = vals[0, c0, g] + vals[1, c1, g]
+            if wkeys is None:
+                ks = ks + ks
             if wkeys is not None:
                 ks.append(wkeys[g])
                 v = jnp.concatenate([v, wvals[g]], axis=1)
             scores = dot(jnp.concatenate(ks, axis=0), q)
             pieces = [scores[:rows], scores[rows : 2 * rows]]
             if seen is not None:
-                pieces[0] = jnp.where(seen[c0] >= 2, pieces[0], NEVER)
-                pieces[1] = jnp.where(seen[c1] >= 2, pieces[1], NEVER)
+                pieces[0] += jnp.where(seen[c0] >= 2, 0.0, NEVER)
+                pieces[1] += jnp.where(seen[c1] >= 2, 0.0, NEVER)
             if wkeys is not None:
                 member = (c0 == wide) | (c1 == wide)
-                pieces.append(jnp.where(member, scores[2 * rows :], NEVER))
+                pieces.append(scores[2 * rows :] + jnp.where(member, 0.0, NEVER))
             scores = jnp.concatenate(pieces, axis=0)
             finish(b, g, *update(scores, v, tuple(r[t] for r in before)))
-
-
-def from_one(keys, vals):
-    return (lambda c, g: keys[c, g]), (lambda side, c, g: vals[side, c, g])
-
-
-def from_two(keys, vals, more_keys, more_vals):
-    first = keys.shape[0]
-
-    def pick_keys(c, g):
-        here, there = keys[jnp.minimum(c, first - 1), g], more_keys[jnp.maximum(c - first, 0), g]
-        return jnp.where(c < first, here, there)
-
-    def pick_vals(side, c, g):
-        here = vals[side, jnp.minimum(c, first - 1), g]
-        there = more_vals[side, jnp.maximum(c - first, 0), g]
-        return jnp.where(c < first, here, there)
-
-    return pick_keys, pick_vals
 
 
 def keep(m, l, acc, groups):
@@ -250,7 +237,7 @@
         tokens[at : at + part.shape[0], :] = part[...]
         at += part.shape[0]
     project_far(tokens, w, wvt, keys, vals, wkeys, wvals)
-    attend_far(nbr, hw, widest_of(hw), qc, *from_one(keys, vals), wkeys, wvals, (m_in, l_in, acc_in), keep(m, l, acc, keys.shape[1]))
+    attend_far(nbr, hw, widest_of(hw), qc, keys, vals, wkeys, wvals, (m_in, l_in, acc_in), keep(m, l, acc, keys.shape[1]))
 
 
 def early_kernel(g0, g1, w, wvt, keys, vals, tokens):
@@ -260,10 +247,12 @@
 
 
 def onward_kernel(nbr, hw, g2, w, wvt, qc, early_keys, early_vals, m_in, l_in, acc_in, m, l, acc, keys, vals):
-    project_far(g2, w, wvt, keys, vals, None, None)
-    picks = from_two(early_keys, early_vals, keys, vals)
+    early = early_keys.shape[0]
+    keys[:early] = early_keys[...]
+    vals[:, :early] = early_vals[...]
+    project_far(g2, w, wvt, keys.at[early:], vals.at[:, early:], None, None)
     store = keep(m, l, acc, keys.shape[1])
-    attend_far(nbr, hw, None, qc, *picks, None, None, (m_in, l_in, acc_in), store)
+    attend_far(nbr, hw, None, qc, keys, vals, None, None, (m_in, l_in, acc_in), store)
 
 
 def payload_kernel(hw, f0, f1, f2, g0, g1, g2, bands, out):
@@ -308,7 +297,7 @@
         ).astype(BF16)
 
     project_far(e, w, wvt, keys, vals, wkeys, wvals)
-    attend_far(nbr, None, widest_of(hw), qc, *from_one(keys, vals), wkeys, wvals, (m_in, l_in, acc_in), store)
+    attend_far(nbr, None, widest_of(hw), qc, keys, vals, wkeys, wvals, (m_in, l_in, acc_in), store)
     for g in range(groups):
         r = dot(attended[...], wout[:, g * WIDE : (g + 1) * WIDE]).astype(BF16)
         for b in range(nlb):
@@ -317,7 +306,7 @@
                 out[o, b * span : (b + 1) * span, g * WIDE : (g + 1) * WIDE] = r[at : at + span, :]
 
 
-def call(kernel, scalars, arrays, outs, scratch, unread=0, cost=COST):
+def call(kernel, scalars, arrays, outs, scratch, unread=0, cost=COST, room=22):
     smem = pl.BlockSpec(memory_space=pltpu.SMEM)
     vmem = pl.BlockSpec(memory_space=pltpu.VMEM)
     single = not isinstance(outs, (list, tuple))
@@ -333,7 +322,7 @@
         in_specs=[smem] * len(scalars) + specs,
         out_specs=vmem if single else [vmem] * len(outs),
         scratch_shapes=scratch,
-        compiler_params=pltpu.CompilerParams(vmem_limit_bytes=VMEM_LIMIT),
+        compiler_params=pltpu.CompilerParams(vmem_limit_bytes=room * MIB),
         cost_estimate=pl.CostEstimate(flops=cost, bytes_accessed=1000, transcendentals=0),
     )(*scalars, *arrays)
 
@@ -384,11 +373,17 @@
     beside = permute(tokens, sibling)
     chunk = jax.ShapeDtypeStruct((nlb * rows // CHUNKS, width), BF16)
     parts = call(
-        prepare_kernel, (), (tokens,), [chunk] * CHUNKS, [pltpu.SemaphoreType.DMA((nlb * lon,))], unread=1
+        prepare_kernel,
+        (),
+        (tokens,),
+        [chunk] * CHUNKS,
+        [pltpu.SemaphoreType.DMA((nlb * lon,))],
+        unread=1,
+        room=4,
     )
     f = [permute(part, across) for part in parts]
     bands = call(
-        band_kernel, (half_width,), (*parts, beside), jax.ShapeDtypeStruct((2 * rows, width), BF16), []
+        band_kernel, (half_width,), (*parts, beside), jax.ShapeDtypeStruct((2 * rows, width), BF16), [], room=4
     )
     bands = permute(bands, outward)
     g0 = permute(f[0], onward)
@@ -413,6 +408,7 @@
         carried_shapes,
         [],
         cost=NEAR_COST,
+        room=12,
     )
     g2 = permute(after(f[2], m), onward)
     m, l, acc = call(
@@ -434,6 +430,7 @@
         ],
         [pltpu.VMEM((early * rows, width), BF16)],
         cost=EARLY_COST,
+        room=16,
     )
     e = call(
         payload_kernel,
@@ -441,6 +438,7 @@
         (*f, g0, g1, g2, after(bands, early_keys)),
         jax.ShapeDtypeStruct(((nlb + 2) * rows, width), BF16),
         [],
+        room=6,
     )
     e = permute(e, sibling)
     m, l, acc = call(
@@ -449,8 +447,8 @@
         (g2, projection, wvt, qc, early_keys, early_vals, m, l, acc),
         carried_shapes,
         [
-            pltpu.VMEM((nlb - early, groups, rows, WIDE), BF16),
-            pltpu.VMEM((2, nlb - early, groups, WIDE, 2 * rows), BF16),
+            key_scratch,
+            val_scratch,
         ],
     )
     return call(

time: 50.5 us -> 48.4 us (0.958)
  Pallas kernels: 31.4 us -> 29.3 us
    pallas_call x9, Pallas kernels: 31.4 us -> 29.3 us  [call(): pl.pallas_call(kernel, out_shape=outs, in_specs=[smem] * len(scalars) + s...]
  transfers between devices with their start and end apart: 9 -> 9, of which waited for: 2 -> 2; matrix products, arithmetic and copies ran while one was open for 0% -> 0% of each run, Pallas kernels for 44% -> 42%
where the time goes in v5:
time: 48.4 us; the launch traced here: 48.2 us
  Pallas kernels  29.3 us (61%)
  starting transfers between devices  12.2 us (25%)
  waiting for transfers between devices  3.68 us (8%)
  local copies, waits for them, and re-layouts  2.89 us (6%)
    pallas_call x9, Pallas kernels, call(): pl.pallas_call(kernel, out_shape=outs, in_specs=[smem] * len(scalars) + s...  29.3 us
    ppermute x9, starting transfers between devices, permute(): return lax.ppermute(block, 'lon', [(i, step(i) % count) for i in devices])  12.2 us
    ppermute x9, waiting for transfers between devices, permute(): return lax.ppermute(block, 'lon', [(i, step(i) % count) for i in devices])  3.68 us
    unnamed x11, local copies, waits for them, and re-layouts  2.89 us
  transfers between devices with their start and end apart: 9, of which 2 were waited for; matrix products, arithmetic and copies ran while one was open for 0% of the time, Pallas kernels for 42%

profile of v5, /device:TPU:0, one launch (start us, length us, event | category | flops | bytes accessed | tf_op | source)
XLA Modules:
  0.0 48.2 jit_solution(243151764120102226)
XLA Ops:
  0.0 0.5 collective-permute-start.4
  0.5 1.3 %shard_map.55 = (bf16[128,1024]{1,0:T(8,128)(2,1)S(1)}, bf16[128,1024]{1,0:T(8,128)(2,1)S(1)}, bf16[128,1024]{1,0:T(8,128)(2,1)S(1)}) custom-call(bf16[2,192,1024]{2,1,0:T(8,128)(2,1)} %x.1), custom_call_target="tpu_custom_call" | custom-call | flops 2000000000 | bytes 1000 | tf_op jit(solution)/shard_map/pallas_call | solution.py:319
  1.7 2.6 %collective-permute-start = (bf16[128,1024]{1,0:T(8,128)(2,1)S(1)}, bf16[128,1024]{1,0:T(8,128)(2,1)S(1)}, u32[]{:S(2)}, u32[]{:S(2)}) collective-permute-start(bf16[128,1024]{1,0:T(8,128)(2,1)S(1)} %get-tuple-element.32.x0), channel_id=1, source_target_pairs={{0,2},{1,3},{2,0},{3,1},{4,6},{5,7},{6,4},{7,5},{8,10},{9,11},{10,... | collective-permute-start | bytes 786440 | tf_op jit(solution)/shard_map/ppermute | solution.py:345
  4.3 0.1 collective-permute-start.1
  4.4 0.6 %shard_map.57 = bf16[128,1024]{1,0:T(8,128)(2,1)S(1)} custom-call(s32[6]{0:T(128)S(1)} %copy-done.3, bf16[128,1024]{1,0:T(8,128)(2,1)S(1)} %get-tuple-element.32.x0, bf16[128,1024]{1,0:T(8,128)(2,1)S(1)} %get-tuple-element.30.x1, bf16[128,1024]{1,0:T(8,128)(2,1)S(1)} %get-tuple-element.31.x2, bf16[2,192,1024]{2,1,0:T(8,128)(2,1)S(1)} %collective-permute-done.4.s), custom_call_target="tpu_custom_call" | custom-call | flops 2000000000 | bytes 1000 | tf_op jit(solution)/shard_map/pallas_call | solution.py:319
  5.0 2.1 %collective-permute-start.6 = (bf16[128,1024]{1,0:T(8,128)(2,1)S(1)}, bf16[128,1024]{1,0:T(8,128)(2,1)S(1)}, u32[]{:S(2)}, u32[]{:S(2)}) collective-permute-start(bf16[128,1024]{1,0:T(8,128)(2,1)S(1)} %shard_map.57), channel_id=1, source_target_pairs={{0,4},{1,13},{2,6},{3,15},{4,8},{5,1},{6,10},{7,3},{8,12},{9,5},{1... | collective-permute-start | bytes 786440 | tf_op jit(solution)/shard_map/ppermute | solution.py:345
  7.1 1.5 %collective-permute-start.2 = (bf16[128,1024]{1,0:T(8,128)(2,1)S(1)}, bf16[128,1024]{1,0:T(8,128)(2,1)S(1)}, u32[]{:S(2)}, u32[]{:S(2)}) collective-permute-start(bf16[128,1024]{1,0:T(8,128)(2,1)S(1)} %get-tuple-element.31.x2), channel_id=1, source_target_pairs={{0,2},{1,3},{2,0},{3,1},{4,6},{5,7},{6,4},{7,5},{8,10},{9,11},{10,... | collective-permute-start | bytes 786440 | tf_op jit(solution)/shard_map/ppermute | solution.py:345
  8.6 0.1 copy.9.nbr
  8.7 2.8 %collective-permute-done.f0 = bf16[128,1024]{1,0:T(8,128)(2,1)S(1)} collective-permute-done((bf16[128,1024]{1,0:T(8,128)(2,1)S(1)}, bf16[128,1024]{1,0:T(8,128)(2,1)S(1)}, u32[]{:S(2)}, u32[]{:S(2)}) %collective-permute-start) | collective-permute-done | bytes 262176 | tf_op jit(solution)/shard_map/ppermute | solution.py:345
  11.5 2.0 %collective-permute-start.3 = (bf16[128,1024]{1,0:T(8,128)(2,1)S(1)}, bf16[128,1024]{1,0:T(8,128)(2,1)S(1)}, u32[]{:S(2)}, u32[]{:S(2)}) collective-permute-start(bf16[128,1024]{1,0:T(8,128)(2,1)S(1)} %collective-permute-done.f0), channel_id=1, source_target_pairs={{0,4},{1,5},{2,14},{3,15},{4,8},{5,9},{6,2},{7,3},{8,12},{9,13},{1... | collective-permute-start | bytes 786440 | tf_op jit(solution)/shard_map/ppermute | solution.py:345
  13.5 2.8 %copy-done = bf16[1024,3072]{1,0:T(8,128)(2,1)S(1)} copy-done((bf16[1024,3072]{1,0:T(8,128)(2,1)S(1)}, bf16[1024,3072]{1,0:T(8,128)(2,1)}, u32[]{:S(2)}) %copy-start) | copy-done | bytes 6291480
  16.3 4.3 %shard_map.56 = (bf16[24,64,256]{2,1,0:T(8,128)(2,1)S(1)}, bf16[6,4,128,256]{3,2,1,0:T(8,128)(2,1)S(1)}, bf16[6,4,256,128]{3,2,1,0:T(8,128)(2,1)S(1)}, bf16[1024,1024]{1,0:T(8,128)(2,1)S(1)}) custom-call(bf16[128,1024]{1,0:T(8,128)(2,1)S(1)} %get-tuple-element.32.x0, bf16[128,1024]{1,0:T(8,128)(2,1)S(1)} %get-tuple-element.30.x1, ...), custom_call_target="tpu_custom_call" | custom-call | flops 2000000000 | bytes 1000 | tf_op jit(solution)/shard_map/pallas_call | solution.py:319
  20.6 1.6 %collective-permute-start.5 = (bf16[128,1024]{1,0:T(8,128)(2,1)S(1)}, bf16[128,1024]{1,0:T(8,128)(2,1)S(1)}, u32[]{:S(2)}, u32[]{:S(2)}) collective-permute-start(bf16[128,1024]{1,0:T(8,128)(2,1)S(1)} %collective-permute-done.1.f1), channel_id=1, source_target_pairs={{0,4},{1,5},{2,14},{3,15},{4,8},{5,9},{6,2},{7,3},{8,12},{9,13},{1... | collective-permute-start | bytes 786440 | tf_op jit(solution)/shard_map/ppermute | solution.py:345
  22.2 2.9 %shard_map.58 = (f32[24,1,256]{2,1,0:T(1,128)S(1)}, f32[24,1,256]{2,1,0:T(1,128)S(1)}, f32[24,64,256]{2,1,0:T(8,128)S(1)}) custom-call(s32[6,2]{1,0:T(8,128)S(1)} %copy.9.nbr, bf16[24,64,256]{2,1,0:T(8,128)(2,1)S(1)} %get-tuple-element.35.qc, bf16[6,4,128,256]{3,2,1,0:T(8,128)(2,1)S(1)} %get-tuple-element.36.keys, ...), custom_call_target="tpu_custom_call" | custom-call | flops 2000000000 | bytes 1000 | tf_op jit(solution)/shard_map/pallas_call | solution.py:319
  25.1 1.8 %collective-permute-start.7 = (bf16[128,1024]{1,0:T(8,128)(2,1)S(1)}, bf16[128,1024]{1,0:T(8,128)(2,1)S(1)}, u32[]{:S(2)}, u32[]{:S(2)}) collective-permute-start(bf16[128,1024]{1,0:T(8,128)(2,1)S(1)} %collective-permute-done.2.f2), channel_id=1, source_target_pairs={{0,4},{1,5},{2,14},{3,15},{4,8},{5,9},{6,2},{7,3},{8,12},{9,13},{1... | collective-permute-start | bytes 786440 | tf_op jit(solution)/shard_map/ppermute | solution.py:345
  26.9 6.1 %shard_map.59 = (f32[24,1,256]{2,1,0:T(1,128)S(1)}, f32[24,1,256]{2,1,0:T(1,128)S(1)}, f32[24,64,256]{2,1,0:T(8,128)S(1)}) custom-call(s32[6,2]{1,0:T(8,128)S(1)} %copy.9.nbr, s32[6]{0:T(128)S(1)} %copy-done.3, bf16[128,1024]{1,0:T(8,128)(2,1)S(1)} %collective-permute-done.f0, bf16[128,1024]{1,0:T(8,128)(2,1)S(1)} %collective-permute-done.1.f1, ...), custom_call_target="tpu_custom_call" | custom-call | flops 2000000000 | bytes 1000 | tf_op jit(solution)/shard_map/pallas_call | solution.py:319
  33.0 1.4 %shard_map.60 = (bf16[4,4,64,256]{3,2,1,0:T(8,128)(2,1)S(1)}, bf16[2,4,4,256,128]{4,3,2,1,0:T(8,128)(2,1)S(1)}) custom-call(bf16[128,1024]{1,0:T(8,128)(2,1)S(1)} %collective-permute-done.3.g0, bf16[128,1024]{1,0:T(8,128)(2,1)S(1)} %collective-permute-done.5.g1, bf16[1024,3072]{1,0:T(8,128)(2,1)S(1)} %copy-done.1, bf16[1024,1024]{1,0:T(8,128)(2,1)S(1)} %get-tuple-element.40.wvt), custom_call_target="tpu_custom_call" | custom-call | flops 4000000000 | bytes 1000 | tf_op jit(solution)/shard_map/pallas_call | solution.py:319
  34.4 0.9 %collective-permute-done.7.g2 = bf16[128,1024]{1,0:T(8,128)(2,1)S(1)} collective-permute-done((bf16[128,1024]{1,0:T(8,128)(2,1)S(1)}, bf16[128,1024]{1,0:T(8,128)(2,1)S(1)}, u32[]{:S(2)}, u32[]{:S(2)}) %collective-permute-start.7) | collective-permute-done | bytes 262176 | tf_op jit(solution)/shard_map/ppermute | solution.py:345
  35.3 0.9 %shard_map.61 = bf16[512,1024]{1,0:T(8,128)(2,1)S(1)} custom-call(s32[6]{0:T(128)S(1)} %copy-done.3, bf16[128,1024]{1,0:T(8,128)(2,1)S(1)} %collective-permute-done.f0, bf16[128,1024]{1,0:T(8,128)(2,1)S(1)} %collective-permute-done.1.f1, bf16[128,1024]{1,0:T(8,128)(2,1)S(1)} %collective-permute-done.2.f2, bf16[128,1024]{1,0:T(8,128)(2,1)S(1)} %collective-permute-done.3.g0, ...), custom_call_target="tpu_custom_call" | custom-call | flops 2000000000 | bytes 1000 | tf_op jit(solution)/shard_map/pallas_call | solution.py:319
  36.2 0.1 collective-permute-start.8
  36.2 0.0 copy-start.2
  36.2 3.7 %shard_map.62 = (f32[24,1,256]{2,1,0:T(1,128)S(1)}, f32[24,1,256]{2,1,0:T(1,128)S(1)}, f32[24,64,256]{2,1,0:T(8,128)S(1)}) custom-call(s32[6,2]{1,0:T(8,128)S(1)} %copy.9.nbr, s32[6]{0:T(128)S(1)} %copy-done.3, bf16[128,1024]{1,0:T(8,128)(2,1)S(1)} %collective-permute-done.7.g2, bf16[1024,3072]{1,0:T(8,128)(2,1)S(1)} %copy-done.1, ...), custom_call_target="tpu_custom_call" | custom-call | flops 2000000000 | bytes 1000 | tf_op jit(solution)/shard_map/pallas_call | solution.py:319
  39.9 0.0 collective-permute-done.8.e
  40.0 8.2 %shard_map.63 = bf16[2,192,1024]{2,1,0:T(8,128)(2,1)} custom-call(s32[6,2]{1,0:T(8,128)S(1)} %copy.9.nbr, s32[6]{0:T(128)S(1)} %copy-done.3, bf16[512,1024]{1,0:T(8,128)(2,1)S(1)} %collective-permute-done.8.e, bf16[1024,3072]{1,0:T(8,128)(2,1)S(1)} %copy-done.1, bf16[1024,1024]{1,0:T(8,128)(2,1)S(1)} %get-tuple-element.40.wvt, ...), custom_call_target="tpu_custom_call" | custom-call | flops 2000000000 | bytes 1000 | tf_op jit(solution)/shard_map/pallas_call | solution.py:319
  (14 shorter events, 0.0 us)
Async XLA Ops:
  0.0 4.4 %copy-start.3 = (s32[6]{0:T(128)S(1)}, s32[6]{0:T(128)}, u32[]{:S(2)}) copy-start(s32[6]{0:T(128)} %hw.9) | copy-start | bytes 76
  0.0 4.4 %collective-permute-start.4 = (bf16[2,192,1024]{2,1,0:T(8,128)(2,1)}, bf16[2,192,1024]{2,1,0:T(8,128)(2,1)S(1)}, u32[]{:S(2)}, u32[]{:S(2)}) collective-permute-start(bf16[2,192,1024]{2,1,0:T(8,128)(2,1)} %x.1), channel_id=1, source_target_pairs={{0,1},{1,0},{2,3},{3,2},{4,5},{5,4},{6,7},{7,6},{8,9},{9,8},{10,11... | collective-permute-start | bytes 2359304 | tf_op jit(solution)/shard_map/ppermute | solution.py:345
  1.7 9.8 %collective-permute-start = (bf16[128,1024]{1,0:T(8,128)(2,1)S(1)}, bf16[128,1024]{1,0:T(8,128)(2,1)S(1)}, u32[]{:S(2)}, u32[]{:S(2)}) collective-permute-start(bf16[128,1024]{1,0:T(8,128)(2,1)S(1)} %get-tuple-element.32.x0), channel_id=1, source_target_pairs={{0,2},{1,3},{2,0},{3,1},{4,6},{5,7},{6,4},{7,5},{8,10},{9,11},{10,... | collective-permute-start | bytes 786440 | tf_op jit(solution)/shard_map/ppermute | solution.py:345
  4.3 16.2 %collective-permute-start.1 = (bf16[128,1024]{1,0:T(8,128)(2,1)S(1)}, bf16[128,1024]{1,0:T(8,128)(2,1)S(1)}, u32[]{:S(2)}, u32[]{:S(2)}) collective-permute-start(bf16[128,1024]{1,0:T(8,128)(2,1)S(1)} %get-tuple-element.30.x1), channel_id=1, source_target_pairs={{0,2},{1,3},{2,0},{3,1},{4,6},{5,7},{6,4},{7,5},{8,10},{9,11},{10,... | collective-permute-start | bytes 786440 | tf_op jit(solution)/shard_map/ppermute | solution.py:345
  4.4 4.2 %copy-start.4 = (s32[6,2]{0,1:T(2,128)S(1)}, s32[6,2]{0,1:T(2,128)}, u32[]{:S(2)}) copy-start(s32[6,2]{0,1:T(2,128)} %param.9) | copy-start | bytes 148
  5.0 17.2 %collective-permute-start.6 = (bf16[128,1024]{1,0:T(8,128)(2,1)S(1)}, bf16[128,1024]{1,0:T(8,128)(2,1)S(1)}, u32[]{:S(2)}, u32[]{:S(2)}) collective-permute-start(bf16[128,1024]{1,0:T(8,128)(2,1)S(1)} %shard_map.57), channel_id=1, source_target_pairs={{0,4},{1,13},{2,6},{3,15},{4,8},{5,1},{6,10},{7,3},{8,12},{9,5},{1... | collective-permute-start | bytes 786440 | tf_op jit(solution)/shard_map/ppermute | solution.py:345
  7.1 18.1 %collective-permute-start.2 = (bf16[128,1024]{1,0:T(8,128)(2,1)S(1)}, bf16[128,1024]{1,0:T(8,128)(2,1)S(1)}, u32[]{:S(2)}, u32[]{:S(2)}) collective-permute-start(bf16[128,1024]{1,0:T(8,128)(2,1)S(1)} %get-tuple-element.31.x2), channel_id=1, source_target_pairs={{0,2},{1,3},{2,0},{3,1},{4,6},{5,7},{6,4},{7,5},{8,10},{9,11},{10,... | collective-permute-start | bytes 786440 | tf_op jit(solution)/shard_map/ppermute | solution.py:345
  11.5 21.6 %collective-permute-start.3 = (bf16[128,1024]{1,0:T(8,128)(2,1)S(1)}, bf16[128,1024]{1,0:T(8,128)(2,1)S(1)}, u32[]{:S(2)}, u32[]{:S(2)}) collective-permute-start(bf16[128,1024]{1,0:T(8,128)(2,1)S(1)} %collective-permute-done.f0), channel_id=1, source_target_pairs={{0,4},{1,5},{2,14},{3,15},{4,8},{5,9},{6,2},{7,3},{8,12},{9,13},{1... | collective-permute-start | bytes 786440 | tf_op jit(solution)/shard_map/ppermute | solution.py:345
  13.5 2.8 %copy-start = (bf16[1024,3072]{1,0:T(8,128)(2,1)S(1)}, bf16[1024,3072]{1,0:T(8,128)(2,1)}, u32[]{:S(2)}) copy-start(bf16[1024,3072]{1,0:T(8,128)(2,1)} %w.9) | copy-start | bytes 18874372
  20.6 12.5 %collective-permute-start.5 = (bf16[128,1024]{1,0:T(8,128)(2,1)S(1)}, bf16[128,1024]{1,0:T(8,128)(2,1)S(1)}, u32[]{:S(2)}, u32[]{:S(2)}) collective-permute-start(bf16[128,1024]{1,0:T(8,128)(2,1)S(1)} %collective-permute-done.1.f1), channel_id=1, source_target_pairs={{0,4},{1,5},{2,14},{3,15},{4,8},{5,9},{6,2},{7,3},{8,12},{9,13},{1... | collective-permute-start | bytes 786440 | tf_op jit(solution)/shard_map/ppermute | solution.py:345
  22.2 4.7 %copy-start.1 = (bf16[1024,3072]{1,0:T(8,128)(2,1)S(1)}, bf16[1024,3072]{1,0:T(8,128)(2,1)}, u32[]{:S(2)}) copy-start(bf16[1024,3072]{1,0:T(8,128)(2,1)} %w.9) | copy-start | bytes 18874372
  25.1 10.2 %collective-permute-start.7 = (bf16[128,1024]{1,0:T(8,128)(2,1)S(1)}, bf16[128,1024]{1,0:T(8,128)(2,1)S(1)}, u32[]{:S(2)}, u32[]{:S(2)}) collective-permute-start(bf16[128,1024]{1,0:T(8,128)(2,1)S(1)} %collective-permute-done.2.f2), channel_id=1, source_target_pairs={{0,4},{1,5},{2,14},{3,15},{4,8},{5,9},{6,2},{7,3},{8,12},{9,13},{1... | collective-permute-start | bytes 786440 | tf_op jit(solution)/shard_map/ppermute | solution.py:345
  36.2 3.8 %collective-permute-start.8 = (bf16[512,1024]{1,0:T(8,128)(2,1)S(1)}, bf16[512,1024]{1,0:T(8,128)(2,1)S(1)}, u32[]{:S(2)}, u32[]{:S(2)}) collective-permute-start(bf16[512,1024]{1,0:T(8,128)(2,1)S(1)} %shard_map.61), channel_id=1, source_target_pairs={{0,1},{1,0},{2,3},{3,2},{4,5},{5,4},{6,7},{7,6},{8,9},{9,8},{10,11... | collective-permute-start | bytes 3145736 | tf_op jit(solution)/shard_map/ppermute | solution.py:345
  36.2 3.7 %copy-start.2 = (bf16[1024,1024]{1,0:T(8,128)(2,1)S(1)}, bf16[1024,1024]{1,0:T(8,128)(2,1)}, u32[]{:S(2)}) copy-start(bf16[1024,1024]{1,0:T(8,128)(2,1)} %wout.1) | copy-start | bytes 6291460

commit v6 on v5

--- a/solution.py
+++ b/solution.py
@@ -18,7 +18,7 @@
 SCALE = math.log2(math.e) / math.sqrt(HEAD)
 MIB = 1024 * 1024
 COST = 2000000000
-EARLY_COST = 4000000000
+EARLY_COST = 2000000000
 NEAR_COST = 2000000000
 ACROSS_COST = 2000000000
 
@@ -126,35 +126,63 @@
                 bands[rows + o * span : rows + (o + 1) * span, :] = s[o, c * span : (c + 1) * span, :]
 
 
-def own_kernel(x0, x1, x2, s, w, qc, keys, vals, wvt, own, both):
+def query_kernel(x0, x1, x2, w, qc, wvt, own, wq, wv, turned, sems):
+    width = wq.shape[0]
+    groups = width // WIDE
+    blocks = qc.shape[0] // groups
+    rows = own.shape[0] // blocks
+    fetch_v = pltpu.make_async_copy(w.at[:, pl.ds(2 * width, width)], wv, sems.at[0])
+    fetch_q = pltpu.make_async_copy(w.at[:, pl.ds(0, width)], wq, sems.at[1])
+    fetch_v.start()
+    fetch_q.start()
+    at = 0
+    for part in (x0, x1, x2):
+        own[at : at + part.shape[0], :] = part[...]
+        at += part.shape[0]
+    tiles = [slice(g * WIDE, (g + 1) * WIDE) for g in range(groups)]
+    fetch_v.wait()
+    for columns in tiles:
+        turned[columns, :] = wv[:, columns].T
+    put_back = pltpu.make_async_copy(turned, wvt, sems.at[2])
+    put_back.start()
+    fetch_q.wait()
+    for g, columns in enumerate(tiles):
+        q = dot(own[...], wq[:, columns]).astype(BF16).astype(F32)
+        for b in range(blocks):
+            qt = q[b * rows : (b + 1) * rows, :].T
+            qc[b * groups + g] = jnp.concatenate(
+                [qt[h * HEAD : (h + 1) * HEAD, :] for h in range(PACK)], axis=1
+            ).astype(BF16)
+    put_back.wait()
+
+
+def own_kernel(x0, x1, x2, s, w, far_wvt, keys, vals, wk, wvt, both, sems):
     lon, _, width = s.shape
     nlb, groups, rows, _ = keys.shape
     rows //= 2
     span = rows // lon
+    fetch_k = pltpu.make_async_copy(w.at[:, pl.ds(width, width)], wk, sems.at[0])
+    fetch_v = pltpu.make_async_copy(far_wvt, wvt, sems.at[1])
+    fetch_k.start()
     at = 0
     for part in (x0, x1, x2):
         for c in range(part.shape[0] // rows):
-            block = part[c * rows : (c + 1) * rows, :]
-            own[at : at + rows, :] = block
-            both[2 * at : 2 * at + rows, :] = block
+            both[2 * at : 2 * at + rows, :] = part[c * rows : (c + 1) * rows, :]
             at += rows
     for c in range(nlb):
         for o in range(lon):
             at = (2 * c + 1) * rows + o * span
             both[at : at + span, :] = s[o, c * span : (c + 1) * span, :]
-    for g in range(groups):
-        k = dot(both[...], w[:, width + g * WIDE : width + (g + 1) * WIDE]).astype(BF16)
+    tiles = [slice(g * WIDE, (g + 1) * WIDE) for g in range(groups)]
+    fetch_k.wait()
+    fetch_v.start()
+    for g, columns in enumerate(tiles):
+        k = dot(both[...], wk[:, columns]).astype(BF16)
         for c in range(nlb):
             keys[c, g] = k[2 * c * rows : 2 * (c + 1) * rows, :]
-        q = dot(own[...], w[:, g * WIDE : (g + 1) * WIDE]).astype(BF16).astype(F32)
-        for b in range(nlb):
-            qt = q[b * rows : (b + 1) * rows, :].T
-            qc[b * groups + g] = jnp.concatenate(
-                [qt[h * HEAD : (h + 1) * HEAD, :] for h in range(PACK)], axis=1
-            ).astype(BF16)
-        at = 2 * width + g * WIDE
-        wvt[g * WIDE : (g + 1) * WIDE, :] = w[:, at : at + WIDE].T
-        v = dot_nt(wvt[g * WIDE : (g + 1) * WIDE, :], both[...]).astype(BF16)
+    fetch_v.wait()
+    for g, columns in enumerate(tiles):
+        v = dot_nt(wvt[columns, :], both[...]).astype(BF16)
         for c in range(nlb):
             vals[c, g] = v[:, 2 * c * rows : 2 * (c + 1) * rows]
 
@@ -177,9 +205,8 @@
 
 def project_far(tokens, w, wvt, keys, vals, wkeys, wvals):
     nlb, groups, rows, _ = keys.shape
-    width = tokens.shape[1]
     ks = [
-        dot(tokens[...], w[:, width + g * WIDE : width + (g + 1) * WIDE]).astype(BF16)
+        dot(tokens[...], w[:, g * WIDE : (g + 1) * WIDE]).astype(BF16)
         for g in range(groups)
     ]
     for g in range(groups):
@@ -306,7 +333,7 @@
                 out[o, b * span : (b + 1) * span, g * WIDE : (g + 1) * WIDE] = r[at : at + span, :]
 
 
-def call(kernel, scalars, arrays, outs, scratch, unread=0, cost=COST, room=22):
+def call(kernel, scalars, arrays, outs, scratch, unread=0, unwritten=0, cost=COST, room=22):
     smem = pl.BlockSpec(memory_space=pltpu.SMEM)
     vmem = pl.BlockSpec(memory_space=pltpu.VMEM)
     single = not isinstance(outs, (list, tuple))
@@ -320,7 +347,9 @@
         kernel,
         out_shape=outs,
         in_specs=[smem] * len(scalars) + specs,
-        out_specs=vmem if single else [vmem] * len(outs),
+        out_specs=vmem
+        if single
+        else [vmem] * (len(outs) - unwritten) + [pl.BlockSpec(memory_space=pltpu.HBM)] * unwritten,
         scratch_shapes=scratch,
         compiler_params=pltpu.CompilerParams(vmem_limit_bytes=room * MIB),
         cost_estimate=pl.CostEstimate(flops=cost, bytes_accessed=1000, transcendentals=0),
@@ -381,26 +410,51 @@
         unread=1,
         room=4,
     )
-    f = [permute(part, across) for part in parts]
+    f = [permute(parts[0], across)]
+    weight = jax.ShapeDtypeStruct((width, width), BF16)
+    qc, far_wvt = call(
+        query_kernel,
+        (),
+        (*parts, projection),
+        [jax.ShapeDtypeStruct(tile, BF16), pltpu.HBM(weight.shape, BF16)],
+        [
+            pltpu.VMEM((nlb * rows, width), BF16),
+            pltpu.VMEM((width, width), BF16),
+            pltpu.VMEM((width, width), BF16),
+            pltpu.VMEM((width, width), BF16),
+            pltpu.SemaphoreType.DMA((3,)),
+        ],
+        unread=1,
+        unwritten=1,
+        room=16,
+    )
     bands = call(
-        band_kernel, (half_width,), (*parts, beside), jax.ShapeDtypeStruct((2 * rows, width), BF16), [], room=4
-    )
+        band_kernel,
+        (half_width,),
+        (*parts, after(beside, qc)),
+        jax.ShapeDtypeStruct((2 * rows, width), BF16),
+        [],
+        room=4,
+    )
+    f.append(permute(after(parts[1], qc), across))
+    f.append(permute(after(parts[2], bands), across))
     bands = permute(bands, outward)
     g0 = permute(f[0], onward)
     held, *_ = lax.optimization_barrier((parts[0], f[0]))
-    qc, keys, vals, wvt = call(
+    keys, vals, wk, wvt = call(
         own_kernel,
         (),
-        (held, *parts[1:], beside, projection),
+        (held, *parts[1:], beside, projection, far_wvt),
         [
-            jax.ShapeDtypeStruct(tile, BF16),
             jax.ShapeDtypeStruct((nlb, groups, 2 * rows, WIDE), BF16),
             jax.ShapeDtypeStruct((nlb, groups, WIDE, 2 * rows), BF16),
-            jax.ShapeDtypeStruct((width, width), BF16),
+            weight,
+            weight,
         ],
-        [pltpu.VMEM((nlb * rows, width), BF16), pltpu.VMEM((2 * nlb * rows, width), BF16)],
-    )
-    g1 = permute(after(f[1], qc), onward)
+        [pltpu.VMEM((2 * nlb * rows, width), BF16), pltpu.SemaphoreType.DMA((2,))],
+        unread=2,
+    )
+    g1 = permute(after(f[1], keys), onward)
     m, l, acc = call(
         near_kernel,
         (neighbours,),
@@ -414,7 +468,7 @@
     m, l, acc = call(
         across_kernel,
         (neighbours, half_width),
-        (*f, bands, projection, wvt, qc, m, l, acc),
+        (*f, bands, wk, wvt, qc, m, l, acc),
         carried_shapes,
         [pltpu.VMEM(((nlb + 2) * rows, width), BF16), key_scratch, val_scratch, *wide_scratch],
         cost=ACROSS_COST,
@@ -423,7 +477,7 @@
     early_keys, early_vals = call(
         early_kernel,
         (),
-        (after(g0, m), g1, projection, wvt),
+        (after(g0, m), g1, wk, wvt),
         [
             jax.ShapeDtypeStruct((early, groups, rows, WIDE), BF16),
             jax.ShapeDtypeStruct((2, early, groups, WIDE, 2 * rows), BF16),
@@ -444,7 +498,7 @@
     m, l, acc = call(
         onward_kernel,
         (neighbours, half_width),
-        (g2, projection, wvt, qc, early_keys, early_vals, m, l, acc),
+        (g2, wk, wvt, qc, early_keys, early_vals, m, l, acc),
         carried_shapes,
         [
             key_scratch,
@@ -454,7 +508,7 @@
     return call(
         last_kernel,
         (neighbours, half_width),
-        (e, projection, wvt, out_weight, qc, m, l, acc),
+        (e, wk, wvt, out_weight, qc, m, l, acc),
         jax.ShapeDtypeStruct(tokens.shape, BF16),
         [
             key_scratch,

time: 48.4 us -> 59 us (1.22)
  the two profiles are of different devices: /device:TPU:0 before, /device:TPU:5 now
where the time goes in v6:
time: 59 us; the launch traced here: 58.8 us
  Pallas kernels  33.9 us (57%)
  starting transfers between devices  24.4 us (41%)
    pallas_call x10, Pallas kernels, call(): pl.pallas_call(kernel, out_shape=outs, in_specs=[smem] * len(scalars) + s...  33.9 us
    ppermute x9, starting transfers between devices, permute(): return lax.ppermute(block, 'lon', [(i, step(i) % count) for i in devices])  24.4 us
  transfers between devices with their start and end apart: 9, of which 1 were waited for; matrix products, arithmetic and copies ran while one was open for 0% of the time, Pallas kernels for 42%

profile of v6, /device:TPU:5, one launch (start us, length us, event | category | flops | bytes accessed | tf_op | source)
XLA Modules:
  0.0 58.8 jit_solution(2528695954630314640)
XLA Ops:
  0.0 0.7 %collective-permute-start.2 = (bf16[2,192,1024]{2,1,0:T(8,128)(2,1)}, bf16[2,192,1024]{2,1,0:T(8,128)(2,1)S(1)}, u32[]{:S(2)}, u32[]{:S(2)}) collective-permute-start(bf16[2,192,1024]{2,1,0:T(8,128)(2,1)} %x.1), channel_id=1, source_target_pairs={{0,1},{1,0},{2,3},{3,2},{4,5},{5,4},{6,7},{7,6},{8,9},{9,8},{10,11... | collective-permute-start | bytes 2359304 | tf_op jit(solution)/shard_map/ppermute | solution.py:374
  0.7 1.3 %shard_map.55 = (bf16[128,1024]{1,0:T(8,128)(2,1)S(1)}, bf16[128,1024]{1,0:T(8,128)(2,1)S(1)}, bf16[128,1024]{1,0:T(8,128)(2,1)S(1)}) custom-call(bf16[2,192,1024]{2,1,0:T(8,128)(2,1)} %x.1), custom_call_target="tpu_custom_call" | custom-call | flops 2000000000 | bytes 1000 | tf_op jit(solution)/shard_map/pallas_call | solution.py:346
  1.9 0.1 collective-permute-start
  2.0 0.0 copy-start.1
  2.0 3.7 %shard_map.56 = (bf16[24,64,256]{2,1,0:T(8,128)(2,1)S(1)}, bf16[1024,1024]{1,0:T(8,128)(2,1)}) custom-call(bf16[128,1024]{1,0:T(8,128)(2,1)S(1)} %get-tuple-element.41.x0, bf16[128,1024]{1,0:T(8,128)(2,1)S(1)} %get-tuple-element.38.x1, bf16[128,1024]{1,0:T(8,128)(2,1)S(1)} %get-tuple-element.40.x2, bf16[1024,3072]{1,0:T(8,128)(2,1)} %w.3), custom_call_target="tpu_custom_call" | custom-call | flops 2000000000 | bytes 1000 | tf_op jit(solution)/shard_map/pallas_call | solution.py:346
  5.7 0.0 copy-start.2
  5.7 1.5 %collective-permute-start.1 = (bf16[128,1024]{1,0:T(8,128)(2,1)S(1)}, bf16[128,1024]{1,0:T(8,128)(2,1)S(1)}, u32[]{:S(2)}, u32[]{:S(2)}) collective-permute-start(bf16[128,1024]{1,0:T(8,128)(2,1)S(1)} %get-tuple-element.38.x1), channel_id=1, source_target_pairs={{0,2},{1,3},{2,0},{3,1},{4,6},{5,7},{6,4},{7,5},{8,10},{9,11},{10,... | collective-permute-start | bytes 786440 | tf_op jit(solution)/shard_map/ppermute | solution.py:374
  7.2 0.6 %shard_map.57 = bf16[128,1024]{1,0:T(8,128)(2,1)S(1)} custom-call(s32[6]{0:T(128)S(1)} %copy-done.1, bf16[128,1024]{1,0:T(8,128)(2,1)S(1)} %get-tuple-element.41.x0, bf16[128,1024]{1,0:T(8,128)(2,1)S(1)} %get-tuple-element.38.x1, bf16[128,1024]{1,0:T(8,128)(2,1)S(1)} %get-tuple-element.40.x2, bf16[2,192,1024]{2,1,0:T(8,128)(2,1)S(1)} %collective-permute-done.2.s), custom_call_target="tpu_custom_call" | custom-call | flops 2000000000 | bytes 1000 | tf_op jit(solution)/shard_map/pallas_call | solution.py:346
  7.9 3.4 %collective-permute-start.6 = (bf16[128,1024]{1,0:T(8,128)(2,1)S(1)}, bf16[128,1024]{1,0:T(8,128)(2,1)S(1)}, u32[]{:S(2)}, u32[]{:S(2)}) collective-permute-start(bf16[128,1024]{1,0:T(8,128)(2,1)S(1)} %shard_map.57), channel_id=1, source_target_pairs={{0,4},{1,13},{2,6},{3,15},{4,8},{5,1},{6,10},{7,3},{8,12},{9,5},{1... | collective-permute-start | bytes 786440 | tf_op jit(solution)/shard_map/ppermute | solution.py:374
  11.2 0.1 copy.9.nbr
  11.3 0.0 collective-permute-done.f0
  11.3 1.9 %collective-permute-start.4 = (bf16[128,1024]{1,0:T(8,128)(2,1)S(1)}, bf16[128,1024]{1,0:T(8,128)(2,1)S(1)}, u32[]{:S(2)}, u32[]{:S(2)}) collective-permute-start(bf16[128,1024]{1,0:T(8,128)(2,1)S(1)} %collective-permute-done.f0), channel_id=1, source_target_pairs={{0,4},{1,5},{2,14},{3,15},{4,8},{5,9},{6,2},{7,3},{8,12},{9,13},{1... | collective-permute-start | bytes 786440 | tf_op jit(solution)/shard_map/ppermute | solution.py:374
  13.3 5.2 %shard_map.58 = (bf16[6,4,128,256]{3,2,1,0:T(8,128)(2,1)S(1)}, bf16[6,4,256,128]{3,2,1,0:T(8,128)(2,1)S(1)}, bf16[1024,1024]{1,0:T(8,128)(2,1)S(1)}, bf16[1024,1024]{1,0:T(8,128)(2,1)S(1)}) custom-call(bf16[128,1024]{1,0:T(8,128)(2,1)S(1)} %get-tuple-element.41.x0, bf16[128,1024]{1,0:T(8,128)(2,1)S(1)} %get-tuple-element.38.x1, ...), custom_call_target="tpu_custom_call" | custom-call | flops 2000000000 | bytes 1000 | tf_op jit(solution)/shard_map/pallas_call | solution.py:346
  18.5 0.0 collective-permute-done.1.f1
  18.5 1.6 %collective-permute-start.5 = (bf16[128,1024]{1,0:T(8,128)(2,1)S(1)}, bf16[128,1024]{1,0:T(8,128)(2,1)S(1)}, u32[]{:S(2)}, u32[]{:S(2)}) collective-permute-start(bf16[128,1024]{1,0:T(8,128)(2,1)S(1)} %collective-permute-done.1.f1), channel_id=1, source_target_pairs={{0,4},{1,5},{2,14},{3,15},{4,8},{5,9},{6,2},{7,3},{8,12},{9,13},{1... | collective-permute-start | bytes 786440 | tf_op jit(solution)/shard_map/ppermute | solution.py:374
  20.1 3.0 %shard_map.59 = (f32[24,1,256]{2,1,0:T(1,128)S(1)}, f32[24,1,256]{2,1,0:T(1,128)S(1)}, f32[24,64,256]{2,1,0:T(8,128)S(1)}) custom-call(s32[6,2]{1,0:T(8,128)S(1)} %copy.9.nbr, bf16[24,64,256]{2,1,0:T(8,128)(2,1)S(1)} %get-tuple-element.45.qc, bf16[6,4,128,256]{3,2,1,0:T(8,128)(2,1)S(1)} %get-tuple-element.43.keys, ...), custom_call_target="tpu_custom_call" | custom-call | flops 2000000000 | bytes 1000 | tf_op jit(solution)/shard_map/pallas_call | solution.py:346
  23.2 1.4 %collective-permute-start.7 = (bf16[128,1024]{1,0:T(8,128)(2,1)S(1)}, bf16[128,1024]{1,0:T(8,128)(2,1)S(1)}, u32[]{:S(2)}, u32[]{:S(2)}) collective-permute-start(bf16[128,1024]{1,0:T(8,128)(2,1)S(1)} %collective-permute-done.3.f2), channel_id=1, source_target_pairs={{0,4},{1,5},{2,14},{3,15},{4,8},{5,9},{6,2},{7,3},{8,12},{9,13},{1... | collective-permute-start | bytes 786440 | tf_op jit(solution)/shard_map/ppermute | solution.py:374
  24.6 6.0 %shard_map.60 = (f32[24,1,256]{2,1,0:T(1,128)S(1)}, f32[24,1,256]{2,1,0:T(1,128)S(1)}, f32[24,64,256]{2,1,0:T(8,128)S(1)}) custom-call(s32[6,2]{1,0:T(8,128)S(1)} %copy.9.nbr, s32[6]{0:T(128)S(1)} %copy-done.1, bf16[128,1024]{1,0:T(8,128)(2,1)S(1)} %collective-permute-done.f0, bf16[128,1024]{1,0:T(8,128)(2,1)S(1)} %collective-permute-done.1.f1, ...), custom_call_target="tpu_custom_call" | custom-call | flops 2000000000 | bytes 1000 | tf_op jit(solution)/shard_map/pallas_call | solution.py:346
  30.6 1.4 %shard_map.61 = (bf16[4,4,64,256]{3,2,1,0:T(8,128)(2,1)S(1)}, bf16[2,4,4,256,128]{4,3,2,1,0:T(8,128)(2,1)S(1)}) custom-call(bf16[128,1024]{1,0:T(8,128)(2,1)S(1)} %collective-permute-done.4.g0, bf16[128,1024]{1,0:T(8,128)(2,1)S(1)} %collective-permute-done.5.g1, bf16[1024,1024]{1,0:T(8,128)(2,1)S(1)} %get-tuple-element.49.w, ...), custom_call_target="tpu_custom_call" | custom-call | flops 2000000000 | bytes 1000 | tf_op jit(solution)/shard_map/pallas_call | solution.py:346
  32.0 0.2 collective-permute-done.7.g2
  32.3 0.9 %shard_map.62 = bf16[512,1024]{1,0:T(8,128)(2,1)S(1)} custom-call(s32[6]{0:T(128)S(1)} %copy-done.1, bf16[128,1024]{1,0:T(8,128)(2,1)S(1)} %collective-permute-done.f0, bf16[128,1024]{1,0:T(8,128)(2,1)S(1)} %collective-permute-done.1.f1, bf16[128,1024]{1,0:T(8,128)(2,1)S(1)} %collective-permute-done.3.f2, bf16[128,1024]{1,0:T(8,128)(2,1)S(1)} %collective-permute-done.4.g0, ...), custom_call_target="tpu_custom_call" | custom-call | flops 2000000000 | bytes 1000 | tf_op jit(solution)/shard_map/pallas_call | solution.py:346
  33.1 13.9 %collective-permute-start.8 = (bf16[512,1024]{1,0:T(8,128)(2,1)S(1)}, bf16[512,1024]{1,0:T(8,128)(2,1)S(1)}, u32[]{:S(2)}, u32[]{:S(2)}) collective-permute-start(bf16[512,1024]{1,0:T(8,128)(2,1)S(1)} %shard_map.62), channel_id=1, source_target_pairs={{0,1},{1,0},{2,3},{3,2},{4,5},{5,4},{6,7},{7,6},{8,9},{9,8},{10,11... | collective-permute-start | bytes 3145736 | tf_op jit(solution)/shard_map/ppermute | solution.py:374
  47.0 3.6 %shard_map.63 = (f32[24,1,256]{2,1,0:T(1,128)S(1)}, f32[24,1,256]{2,1,0:T(1,128)S(1)}, f32[24,64,256]{2,1,0:T(8,128)S(1)}) custom-call(s32[6,2]{1,0:T(8,128)S(1)} %copy.9.nbr, s32[6]{0:T(128)S(1)} %copy-done.1, bf16[128,1024]{1,0:T(8,128)(2,1)S(1)} %collective-permute-done.7.g2, bf16[1024,1024]{1,0:T(8,128)(2,1)S(1)} %get-tuple-element.49.w, ...), custom_call_target="tpu_custom_call" | custom-call | flops 2000000000 | bytes 1000 | tf_op jit(solution)/shard_map/pallas_call | solution.py:346
  50.7 8.2 %shard_map.64 = bf16[2,192,1024]{2,1,0:T(8,128)(2,1)} custom-call(s32[6,2]{1,0:T(8,128)S(1)} %copy.9.nbr, s32[6]{0:T(128)S(1)} %copy-done.1, bf16[512,1024]{1,0:T(8,128)(2,1)S(1)} %collective-permute-done.8.e, bf16[1024,1024]{1,0:T(8,128)(2,1)S(1)} %get-tuple-element.49.w, bf16[1024,1024]{1,0:T(8,128)(2,1)S(1)} %get-tuple-element.50.wvt, ...), custom_call_target="tpu_custom_call" | custom-call | flops 2000000000 | bytes 1000 | tf_op jit(solution)/shard_map/pallas_call | solution.py:346
  (11 shorter events, 0.0 us)
Async XLA Ops:
  0.0 7.2 %collective-permute-start.2 = (bf16[2,192,1024]{2,1,0:T(8,128)(2,1)}, bf16[2,192,1024]{2,1,0:T(8,128)(2,1)S(1)}, u32[]{:S(2)}, u32[]{:S(2)}) collective-permute-start(bf16[2,192,1024]{2,1,0:T(8,128)(2,1)} %x.1), channel_id=1, source_target_pairs={{0,1},{1,0},{2,3},{3,2},{4,5},{5,4},{6,7},{7,6},{8,9},{9,8},{10,11... | collective-permute-start | bytes 2359304 | tf_op jit(solution)/shard_map/ppermute | solution.py:374
  1.9 9.4 %collective-permute-start = (bf16[128,1024]{1,0:T(8,128)(2,1)S(1)}, bf16[128,1024]{1,0:T(8,128)(2,1)S(1)}, u32[]{:S(2)}, u32[]{:S(2)}) collective-permute-start(bf16[128,1024]{1,0:T(8,128)(2,1)S(1)} %get-tuple-element.41.x0), channel_id=1, source_target_pairs={{0,2},{1,3},{2,0},{3,1},{4,6},{5,7},{6,4},{7,5},{8,10},{9,11},{10,... | collective-permute-start | bytes 786440 | tf_op jit(solution)/shard_map/ppermute | solution.py:374
  2.0 5.2 %copy-start.1 = (s32[6]{0:T(128)S(1)}, s32[6]{0:T(128)}, u32[]{:S(2)}) copy-start(s32[6]{0:T(128)} %hw.9) | copy-start | bytes 76
  5.7 5.5 %copy-start.2 = (s32[6,2]{0,1:T(2,128)S(1)}, s32[6,2]{0,1:T(2,128)}, u32[]{:S(2)}) copy-start(s32[6,2]{0,1:T(2,128)} %param.9) | copy-start | bytes 148
  5.7 12.8 %collective-permute-start.1 = (bf16[128,1024]{1,0:T(8,128)(2,1)S(1)}, bf16[128,1024]{1,0:T(8,128)(2,1)S(1)}, u32[]{:S(2)}, u32[]{:S(2)}) collective-permute-start(bf16[128,1024]{1,0:T(8,128)(2,1)S(1)} %get-tuple-element.38.x1), channel_id=1, source_target_pairs={{0,2},{1,3},{2,0},{3,1},{4,6},{5,7},{6,4},{7,5},{8,10},{9,11},{10,... | collective-permute-start | bytes 786440 | tf_op jit(solution)/shard_map/ppermute | solution.py:374
  7.9 12.3 %collective-permute-start.6 = (bf16[128,1024]{1,0:T(8,128)(2,1)S(1)}, bf16[128,1024]{1,0:T(8,128)(2,1)S(1)}, u32[]{:S(2)}, u32[]{:S(2)}) collective-permute-start(bf16[128,1024]{1,0:T(8,128)(2,1)S(1)} %shard_map.57), channel_id=1, source_target_pairs={{0,4},{1,13},{2,6},{3,15},{4,8},{5,1},{6,10},{7,3},{8,12},{9,5},{1... | collective-permute-start | bytes 786440 | tf_op jit(solution)/shard_map/ppermute | solution.py:374
  11.3 19.3 %collective-permute-start.4 = (bf16[128,1024]{1,0:T(8,128)(2,1)S(1)}, bf16[128,1024]{1,0:T(8,128)(2,1)S(1)}, u32[]{:S(2)}, u32[]{:S(2)}) collective-permute-start(bf16[128,1024]{1,0:T(8,128)(2,1)S(1)} %collective-permute-done.f0), channel_id=1, source_target_pairs={{0,4},{1,5},{2,14},{3,15},{4,8},{5,9},{6,2},{7,3},{8,12},{9,13},{1... | collective-permute-start | bytes 786440 | tf_op jit(solution)/shard_map/ppermute | solution.py:374
  13.3 9.9 %collective-permute-start.3 = (bf16[128,1024]{1,0:T(8,128)(2,1)S(1)}, bf16[128,1024]{1,0:T(8,128)(2,1)S(1)}, u32[]{:S(2)}, u32[]{:S(2)}) collective-permute-start(bf16[128,1024]{1,0:T(8,128)(2,1)S(1)} %get-tuple-element.40.x2), channel_id=1, source_target_pairs={{0,2},{1,3},{2,0},{3,1},{4,6},{5,7},{6,4},{7,5},{8,10},{9,11},{10,... | collective-permute-start | bytes 786440 | tf_op jit(solution)/shard_map/ppermute | solution.py:374
  18.5 12.1 %collective-permute-start.5 = (bf16[128,1024]{1,0:T(8,128)(2,1)S(1)}, bf16[128,1024]{1,0:T(8,128)(2,1)S(1)}, u32[]{:S(2)}, u32[]{:S(2)}) collective-permute-start(bf16[128,1024]{1,0:T(8,128)(2,1)S(1)} %collective-permute-done.1.f1), channel_id=1, source_target_pairs={{0,4},{1,5},{2,14},{3,15},{4,8},{5,9},{6,2},{7,3},{8,12},{9,13},{1... | collective-permute-start | bytes 786440 | tf_op jit(solution)/shard_map/ppermute | solution.py:374
  23.2 9.1 %collective-permute-start.7 = (bf16[128,1024]{1,0:T(8,128)(2,1)S(1)}, bf16[128,1024]{1,0:T(8,128)(2,1)S(1)}, u32[]{:S(2)}, u32[]{:S(2)}) collective-permute-start(bf16[128,1024]{1,0:T(8,128)(2,1)S(1)} %collective-permute-done.3.f2), channel_id=1, source_target_pairs={{0,4},{1,5},{2,14},{3,15},{4,8},{5,9},{6,2},{7,3},{8,12},{9,13},{1... | collective-permute-start | bytes 786440 | tf_op jit(solution)/shard_map/ppermute | solution.py:374
  33.1 17.5 %collective-permute-start.8 = (bf16[512,1024]{1,0:T(8,128)(2,1)S(1)}, bf16[512,1024]{1,0:T(8,128)(2,1)S(1)}, u32[]{:S(2)}, u32[]{:S(2)}) collective-permute-start(bf16[512,1024]{1,0:T(8,128)(2,1)S(1)} %shard_map.62), channel_id=1, source_target_pairs={{0,1},{1,0},{2,3},{3,2},{4,5},{5,4},{6,7},{7,6},{8,9},{9,8},{10,11... | collective-permute-start | bytes 3145736 | tf_op jit(solution)/shard_map/ppermute | solution.py:374
  47.0 3.7 %copy-start = (bf16[1024,1024]{1,0:T(8,128)(2,1)S(1)}, bf16[1024,1024]{1,0:T(8,128)(2,1)}, u32[]{:S(2)}) copy-start(bf16[1024,1024]{1,0:T(8,128)(2,1)} %wout.1) | copy-start | bytes 6291460

commit v7 on v5

--- a/solution.py
+++ b/solution.py
@@ -126,11 +126,16 @@
                 bands[rows + o * span : rows + (o + 1) * span, :] = s[o, c * span : (c + 1) * span, :]
 
 
-def own_kernel(x0, x1, x2, s, w, qc, keys, vals, wvt, own, both):
+def own_kernel(x0, x1, x2, s, w, qc, keys, vals, wk, wvt, own, both, wq, wv, sems):
     lon, _, width = s.shape
     nlb, groups, rows, _ = keys.shape
     rows //= 2
     span = rows // lon
+    fetch = [
+        pltpu.make_async_copy(w.at[:, pl.ds(which * width, width)], place, sems.at[which])
+        for which, place in ((0, wq), (1, wk), (2, wv))
+    ]
+    fetch[1].start()
     at = 0
     for part in (x0, x1, x2):
         for c in range(part.shape[0] // rows):
@@ -142,19 +147,25 @@
         for o in range(lon):
             at = (2 * c + 1) * rows + o * span
             both[at : at + span, :] = s[o, c * span : (c + 1) * span, :]
-    for g in range(groups):
-        k = dot(both[...], w[:, width + g * WIDE : width + (g + 1) * WIDE]).astype(BF16)
+    tiles = [slice(g * WIDE, (g + 1) * WIDE) for g in range(groups)]
+    fetch[1].wait()
+    fetch[0].start()
+    fetch[2].start()
+    for g, columns in enumerate(tiles):
+        k = dot(both[...], wk[:, columns]).astype(BF16)
         for c in range(nlb):
             keys[c, g] = k[2 * c * rows : 2 * (c + 1) * rows, :]
-        q = dot(own[...], w[:, g * WIDE : (g + 1) * WIDE]).astype(BF16).astype(F32)
+    fetch[0].wait()
+    fetch[2].wait()
+    for g, columns in enumerate(tiles):
+        q = dot(own[...], wq[:, columns]).astype(BF16).astype(F32)
         for b in range(nlb):
             qt = q[b * rows : (b + 1) * rows, :].T
             qc[b * groups + g] = jnp.concatenate(
                 [qt[h * HEAD : (h + 1) * HEAD, :] for h in range(PACK)], axis=1
             ).astype(BF16)
-        at = 2 * width + g * WIDE
-        wvt[g * WIDE : (g + 1) * WIDE, :] = w[:, at : at + WIDE].T
-        v = dot_nt(wvt[g * WIDE : (g + 1) * WIDE, :], both[...]).astype(BF16)
+        wvt[columns, :] = wv[:, columns].T
+        v = dot_nt(wvt[columns, :], both[...]).astype(BF16)
         for c in range(nlb):
             vals[c, g] = v[:, 2 * c * rows : 2 * (c + 1) * rows]
 
@@ -177,9 +188,8 @@
 
 def project_far(tokens, w, wvt, keys, vals, wkeys, wvals):
     nlb, groups, rows, _ = keys.shape
-    width = tokens.shape[1]
     ks = [
-        dot(tokens[...], w[:, width + g * WIDE : width + (g + 1) * WIDE]).astype(BF16)
+        dot(tokens[...], w[:, g * WIDE : (g + 1) * WIDE]).astype(BF16)
         for g in range(groups)
     ]
     for g in range(groups):
@@ -388,7 +398,7 @@
     bands = permute(bands, outward)
     g0 = permute(f[0], onward)
     held, *_ = lax.optimization_barrier((parts[0], f[0]))
-    qc, keys, vals, wvt = call(
+    qc, keys, vals, wk, wvt = call(
         own_kernel,
         (),
         (held, *parts[1:], beside, projection),
@@ -397,8 +407,16 @@
             jax.ShapeDtypeStruct((nlb, groups, 2 * rows, WIDE), BF16),
             jax.ShapeDtypeStruct((nlb, groups, WIDE, 2 * rows), BF16),
             jax.ShapeDtypeStruct((width, width), BF16),
+            jax.ShapeDtypeStruct((width, width), BF16),
         ],
-        [pltpu.VMEM((nlb * rows, width), BF16), pltpu.VMEM((2 * nlb * rows, width), BF16)],
+        [
+            pltpu.VMEM((nlb * rows, width), BF16),
+            pltpu.VMEM((2 * nlb * rows, width), BF16),
+            pltpu.VMEM((width, width), BF16),
+            pltpu.VMEM((width, width), BF16),
+            pltpu.SemaphoreType.DMA((3,)),
+        ],
+        unread=1,
     )
     g1 = permute(after(f[1], qc), onward)
     m, l, acc = call(
@@ -414,7 +432,7 @@
     m, l, acc = call(
         across_kernel,
         (neighbours, half_width),
-        (*f, bands, projection, wvt, qc, m, l, acc),
+        (*f, bands, wk, wvt, qc, m, l, acc),
         carried_shapes,
         [pltpu.VMEM(((nlb + 2) * rows, width), BF16), key_scratch, val_scratch, *wide_scratch],
         cost=ACROSS_COST,
@@ -423,7 +441,7 @@
     early_keys, early_vals = call(
         early_kernel,
         (),
-        (after(g0, m), g1, projection, wvt),
+        (after(g0, m), g1, wk, wvt),
         [
             jax.ShapeDtypeStruct((early, groups, rows, WIDE), BF16),
             jax.ShapeDtypeStruct((2, early, groups, WIDE, 2 * rows), BF16),
@@ -444,7 +462,7 @@
     m, l, acc = call(
         onward_kernel,
         (neighbours, half_width),
-        (g2, projection, wvt, qc, early_keys, early_vals, m, l, acc),
+        (g2, wk, wvt, qc, early_keys, early_vals, m, l, acc),
         carried_shapes,
         [
             key_scratch,
@@ -454,7 +472,7 @@
     return call(
         last_kernel,
         (neighbours, half_width),
-        (e, projection, wvt, out_weight, qc, m, l, acc),
+        (e, wk, wvt, out_weight, qc, m, l, acc),
         jax.ShapeDtypeStruct(tokens.shape, BF16),
         [
             key_scratch,

time: 48.4 us -> 47.9 us (0.990)
  local copies, waits for them, and re-layouts: 2.89 us -> 0.11 us
  Pallas kernels: 29.3 us -> 31.7 us
    unnamed x11 -> x7, local copies, waits for them, and re-layouts: 2.89 us -> 0.11 us
    pallas_call x9, Pallas kernels: 29.3 us -> 31.7 us  [call(): pl.pallas_call(kernel, out_shape=outs, in_specs=[smem] * len(scalars) + s...]
  transfers between devices with their start and end apart: 9 -> 9, of which waited for: 2 -> 2; matrix products, arithmetic and copies ran while one was open for 0% -> 0% of each run, Pallas kernels for 42% -> 47%
where the time goes in v7:
time: 47.9 us; the launch traced here: 47.7 us
  Pallas kernels  31.7 us (66%)
  starting transfers between devices  12.2 us (25%)
  waiting for transfers between devices  3.51 us (7%)
    pallas_call x9, Pallas kernels, call(): pl.pallas_call(kernel, out_shape=outs, in_specs=[smem] * len(scalars) + s...  31.7 us
    ppermute x9, starting transfers between devices, permute(): return lax.ppermute(block, 'lon', [(i, step(i) % count) for i in devices])  12.2 us
    ppermute x9, waiting for transfers between devices, permute(): return lax.ppermute(block, 'lon', [(i, step(i) % count) for i in devices])  3.51 us
  transfers between devices with their start and end apart: 9, of which 2 were waited for; matrix products, arithmetic and copies ran while one was open for 0% of the time, Pallas kernels for 47%

profile of v7, /device:TPU:0, one launch (start us, length us, event | category | flops | bytes accessed | tf_op | source)
XLA Modules:
  0.0 47.7 jit_solution(5103329307284425934)
XLA Ops:
  0.0 0.5 collective-permute-start.4
  0.5 1.3 %shard_map.55 = (bf16[128,1024]{1,0:T(8,128)(2,1)S(1)}, bf16[128,1024]{1,0:T(8,128)(2,1)S(1)}, bf16[128,1024]{1,0:T(8,128)(2,1)S(1)}) custom-call(bf16[2,192,1024]{2,1,0:T(8,128)(2,1)} %x.1), custom_call_target="tpu_custom_call" | custom-call | flops 2000000000 | bytes 1000 | tf_op jit(solution)/shard_map/pallas_call | solution.py:329
  1.7 2.6 %collective-permute-start = (bf16[128,1024]{1,0:T(8,128)(2,1)S(1)}, bf16[128,1024]{1,0:T(8,128)(2,1)S(1)}, u32[]{:S(2)}, u32[]{:S(2)}) collective-permute-start(bf16[128,1024]{1,0:T(8,128)(2,1)S(1)} %get-tuple-element.33.x0), channel_id=1, source_target_pairs={{0,2},{1,3},{2,0},{3,1},{4,6},{5,7},{6,4},{7,5},{8,10},{9,11},{10,... | collective-permute-start | bytes 786440 | tf_op jit(solution)/shard_map/ppermute | solution.py:355
  4.3 0.1 collective-permute-start.1
  4.4 0.6 %shard_map.57 = bf16[128,1024]{1,0:T(8,128)(2,1)S(1)} custom-call(s32[6]{0:T(128)S(1)} %copy-done.1, bf16[128,1024]{1,0:T(8,128)(2,1)S(1)} %get-tuple-element.33.x0, bf16[128,1024]{1,0:T(8,128)(2,1)S(1)} %get-tuple-element.31.x1, bf16[128,1024]{1,0:T(8,128)(2,1)S(1)} %get-tuple-element.32.x2, bf16[2,192,1024]{2,1,0:T(8,128)(2,1)S(1)} %collective-permute-done.4.s), custom_call_target="tpu_custom_call" | custom-call | flops 2000000000 | bytes 1000 | tf_op jit(solution)/shard_map/pallas_call | solution.py:329
  5.0 2.1 %collective-permute-start.6 = (bf16[128,1024]{1,0:T(8,128)(2,1)S(1)}, bf16[128,1024]{1,0:T(8,128)(2,1)S(1)}, u32[]{:S(2)}, u32[]{:S(2)}) collective-permute-start(bf16[128,1024]{1,0:T(8,128)(2,1)S(1)} %shard_map.57), channel_id=1, source_target_pairs={{0,4},{1,13},{2,6},{3,15},{4,8},{5,1},{6,10},{7,3},{8,12},{9,5},{1... | collective-permute-start | bytes 786440 | tf_op jit(solution)/shard_map/ppermute | solution.py:355
  7.1 1.5 %collective-permute-start.2 = (bf16[128,1024]{1,0:T(8,128)(2,1)S(1)}, bf16[128,1024]{1,0:T(8,128)(2,1)S(1)}, u32[]{:S(2)}, u32[]{:S(2)}) collective-permute-start(bf16[128,1024]{1,0:T(8,128)(2,1)S(1)} %get-tuple-element.32.x2), channel_id=1, source_target_pairs={{0,2},{1,3},{2,0},{3,1},{4,6},{5,7},{6,4},{7,5},{8,10},{9,11},{10,... | collective-permute-start | bytes 786440 | tf_op jit(solution)/shard_map/ppermute | solution.py:355
  8.6 0.1 copy.9.nbr
  8.7 2.8 %collective-permute-done.f0 = bf16[128,1024]{1,0:T(8,128)(2,1)S(1)} collective-permute-done((bf16[128,1024]{1,0:T(8,128)(2,1)S(1)}, bf16[128,1024]{1,0:T(8,128)(2,1)S(1)}, u32[]{:S(2)}, u32[]{:S(2)}) %collective-permute-start) | collective-permute-done | bytes 262176 | tf_op jit(solution)/shard_map/ppermute | solution.py:355
  11.5 2.0 %collective-permute-start.3 = (bf16[128,1024]{1,0:T(8,128)(2,1)S(1)}, bf16[128,1024]{1,0:T(8,128)(2,1)S(1)}, u32[]{:S(2)}, u32[]{:S(2)}) collective-permute-start(bf16[128,1024]{1,0:T(8,128)(2,1)S(1)} %collective-permute-done.f0), channel_id=1, source_target_pairs={{0,4},{1,5},{2,14},{3,15},{4,8},{5,9},{6,2},{7,3},{8,12},{9,13},{1... | collective-permute-start | bytes 786440 | tf_op jit(solution)/shard_map/ppermute | solution.py:355
  13.5 6.5 %shard_map.56 = (bf16[24,64,256]{2,1,0:T(8,128)(2,1)S(1)}, bf16[6,4,128,256]{3,2,1,0:T(8,128)(2,1)S(1)}, bf16[6,4,256,128]{3,2,1,0:T(8,128)(2,1)S(1)}, bf16[1024...) custom-call(bf16[128,1024]{1,0:T(8,128)(2,1)S(1)} %get-tuple-element.33.x0, bf16[128,1024]{1,0:T(8,128)(2,1)S(1)} %get-tuple-element.31.x1, ...), custom_call_target="tpu_custom_call" | custom-call | flops 2000000000 | bytes 1000 | tf_op jit(solution)/shard_map/pallas_call | solution.py:329
  20.0 0.0 collective-permute-done.1.f1
  20.0 1.6 %collective-permute-start.5 = (bf16[128,1024]{1,0:T(8,128)(2,1)S(1)}, bf16[128,1024]{1,0:T(8,128)(2,1)S(1)}, u32[]{:S(2)}, u32[]{:S(2)}) collective-permute-start(bf16[128,1024]{1,0:T(8,128)(2,1)S(1)} %collective-permute-done.1.f1), channel_id=1, source_target_pairs={{0,4},{1,5},{2,14},{3,15},{4,8},{5,9},{6,2},{7,3},{8,12},{9,13},{1... | collective-permute-start | bytes 786440 | tf_op jit(solution)/shard_map/ppermute | solution.py:355
  21.7 0.0 collective-permute-done.6.bands
  21.7 3.1 %shard_map.58 = (f32[24,1,256]{2,1,0:T(1,128)S(1)}, f32[24,1,256]{2,1,0:T(1,128)S(1)}, f32[24,64,256]{2,1,0:T(8,128)S(1)}) custom-call(s32[6,2]{1,0:T(8,128)S(1)} %copy.9.nbr, bf16[24,64,256]{2,1,0:T(8,128)(2,1)S(1)} %get-tuple-element.36.qc, bf16[6,4,128,256]{3,2,1,0:T(8,128)(2,1)S(1)} %get-tuple-element.37.keys, ...), custom_call_target="tpu_custom_call" | custom-call | flops 2000000000 | bytes 1000 | tf_op jit(solution)/shard_map/pallas_call | solution.py:329
  24.7 1.8 %collective-permute-start.7 = (bf16[128,1024]{1,0:T(8,128)(2,1)S(1)}, bf16[128,1024]{1,0:T(8,128)(2,1)S(1)}, u32[]{:S(2)}, u32[]{:S(2)}) collective-permute-start(bf16[128,1024]{1,0:T(8,128)(2,1)S(1)} %collective-permute-done.2.f2), channel_id=1, source_target_pairs={{0,4},{1,5},{2,14},{3,15},{4,8},{5,9},{6,2},{7,3},{8,12},{9,13},{1... | collective-permute-start | bytes 786440 | tf_op jit(solution)/shard_map/ppermute | solution.py:355
  26.6 6.1 %shard_map.59 = (f32[24,1,256]{2,1,0:T(1,128)S(1)}, f32[24,1,256]{2,1,0:T(1,128)S(1)}, f32[24,64,256]{2,1,0:T(8,128)S(1)}) custom-call(s32[6,2]{1,0:T(8,128)S(1)} %copy.9.nbr, s32[6]{0:T(128)S(1)} %copy-done.1, bf16[128,1024]{1,0:T(8,128)(2,1)S(1)} %collective-permute-done.f0, bf16[128,1024]{1,0:T(8,128)(2,1)S(1)} %collective-permute-done.1.f1, ...), custom_call_target="tpu_custom_call" | custom-call | flops 2000000000 | bytes 1000 | tf_op jit(solution)/shard_map/pallas_call | solution.py:329
  32.7 1.4 %shard_map.60 = (bf16[4,4,64,256]{3,2,1,0:T(8,128)(2,1)S(1)}, bf16[2,4,4,256,128]{4,3,2,1,0:T(8,128)(2,1)S(1)}) custom-call(bf16[128,1024]{1,0:T(8,128)(2,1)S(1)} %collective-permute-done.3.g0, bf16[128,1024]{1,0:T(8,128)(2,1)S(1)} %collective-permute-done.5.g1, bf16[1024,1024]{1,0:T(8,128)(2,1)S(1)} %get-tuple-element.41.w, ...), custom_call_target="tpu_custom_call" | custom-call | flops 4000000000 | bytes 1000 | tf_op jit(solution)/shard_map/pallas_call | solution.py:329
  34.1 0.7 %collective-permute-done.7.g2 = bf16[128,1024]{1,0:T(8,128)(2,1)S(1)} collective-permute-done((bf16[128,1024]{1,0:T(8,128)(2,1)S(1)}, bf16[128,1024]{1,0:T(8,128)(2,1)S(1)}, u32[]{:S(2)}, u32[]{:S(2)}) %collective-permute-start.7) | collective-permute-done | bytes 262176 | tf_op jit(solution)/shard_map/ppermute | solution.py:355
  34.7 0.9 %shard_map.61 = bf16[512,1024]{1,0:T(8,128)(2,1)S(1)} custom-call(s32[6]{0:T(128)S(1)} %copy-done.1, bf16[128,1024]{1,0:T(8,128)(2,1)S(1)} %collective-permute-done.f0, bf16[128,1024]{1,0:T(8,128)(2,1)S(1)} %collective-permute-done.1.f1, bf16[128,1024]{1,0:T(8,128)(2,1)S(1)} %collective-permute-done.2.f2, bf16[128,1024]{1,0:T(8,128)(2,1)S(1)} %collective-permute-done.3.g0, ...), custom_call_target="tpu_custom_call" | custom-call | flops 2000000000 | bytes 1000 | tf_op jit(solution)/shard_map/pallas_call | solution.py:329
  35.6 0.1 collective-permute-start.8
  35.7 0.0 copy-start
  35.7 3.7 %shard_map.62 = (f32[24,1,256]{2,1,0:T(1,128)S(1)}, f32[24,1,256]{2,1,0:T(1,128)S(1)}, f32[24,64,256]{2,1,0:T(8,128)S(1)}) custom-call(s32[6,2]{1,0:T(8,128)S(1)} %copy.9.nbr, s32[6]{0:T(128)S(1)} %copy-done.1, bf16[128,1024]{1,0:T(8,128)(2,1)S(1)} %collective-permute-done.7.g2, bf16[1024,1024]{1,0:T(8,128)(2,1)S(1)} %get-tuple-element.41.w, ...), custom_call_target="tpu_custom_call" | custom-call | flops 2000000000 | bytes 1000 | tf_op jit(solution)/shard_map/pallas_call | solution.py:329
  39.4 8.2 %shard_map.63 = bf16[2,192,1024]{2,1,0:T(8,128)(2,1)} custom-call(s32[6,2]{1,0:T(8,128)S(1)} %copy.9.nbr, s32[6]{0:T(128)S(1)} %copy-done.1, bf16[512,1024]{1,0:T(8,128)(2,1)S(1)} %collective-permute-done.8.e, bf16[1024,1024]{1,0:T(8,128)(2,1)S(1)} %get-tuple-element.41.w, bf16[1024,1024]{1,0:T(8,128)(2,1)S(1)} %get-tuple-element.42.wvt, ...), custom_call_target="tpu_custom_call" | custom-call | flops 2000000000 | bytes 1000 | tf_op jit(solution)/shard_map/pallas_call | solution.py:329
  (10 shorter events, 0.0 us)
Async XLA Ops:
  0.0 4.4 %copy-start.1 = (s32[6]{0:T(128)S(1)}, s32[6]{0:T(128)}, u32[]{:S(2)}) copy-start(s32[6]{0:T(128)} %hw.9) | copy-start | bytes 76
  0.0 4.4 %collective-permute-start.4 = (bf16[2,192,1024]{2,1,0:T(8,128)(2,1)}, bf16[2,192,1024]{2,1,0:T(8,128)(2,1)S(1)}, u32[]{:S(2)}, u32[]{:S(2)}) collective-permute-start(bf16[2,192,1024]{2,1,0:T(8,128)(2,1)} %x.1), channel_id=1, source_target_pairs={{0,1},{1,0},{2,3},{3,2},{4,5},{5,4},{6,7},{7,6},{8,9},{9,8},{10,11... | collective-permute-start | bytes 2359304 | tf_op jit(solution)/shard_map/ppermute | solution.py:355
  1.7 9.8 %collective-permute-start = (bf16[128,1024]{1,0:T(8,128)(2,1)S(1)}, bf16[128,1024]{1,0:T(8,128)(2,1)S(1)}, u32[]{:S(2)}, u32[]{:S(2)}) collective-permute-start(bf16[128,1024]{1,0:T(8,128)(2,1)S(1)} %get-tuple-element.33.x0), channel_id=1, source_target_pairs={{0,2},{1,3},{2,0},{3,1},{4,6},{5,7},{6,4},{7,5},{8,10},{9,11},{10,... | collective-permute-start | bytes 786440 | tf_op jit(solution)/shard_map/ppermute | solution.py:355
  4.3 15.7 %collective-permute-start.1 = (bf16[128,1024]{1,0:T(8,128)(2,1)S(1)}, bf16[128,1024]{1,0:T(8,128)(2,1)S(1)}, u32[]{:S(2)}, u32[]{:S(2)}) collective-permute-start(bf16[128,1024]{1,0:T(8,128)(2,1)S(1)} %get-tuple-element.31.x1), channel_id=1, source_target_pairs={{0,2},{1,3},{2,0},{3,1},{4,6},{5,7},{6,4},{7,5},{8,10},{9,11},{10,... | collective-permute-start | bytes 786440 | tf_op jit(solution)/shard_map/ppermute | solution.py:355
  4.4 4.2 %copy-start.2 = (s32[6,2]{0,1:T(2,128)S(1)}, s32[6,2]{0,1:T(2,128)}, u32[]{:S(2)}) copy-start(s32[6,2]{0,1:T(2,128)} %param.9) | copy-start | bytes 148
  5.0 16.7 %collective-permute-start.6 = (bf16[128,1024]{1,0:T(8,128)(2,1)S(1)}, bf16[128,1024]{1,0:T(8,128)(2,1)S(1)}, u32[]{:S(2)}, u32[]{:S(2)}) collective-permute-start(bf16[128,1024]{1,0:T(8,128)(2,1)S(1)} %shard_map.57), channel_id=1, source_target_pairs={{0,4},{1,13},{2,6},{3,15},{4,8},{5,1},{6,10},{7,3},{8,12},{9,5},{1... | collective-permute-start | bytes 786440 | tf_op jit(solution)/shard_map/ppermute | solution.py:355
  7.1 17.7 %collective-permute-start.2 = (bf16[128,1024]{1,0:T(8,128)(2,1)S(1)}, bf16[128,1024]{1,0:T(8,128)(2,1)S(1)}, u32[]{:S(2)}, u32[]{:S(2)}) collective-permute-start(bf16[128,1024]{1,0:T(8,128)(2,1)S(1)} %get-tuple-element.32.x2), channel_id=1, source_target_pairs={{0,2},{1,3},{2,0},{3,1},{4,6},{5,7},{6,4},{7,5},{8,10},{9,11},{10,... | collective-permute-start | bytes 786440 | tf_op jit(solution)/shard_map/ppermute | solution.py:355
  11.5 21.2 %collective-permute-start.3 = (bf16[128,1024]{1,0:T(8,128)(2,1)S(1)}, bf16[128,1024]{1,0:T(8,128)(2,1)S(1)}, u32[]{:S(2)}, u32[]{:S(2)}) collective-permute-start(bf16[128,1024]{1,0:T(8,128)(2,1)S(1)} %collective-permute-done.f0), channel_id=1, source_target_pairs={{0,4},{1,5},{2,14},{3,15},{4,8},{5,9},{6,2},{7,3},{8,12},{9,13},{1... | collective-permute-start | bytes 786440 | tf_op jit(solution)/shard_map/ppermute | solution.py:355
  20.0 12.6 %collective-permute-start.5 = (bf16[128,1024]{1,0:T(8,128)(2,1)S(1)}, bf16[128,1024]{1,0:T(8,128)(2,1)S(1)}, u32[]{:S(2)}, u32[]{:S(2)}) collective-permute-start(bf16[128,1024]{1,0:T(8,128)(2,1)S(1)} %collective-permute-done.1.f1), channel_id=1, source_target_pairs={{0,4},{1,5},{2,14},{3,15},{4,8},{5,9},{6,2},{7,3},{8,12},{9,13},{1... | collective-permute-start | bytes 786440 | tf_op jit(solution)/shard_map/ppermute | solution.py:355
  24.7 10.0 %collective-permute-start.7 = (bf16[128,1024]{1,0:T(8,128)(2,1)S(1)}, bf16[128,1024]{1,0:T(8,128)(2,1)S(1)}, u32[]{:S(2)}, u32[]{:S(2)}) collective-permute-start(bf16[128,1024]{1,0:T(8,128)(2,1)S(1)} %collective-permute-done.2.f2), channel_id=1, source_target_pairs={{0,4},{1,5},{2,14},{3,15},{4,8},{5,9},{6,2},{7,3},{8,12},{9,13},{1... | collective-permute-start | bytes 786440 | tf_op jit(solution)/shard_map/ppermute | solution.py:355
  35.6 3.8 %collective-permute-start.8 = (bf16[512,1024]{1,0:T(8,128)(2,1)S(1)}, bf16[512,1024]{1,0:T(8,128)(2,1)S(1)}, u32[]{:S(2)}, u32[]{:S(2)}) collective-permute-start(bf16[512,1024]{1,0:T(8,128)(2,1)S(1)} %shard_map.61), channel_id=1, source_target_pairs={{0,1},{1,0},{2,3},{3,2},{4,5},{5,4},{6,7},{7,6},{8,9},{9,8},{10,11... | collective-permute-start | bytes 3145736 | tf_op jit(solution)/shard_map/ppermute | solution.py:355
  35.7 3.7 %copy-start = (bf16[1024,1024]{1,0:T(8,128)(2,1)S(1)}, bf16[1024,1024]{1,0:T(8,128)(2,1)}, u32[]{:S(2)}) copy-start(bf16[1024,1024]{1,0:T(8,128)(2,1)} %wout.1) | copy-start | bytes 6291460

commit v8 on v7

--- a/solution.py
+++ b/solution.py
@@ -149,14 +149,18 @@
             both[at : at + span, :] = s[o, c * span : (c + 1) * span, :]
     tiles = [slice(g * WIDE, (g + 1) * WIDE) for g in range(groups)]
     fetch[1].wait()
+    fetch[2].start()
     fetch[0].start()
-    fetch[2].start()
     for g, columns in enumerate(tiles):
+        if g == groups // 2:
+            fetch[2].wait()
+        if g >= groups // 2:
+            for turned in tiles[2 * (g - groups // 2) : 2 * (g - groups // 2) + 2]:
+                wvt[turned, :] = wv[:, turned].T
         k = dot(both[...], wk[:, columns]).astype(BF16)
         for c in range(nlb):
             keys[c, g] = k[2 * c * rows : 2 * (c + 1) * rows, :]
     fetch[0].wait()
-    fetch[2].wait()
     for g, columns in enumerate(tiles):
         q = dot(own[...], wq[:, columns]).astype(BF16).astype(F32)
         for b in range(nlb):
@@ -164,7 +168,6 @@
             qc[b * groups + g] = jnp.concatenate(
                 [qt[h * HEAD : (h + 1) * HEAD, :] for h in range(PACK)], axis=1
             ).astype(BF16)
-        wvt[columns, :] = wv[:, columns].T
         v = dot_nt(wvt[columns, :], both[...]).astype(BF16)
         for c in range(nlb):
             vals[c, g] = v[:, 2 * c * rows : 2 * (c + 1) * rows]

time: 47.9 us -> 48.3 us (level)
  transfers between devices with their start and end apart: 9 -> 9, of which waited for: 2 -> 2; matrix products, arithmetic and copies ran while one was open for 0% -> 0% of each run, Pallas kernels for 47% -> 48%
where the time goes in v8:
time: 48.3 us; the launch traced here: 48 us
  Pallas kernels  32.1 us (66%)
  starting transfers between devices  12.2 us (25%)
  waiting for transfers between devices  3.5 us (7%)
    pallas_call x9, Pallas kernels, call(): pl.pallas_call(kernel, out_shape=outs, in_specs=[smem] * len(scalars) + s...  32.1 us
    ppermute x9, starting transfers between devices, permute(): return lax.ppermute(block, 'lon', [(i, step(i) % count) for i in devices])  12.2 us
    ppermute x9, waiting for transfers between devices, permute(): return lax.ppermute(block, 'lon', [(i, step(i) % count) for i in devices])  3.5 us
  transfers between devices with their start and end apart: 9, of which 2 were waited for; matrix products, arithmetic and copies ran while one was open for 0% of the time, Pallas kernels for 48%

profile of v8, /device:TPU:0, one launch (start us, length us, event | category | flops | bytes accessed | tf_op | source)
XLA Modules:
  0.0 48.0 jit_solution(14715297928508747856)
XLA Ops:
  0.0 0.5 collective-permute-start.4
  0.5 1.3 %shard_map.55 = (bf16[128,1024]{1,0:T(8,128)(2,1)S(1)}, bf16[128,1024]{1,0:T(8,128)(2,1)S(1)}, bf16[128,1024]{1,0:T(8,128)(2,1)S(1)}) custom-call(bf16[2,192,1024]{2,1,0:T(8,128)(2,1)} %x.1), custom_call_target="tpu_custom_call" | custom-call | flops 2000000000 | bytes 1000 | tf_op jit(solution)/shard_map/pallas_call | solution.py:332
  1.7 2.6 %collective-permute-start = (bf16[128,1024]{1,0:T(8,128)(2,1)S(1)}, bf16[128,1024]{1,0:T(8,128)(2,1)S(1)}, u32[]{:S(2)}, u32[]{:S(2)}) collective-permute-start(bf16[128,1024]{1,0:T(8,128)(2,1)S(1)} %get-tuple-element.33.x0), channel_id=1, source_target_pairs={{0,2},{1,3},{2,0},{3,1},{4,6},{5,7},{6,4},{7,5},{8,10},{9,11},{10,... | collective-permute-start | bytes 786440 | tf_op jit(solution)/shard_map/ppermute | solution.py:358
  4.3 0.1 collective-permute-start.1
  4.4 0.0 collective-permute-done.4.s
  4.4 0.6 %shard_map.57 = bf16[128,1024]{1,0:T(8,128)(2,1)S(1)} custom-call(s32[6]{0:T(128)S(1)} %copy-done.1, bf16[128,1024]{1,0:T(8,128)(2,1)S(1)} %get-tuple-element.33.x0, bf16[128,1024]{1,0:T(8,128)(2,1)S(1)} %get-tuple-element.31.x1, bf16[128,1024]{1,0:T(8,128)(2,1)S(1)} %get-tuple-element.32.x2, bf16[2,192,1024]{2,1,0:T(8,128)(2,1)S(1)} %collective-permute-done.4.s), custom_call_target="tpu_custom_call" | custom-call | flops 2000000000 | bytes 1000 | tf_op jit(solution)/shard_map/pallas_call | solution.py:332
  5.0 2.1 %collective-permute-start.6 = (bf16[128,1024]{1,0:T(8,128)(2,1)S(1)}, bf16[128,1024]{1,0:T(8,128)(2,1)S(1)}, u32[]{:S(2)}, u32[]{:S(2)}) collective-permute-start(bf16[128,1024]{1,0:T(8,128)(2,1)S(1)} %shard_map.57), channel_id=1, source_target_pairs={{0,4},{1,13},{2,6},{3,15},{4,8},{5,1},{6,10},{7,3},{8,12},{9,5},{1... | collective-permute-start | bytes 786440 | tf_op jit(solution)/shard_map/ppermute | solution.py:358
  7.1 1.5 %collective-permute-start.2 = (bf16[128,1024]{1,0:T(8,128)(2,1)S(1)}, bf16[128,1024]{1,0:T(8,128)(2,1)S(1)}, u32[]{:S(2)}, u32[]{:S(2)}) collective-permute-start(bf16[128,1024]{1,0:T(8,128)(2,1)S(1)} %get-tuple-element.32.x2), channel_id=1, source_target_pairs={{0,2},{1,3},{2,0},{3,1},{4,6},{5,7},{6,4},{7,5},{8,10},{9,11},{10,... | collective-permute-start | bytes 786440 | tf_op jit(solution)/shard_map/ppermute | solution.py:358
  8.6 0.1 copy.9.nbr
  8.7 2.8 %collective-permute-done.f0 = bf16[128,1024]{1,0:T(8,128)(2,1)S(1)} collective-permute-done((bf16[128,1024]{1,0:T(8,128)(2,1)S(1)}, bf16[128,1024]{1,0:T(8,128)(2,1)S(1)}, u32[]{:S(2)}, u32[]{:S(2)}) %collective-permute-start) | collective-permute-done | bytes 262176 | tf_op jit(solution)/shard_map/ppermute | solution.py:358
  11.5 2.0 %collective-permute-start.3 = (bf16[128,1024]{1,0:T(8,128)(2,1)S(1)}, bf16[128,1024]{1,0:T(8,128)(2,1)S(1)}, u32[]{:S(2)}, u32[]{:S(2)}) collective-permute-start(bf16[128,1024]{1,0:T(8,128)(2,1)S(1)} %collective-permute-done.f0), channel_id=1, source_target_pairs={{0,4},{1,5},{2,14},{3,15},{4,8},{5,9},{6,2},{7,3},{8,12},{9,13},{1... | collective-permute-start | bytes 786440 | tf_op jit(solution)/shard_map/ppermute | solution.py:358
  13.5 6.9 %shard_map.56 = (bf16[24,64,256]{2,1,0:T(8,128)(2,1)S(1)}, bf16[6,4,128,256]{3,2,1,0:T(8,128)(2,1)S(1)}, bf16[6,4,256,128]{3,2,1,0:T(8,128)(2,1)S(1)}, bf16[1024...) custom-call(bf16[128,1024]{1,0:T(8,128)(2,1)S(1)} %get-tuple-element.33.x0, bf16[128,1024]{1,0:T(8,128)(2,1)S(1)} %get-tuple-element.31.x1, ...), custom_call_target="tpu_custom_call" | custom-call | flops 2000000000 | bytes 1000 | tf_op jit(solution)/shard_map/pallas_call | solution.py:332
  20.4 0.0 collective-permute-done.1.f1
  20.4 1.6 %collective-permute-start.5 = (bf16[128,1024]{1,0:T(8,128)(2,1)S(1)}, bf16[128,1024]{1,0:T(8,128)(2,1)S(1)}, u32[]{:S(2)}, u32[]{:S(2)}) collective-permute-start(bf16[128,1024]{1,0:T(8,128)(2,1)S(1)} %collective-permute-done.1.f1), channel_id=1, source_target_pairs={{0,4},{1,5},{2,14},{3,15},{4,8},{5,9},{6,2},{7,3},{8,12},{9,13},{1... | collective-permute-start | bytes 786440 | tf_op jit(solution)/shard_map/ppermute | solution.py:358
  22.0 3.1 %shard_map.58 = (f32[24,1,256]{2,1,0:T(1,128)S(1)}, f32[24,1,256]{2,1,0:T(1,128)S(1)}, f32[24,64,256]{2,1,0:T(8,128)S(1)}) custom-call(s32[6,2]{1,0:T(8,128)S(1)} %copy.9.nbr, bf16[24,64,256]{2,1,0:T(8,128)(2,1)S(1)} %get-tuple-element.36.qc, bf16[6,4,128,256]{3,2,1,0:T(8,128)(2,1)S(1)} %get-tuple-element.37.keys, ...), custom_call_target="tpu_custom_call" | custom-call | flops 2000000000 | bytes 1000 | tf_op jit(solution)/shard_map/pallas_call | solution.py:332
  25.1 1.8 %collective-permute-start.7 = (bf16[128,1024]{1,0:T(8,128)(2,1)S(1)}, bf16[128,1024]{1,0:T(8,128)(2,1)S(1)}, u32[]{:S(2)}, u32[]{:S(2)}) collective-permute-start(bf16[128,1024]{1,0:T(8,128)(2,1)S(1)} %collective-permute-done.2.f2), channel_id=1, source_target_pairs={{0,4},{1,5},{2,14},{3,15},{4,8},{5,9},{6,2},{7,3},{8,12},{9,13},{1... | collective-permute-start | bytes 786440 | tf_op jit(solution)/shard_map/ppermute | solution.py:358
  26.9 6.1 %shard_map.59 = (f32[24,1,256]{2,1,0:T(1,128)S(1)}, f32[24,1,256]{2,1,0:T(1,128)S(1)}, f32[24,64,256]{2,1,0:T(8,128)S(1)}) custom-call(s32[6,2]{1,0:T(8,128)S(1)} %copy.9.nbr, s32[6]{0:T(128)S(1)} %copy-done.1, bf16[128,1024]{1,0:T(8,128)(2,1)S(1)} %collective-permute-done.f0, bf16[128,1024]{1,0:T(8,128)(2,1)S(1)} %collective-permute-done.1.f1, ...), custom_call_target="tpu_custom_call" | custom-call | flops 2000000000 | bytes 1000 | tf_op jit(solution)/shard_map/pallas_call | solution.py:332
  33.0 1.4 %shard_map.60 = (bf16[4,4,64,256]{3,2,1,0:T(8,128)(2,1)S(1)}, bf16[2,4,4,256,128]{4,3,2,1,0:T(8,128)(2,1)S(1)}) custom-call(bf16[128,1024]{1,0:T(8,128)(2,1)S(1)} %collective-permute-done.3.g0, bf16[128,1024]{1,0:T(8,128)(2,1)S(1)} %collective-permute-done.5.g1, bf16[1024,1024]{1,0:T(8,128)(2,1)S(1)} %get-tuple-element.41.w, ...), custom_call_target="tpu_custom_call" | custom-call | flops 4000000000 | bytes 1000 | tf_op jit(solution)/shard_map/pallas_call | solution.py:332
  34.4 0.7 %collective-permute-done.7.g2 = bf16[128,1024]{1,0:T(8,128)(2,1)S(1)} collective-permute-done((bf16[128,1024]{1,0:T(8,128)(2,1)S(1)}, bf16[128,1024]{1,0:T(8,128)(2,1)S(1)}, u32[]{:S(2)}, u32[]{:S(2)}) %collective-permute-start.7) | collective-permute-done | bytes 262176 | tf_op jit(solution)/shard_map/ppermute | solution.py:358
  35.1 0.9 %shard_map.61 = bf16[512,1024]{1,0:T(8,128)(2,1)S(1)} custom-call(s32[6]{0:T(128)S(1)} %copy-done.1, bf16[128,1024]{1,0:T(8,128)(2,1)S(1)} %collective-permute-done.f0, bf16[128,1024]{1,0:T(8,128)(2,1)S(1)} %collective-permute-done.1.f1, bf16[128,1024]{1,0:T(8,128)(2,1)S(1)} %collective-permute-done.2.f2, bf16[128,1024]{1,0:T(8,128)(2,1)S(1)} %collective-permute-done.3.g0, ...), custom_call_target="tpu_custom_call" | custom-call | flops 2000000000 | bytes 1000 | tf_op jit(solution)/shard_map/pallas_call | solution.py:332
  36.0 0.1 collective-permute-start.8
  36.1 0.0 copy-start
  36.1 3.7 %shard_map.62 = (f32[24,1,256]{2,1,0:T(1,128)S(1)}, f32[24,1,256]{2,1,0:T(1,128)S(1)}, f32[24,64,256]{2,1,0:T(8,128)S(1)}) custom-call(s32[6,2]{1,0:T(8,128)S(1)} %copy.9.nbr, s32[6]{0:T(128)S(1)} %copy-done.1, bf16[128,1024]{1,0:T(8,128)(2,1)S(1)} %collective-permute-done.7.g2, bf16[1024,1024]{1,0:T(8,128)(2,1)S(1)} %get-tuple-element.41.w, ...), custom_call_target="tpu_custom_call" | custom-call | flops 2000000000 | bytes 1000 | tf_op jit(solution)/shard_map/pallas_call | solution.py:332
  39.8 8.2 %shard_map.63 = bf16[2,192,1024]{2,1,0:T(8,128)(2,1)} custom-call(s32[6,2]{1,0:T(8,128)S(1)} %copy.9.nbr, s32[6]{0:T(128)S(1)} %copy-done.1, bf16[512,1024]{1,0:T(8,128)(2,1)S(1)} %collective-permute-done.8.e, bf16[1024,1024]{1,0:T(8,128)(2,1)S(1)} %get-tuple-element.41.w, bf16[1024,1024]{1,0:T(8,128)(2,1)S(1)} %get-tuple-element.42.wvt, ...), custom_call_target="tpu_custom_call" | custom-call | flops 2000000000 | bytes 1000 | tf_op jit(solution)/shard_map/pallas_call | solution.py:332
  (10 shorter events, 0.0 us)
Async XLA Ops:
  0.0 4.4 %copy-start.1 = (s32[6]{0:T(128)S(1)}, s32[6]{0:T(128)}, u32[]{:S(2)}) copy-start(s32[6]{0:T(128)} %hw.9) | copy-start | bytes 76
  0.0 4.4 %collective-permute-start.4 = (bf16[2,192,1024]{2,1,0:T(8,128)(2,1)}, bf16[2,192,1024]{2,1,0:T(8,128)(2,1)S(1)}, u32[]{:S(2)}, u32[]{:S(2)}) collective-permute-start(bf16[2,192,1024]{2,1,0:T(8,128)(2,1)} %x.1), channel_id=1, source_target_pairs={{0,1},{1,0},{2,3},{3,2},{4,5},{5,4},{6,7},{7,6},{8,9},{9,8},{10,11... | collective-permute-start | bytes 2359304 | tf_op jit(solution)/shard_map/ppermute | solution.py:358
  1.7 9.8 %collective-permute-start = (bf16[128,1024]{1,0:T(8,128)(2,1)S(1)}, bf16[128,1024]{1,0:T(8,128)(2,1)S(1)}, u32[]{:S(2)}, u32[]{:S(2)}) collective-permute-start(bf16[128,1024]{1,0:T(8,128)(2,1)S(1)} %get-tuple-element.33.x0), channel_id=1, source_target_pairs={{0,2},{1,3},{2,0},{3,1},{4,6},{5,7},{6,4},{7,5},{8,10},{9,11},{10,... | collective-permute-start | bytes 786440 | tf_op jit(solution)/shard_map/ppermute | solution.py:358
  4.3 16.1 %collective-permute-start.1 = (bf16[128,1024]{1,0:T(8,128)(2,1)S(1)}, bf16[128,1024]{1,0:T(8,128)(2,1)S(1)}, u32[]{:S(2)}, u32[]{:S(2)}) collective-permute-start(bf16[128,1024]{1,0:T(8,128)(2,1)S(1)} %get-tuple-element.31.x1), channel_id=1, source_target_pairs={{0,2},{1,3},{2,0},{3,1},{4,6},{5,7},{6,4},{7,5},{8,10},{9,11},{10,... | collective-permute-start | bytes 786440 | tf_op jit(solution)/shard_map/ppermute | solution.py:358
  4.4 4.2 %copy-start.2 = (s32[6,2]{0,1:T(2,128)S(1)}, s32[6,2]{0,1:T(2,128)}, u32[]{:S(2)}) copy-start(s32[6,2]{0,1:T(2,128)} %param.9) | copy-start | bytes 148
  5.0 17.0 %collective-permute-start.6 = (bf16[128,1024]{1,0:T(8,128)(2,1)S(1)}, bf16[128,1024]{1,0:T(8,128)(2,1)S(1)}, u32[]{:S(2)}, u32[]{:S(2)}) collective-permute-start(bf16[128,1024]{1,0:T(8,128)(2,1)S(1)} %shard_map.57), channel_id=1, source_target_pairs={{0,4},{1,13},{2,6},{3,15},{4,8},{5,1},{6,10},{7,3},{8,12},{9,5},{1... | collective-permute-start | bytes 786440 | tf_op jit(solution)/shard_map/ppermute | solution.py:358
  7.1 18.0 %collective-permute-start.2 = (bf16[128,1024]{1,0:T(8,128)(2,1)S(1)}, bf16[128,1024]{1,0:T(8,128)(2,1)S(1)}, u32[]{:S(2)}, u32[]{:S(2)}) collective-permute-start(bf16[128,1024]{1,0:T(8,128)(2,1)S(1)} %get-tuple-element.32.x2), channel_id=1, source_target_pairs={{0,2},{1,3},{2,0},{3,1},{4,6},{5,7},{6,4},{7,5},{8,10},{9,11},{10,... | collective-permute-start | bytes 786440 | tf_op jit(solution)/shard_map/ppermute | solution.py:358
  11.5 21.5 %collective-permute-start.3 = (bf16[128,1024]{1,0:T(8,128)(2,1)S(1)}, bf16[128,1024]{1,0:T(8,128)(2,1)S(1)}, u32[]{:S(2)}, u32[]{:S(2)}) collective-permute-start(bf16[128,1024]{1,0:T(8,128)(2,1)S(1)} %collective-permute-done.f0), channel_id=1, source_target_pairs={{0,4},{1,5},{2,14},{3,15},{4,8},{5,9},{6,2},{7,3},{8,12},{9,13},{1... | collective-permute-start | bytes 786440 | tf_op jit(solution)/shard_map/ppermute | solution.py:358
  20.4 12.6 %collective-permute-start.5 = (bf16[128,1024]{1,0:T(8,128)(2,1)S(1)}, bf16[128,1024]{1,0:T(8,128)(2,1)S(1)}, u32[]{:S(2)}, u32[]{:S(2)}) collective-permute-start(bf16[128,1024]{1,0:T(8,128)(2,1)S(1)} %collective-permute-done.1.f1), channel_id=1, source_target_pairs={{0,4},{1,5},{2,14},{3,15},{4,8},{5,9},{6,2},{7,3},{8,12},{9,13},{1... | collective-permute-start | bytes 786440 | tf_op jit(solution)/shard_map/ppermute | solution.py:358
  25.1 10.0 %collective-permute-start.7 = (bf16[128,1024]{1,0:T(8,128)(2,1)S(1)}, bf16[128,1024]{1,0:T(8,128)(2,1)S(1)}, u32[]{:S(2)}, u32[]{:S(2)}) collective-permute-start(bf16[128,1024]{1,0:T(8,128)(2,1)S(1)} %collective-permute-done.2.f2), channel_id=1, source_target_pairs={{0,4},{1,5},{2,14},{3,15},{4,8},{5,9},{6,2},{7,3},{8,12},{9,13},{1... | collective-permute-start | bytes 786440 | tf_op jit(solution)/shard_map/ppermute | solution.py:358
  36.0 3.8 %collective-permute-start.8 = (bf16[512,1024]{1,0:T(8,128)(2,1)S(1)}, bf16[512,1024]{1,0:T(8,128)(2,1)S(1)}, u32[]{:S(2)}, u32[]{:S(2)}) collective-permute-start(bf16[512,1024]{1,0:T(8,128)(2,1)S(1)} %shard_map.61), channel_id=1, source_target_pairs={{0,1},{1,0},{2,3},{3,2},{4,5},{5,4},{6,7},{7,6},{8,9},{9,8},{10,11... | collective-permute-start | bytes 3145736 | tf_op jit(solution)/shard_map/ppermute | solution.py:358
  36.1 3.7 %copy-start = (bf16[1024,1024]{1,0:T(8,128)(2,1)S(1)}, bf16[1024,1024]{1,0:T(8,128)(2,1)}, u32[]{:S(2)}) copy-start(bf16[1024,1024]{1,0:T(8,128)(2,1)} %wout.1) | copy-start | bytes 6291460
